TPU v7x, 128 devices: a whole 4x4x4 slice. The times are simulated.
128 devices in a mesh: seq: 32 (over y, x, core), ch: 4 (over z).
Axes of the slice: x: 4, y: 4, z: 4, core: 2. Of those that a mesh axis runs over, the one named last changes fastest.
Arguments:
- qkv: bfloat16 [8192, 3, 4096], P('seq', None, 'ch'), may hold values from -6 to 6
- short_taps: float32 [3, 3, 4096], P(None, None, 'ch'), may hold values from -3 to 3
- lengths: int32 [8], replicated, may hold values from 1 to 2048, 8192 in all
- filter_taps: float32 [4, 1024, 2048], P('ch', 'seq'), may hold values from -2 to 2
- w_out: bfloat16 [4096, 4096], P(None, 'ch'), may hold values from -0.09375 to 0.09375
Outputs:
- mixed: bfloat16 [8192, 4096], P('seq', 'ch')
Inputs may be any that keep to these rules, and one draw needn't show every extreme that they name: The lengths sum to 8192 and the longest is exactly 2048.
All inputs are finite; a program needn't handle non-finite values.
Results may differ from a plain program's by a relative error of at most 0.015.
Values may be sent and summed in bfloat16 or wider, within the bound.
No kernel may reach another device: no remote copies, remote signals or barrier semaphores. Data moves between devices by JAX's collectives and lax.ppermute only.
A program may use at most 128 MiB of HBM per device.

v0:
```python
import functools

import jax
import jax.numpy as jnp
from jax import lax
from jax.experimental import pallas as pl
from jax.experimental.pallas import tpu as pltpu
from jax.sharding import PartitionSpec as P

TAPS = 3
BLK = 128
MIB = 1 << 20


def params(mib):
    return pltpu.CompilerParams(vmem_limit_bytes=mib * MIB)


def starts_of(lengths_ref, positions):
    starts = jnp.zeros(positions.shape, jnp.int32)
    offset = jnp.int32(0)
    for prompt in range(lengths_ref.shape[0]):
        starts = jnp.where(positions >= offset, offset, starts)
        offset = offset + lengths_ref[prompt]
    return starts


def short_filter(scr, taps_ref, which, keeps, tok_rows):
    total = None
    for tap in range(TAPS):
        term = taps_ref[tap, which : which + 1, :] * scr[8 - tap : 8 - tap + tok_rows, :] * keeps[tap]
        total = term if total is None else total + term
    return total


def fill(scr, tok_rows, edge, values):
    scr[6:8, :] = edge.astype(jnp.float32)
    scr[8 : 8 + tok_rows, :] = values.astype(jnp.float32)


def keep_masks(lengths_ref, tok_rows, width):
    place = lax.axis_index("seq") * tok_rows
    positions = place + lax.broadcasted_iota(jnp.int32, (tok_rows, width), 0)
    starts = starts_of(lengths_ref, positions)
    return [(positions - tap >= starts).astype(jnp.float32) for tap in range(TAPS)]


def product_kernel(lengths_ref, kv_ref, edge_ref, taps_ref, out_ref, scr_k, scr_v):
    tok_rows, width = kv_ref.shape[1:]
    keeps = keep_masks(lengths_ref, tok_rows, width)
    fill(scr_k, tok_rows, edge_ref[:, 1, :], kv_ref[1])
    fill(scr_v, tok_rows, edge_ref[:, 2, :], kv_ref[2])
    product = short_filter(scr_k, taps_ref, 1, keeps, tok_rows) * short_filter(
        scr_v, taps_ref, 2, keeps, tok_rows
    )
    out_ref[...] = product.T.astype(jnp.bfloat16)


def query_kernel(lengths_ref, q_ref, edge_ref, taps_ref, out_ref, scr_q):
    tok_rows, width = q_ref.shape[1:]
    keeps = keep_masks(lengths_ref, tok_rows, width)
    fill(scr_q, tok_rows, edge_ref[:, 0, :], q_ref[0])
    out_ref[...] = short_filter(scr_q, taps_ref, 0, keeps, tok_rows).astype(jnp.bfloat16)


def short_call(kernel, lengths, qkv, edge, taps, transposed, scratches, width=256):
    parts, tok_rows, channels = qkv.shape
    if transposed:
        shape, spec = (channels, tok_rows), pl.BlockSpec((width, tok_rows), lambda i: (i, 0))
    else:
        shape, spec = (tok_rows, channels), pl.BlockSpec((tok_rows, width), lambda i: (0, i))
    return pl.pallas_call(
        kernel,
        grid=(channels // width,),
        out_shape=jax.ShapeDtypeStruct(shape, jnp.bfloat16),
        in_specs=[
            pl.BlockSpec(memory_space=pltpu.SMEM),
            pl.BlockSpec((parts, tok_rows, width), lambda i: (0, 0, i)),
            pl.BlockSpec((TAPS - 1, 3, width), lambda i: (0, 0, i)),
            pl.BlockSpec((TAPS, 3, width), lambda i: (0, 0, i)),
        ],
        out_specs=spec,
        scratch_shapes=[pltpu.VMEM((tok_rows + 8, width), jnp.float32)] * scratches,
        compiler_params=params(32),
        cost_estimate=pl.CostEstimate(flops=20 * tok_rows * channels, bytes_accessed=4 * MIB, transcendentals=0),
    )(lengths, qkv, edge, taps)


def toeplitz_kernel(taps_ref, out_ref):
    count, span = taps_ref.shape
    for c in range(count):
        row = jnp.concatenate([taps_ref[c : c + 1, :], jnp.zeros((1, BLK), jnp.float32)], 1)
        wide = jnp.broadcast_to(row, (BLK, span + BLK))
        sheared = pltpu.roll(wide, 0, 1, stride=1, stride_axis=0)
        for t in range(span // BLK + 1):
            out_ref[c, t * BLK : (t + 1) * BLK, :] = sheared[:, t * BLK : (t + 1) * BLK].astype(jnp.bfloat16)


def toeplitz(taps, group=8):
    channels, span = taps.shape
    depth = span + BLK
    return pl.pallas_call(
        toeplitz_kernel,
        grid=(channels // group,),
        out_shape=jax.ShapeDtypeStruct((channels, depth, BLK), jnp.bfloat16),
        in_specs=[pl.BlockSpec((group, span), lambda i: (i, 0))],
        out_specs=pl.BlockSpec((group, depth, BLK), lambda i: (i, 0, 0)),
        compiler_params=params(32),
        cost_estimate=pl.CostEstimate(
            flops=8 * channels * depth * BLK, bytes_accessed=2 * channels * depth * BLK, transcendentals=0
        ),
    )(taps)


def over_rows(lengths_ref, body):
    def prompt_step(prompt, carry):
        offset, row = carry
        end = offset + lengths_ref[prompt]
        first, last = offset // BLK, (end - 1) // BLK

        def block_step(block, _):
            body(row + block - first, block, offset, end)
            return 0

        lax.fori_loop(first, last + 1, block_step, 0)
        return end, row + last - first + 1

    lax.fori_loop(0, lengths_ref.shape[0], prompt_step, (jnp.int32(0), jnp.int32(0)))


def lanes_of(block, start, end, rows):
    positions = block * BLK + lax.broadcasted_iota(jnp.int32, (rows, BLK), 1)
    return (positions >= start) & (positions < end)


def conv_kernel(
    lengths_ref, signal_ref, toep_ref, out_ref, blocks, spread, masks, lhs, result, *, rows, rows_b, lags
):
    step = pl.program_id(0)
    devices, channels, tok_rows = signal_ref.shape
    group = toep_ref.shape[0]
    per = tok_rows // BLK
    pad = lags - 1
    pitch = pad + rows_b

    @pl.when(step == 0)
    def _():
        for device in range(devices):
            for part in range(per):
                blocks[device * per + part] = signal_ref[
                    device, :, part * BLK : (part + 1) * BLK
                ].astype(jnp.float32)
        spread[...] = jnp.zeros_like(spread)

        def place(row, block, start, end):
            slab = jnp.where(lanes_of(block, start, end, channels), blocks[block], 0.0)
            spread[pl.ds(pad + row, channels, stride=pitch), :] = slab

        over_rows(lengths_ref, place)
        row_ids = lax.broadcasted_iota(jnp.int32, (rows_b, BLK), 0)
        firsts = jnp.zeros((rows_b, BLK), jnp.int32)
        offset, row = jnp.int32(0), jnp.int32(0)
        for prompt in range(lengths_ref.shape[0]):
            firsts = jnp.where(row_ids >= row, row, firsts)
            end = offset + lengths_ref[prompt]
            row = row + (end - 1) // BLK - offset // BLK + 1
            offset = end
        for lag in range(lags):
            masks[lag] = (row_ids - lag >= firsts).astype(jnp.float32)

    views = spread.reshape(channels, pitch, BLK)
    for g in range(group):
        channel = step * group + g
        for lag in range(lags):
            shifted = views[channel, pad - lag : pad - lag + rows_b, :]
            lhs[g, :, lag * BLK : (lag + 1) * BLK] = (shifted * masks[lag]).astype(jnp.bfloat16)
        total = jnp.dot(lhs[g], toep_ref[g], preferred_element_type=jnp.float32)
        result[pl.ds(channel * rows, rows), :] = total[:rows]

    @pl.when(step == pl.num_programs(0) - 1)
    def _():
        def collect(row, block, start, end):
            slab = result[pl.ds(row, channels, stride=rows), :]
            blocks[block] = jnp.where(lanes_of(block, start, end, channels), slab, blocks[block])

        over_rows(lengths_ref, collect)
        for device in range(devices):
            for part in range(per):
                out_ref[device, :, part * BLK : (part + 1) * BLK] = blocks[device * per + part].astype(jnp.bfloat16)


def long_conv(lengths, signal, toep, group=2):
    devices, channels, tok_rows = signal.shape
    total = devices * tok_rows
    depth = toep.shape[1]
    lags = depth // BLK
    rows = -(-(total // BLK + lengths.shape[0] - 1) // 8) * 8
    rows_b = -(-rows // 16) * 16
    pitch = lags - 1 + rows_b
    return pl.pallas_call(
        functools.partial(conv_kernel, rows=rows, rows_b=rows_b, lags=lags),
        grid=(channels // group,),
        out_shape=jax.ShapeDtypeStruct(signal.shape, jnp.bfloat16),
        in_specs=[
            pl.BlockSpec(memory_space=pltpu.SMEM),
            pl.BlockSpec(signal.shape, lambda i: (0, 0, 0)),
            pl.BlockSpec((group, depth, BLK), lambda i: (i, 0, 0)),
        ],
        out_specs=pl.BlockSpec(signal.shape, lambda i: (0, 0, 0)),
        scratch_shapes=[
            pltpu.VMEM((total // BLK, channels, BLK), jnp.float32),
            pltpu.VMEM((channels * pitch, BLK), jnp.float32),
            pltpu.VMEM((lags, rows_b, BLK), jnp.float32),
            pltpu.VMEM((group, rows_b, depth), jnp.bfloat16),
            pltpu.VMEM((channels * rows, BLK), jnp.float32),
        ],
        compiler_params=params(40),
        cost_estimate=pl.CostEstimate(
            flops=2 * channels * rows * depth * BLK, bytes_accessed=2 * channels * depth * BLK, transcendentals=0
        ),
    )(lengths, signal, toep)


def gate_kernel(query_ref, conv_ref, out_ref):
    conv = conv_ref[...].astype(jnp.float32).T
    out_ref[...] = (query_ref[...].astype(jnp.float32) * conv).astype(jnp.bfloat16)


def gate(query, conv_t, width=256):
    tok_rows, channels = query.shape
    return pl.pallas_call(
        gate_kernel,
        grid=(channels // width,),
        out_shape=jax.ShapeDtypeStruct(query.shape, jnp.bfloat16),
        in_specs=[
            pl.BlockSpec((tok_rows, width), lambda i: (0, i)),
            pl.BlockSpec((width, tok_rows), lambda i: (i, 0)),
        ],
        out_specs=pl.BlockSpec((tok_rows, width), lambda i: (0, i)),
        compiler_params=params(32),
        cost_estimate=pl.CostEstimate(flops=tok_rows * channels, bytes_accessed=2 * MIB, transcendentals=0),
    )(query, conv_t)


def shift(array, axis, by):
    length = lax.axis_size(axis)
    return lax.ppermute(array, axis, [(i, (i + by) % length) for i in range(length)])


def project(gated, w_out):
    size = lax.axis_size("ch")
    depth = gated.shape[1]
    place = lax.axis_index("ch")

    def part(block, owner):
        rows = lax.dynamic_slice_in_dim(w_out, owner % size * depth, depth, 0)
        return jnp.dot(block, rows, preferred_element_type=jnp.float32)

    half = gated.shape[0] // 2
    right, left = shift(gated, "ch", 1), shift(gated, "ch", -1)
    far = jnp.concatenate([shift(right[:half], "ch", 1), shift(left[half:], "ch", -1)], 0)
    total = part(gated, place) + part(right, place + size - 1) + part(left, place + 1)
    return (total + part(far, place + 2)).astype(jnp.bfloat16)


def per_device(qkv, short_taps, lengths, filter_taps, w_out):
    tok_rows, _, width = qkv.shape
    lead = TAPS - 1
    seq = lax.axis_size("seq")
    edge = lax.ppermute(qkv[tok_rows - lead :], "seq", [(i, i + 1) for i in range(seq - 1)])
    by_kind = qkv.transpose(1, 0, 2)
    product_t = short_call(product_kernel, lengths, by_kind, edge, short_taps, True, 2)
    query = short_call(query_kernel, lengths, by_kind, edge, short_taps, False, 1)
    toep = toeplitz(filter_taps[0])
    signal = lax.all_to_all(product_t.reshape(seq, width // seq, tok_rows), "seq", 0, 0, tiled=True)
    conv = long_conv(lengths, signal, toep)
    conv_t = lax.all_to_all(conv, "seq", 0, 0, tiled=True).reshape(width, tok_rows)
    return project(gate(query, conv_t), w_out)


def solution(mesh):
    placed = (P("seq", None, "ch"), P(None, None, "ch"), P(), P("ch", "seq", None), P(None, "ch"))
    return jax.shard_map(
        per_device, mesh=mesh, in_specs=placed, out_specs=P("seq", "ch"), check_vma=False
    )
```

profile of v0, /device:TPU:1, one launch (start us, length us, event | category | flops | bytes accessed | tf_op | source)
XLA Modules:
  0.0 100.4 jit_solution(7531329124067540480)
XLA Ops:
  0.0 0.8 slice.9
  0.8 4.5 %collective-permute-start = (bf16[2,3,1024]{2,1,0:T(4,128)(2,1)S(1)}, bf16[2,3,1024]{2,1,0:T(4,128)(2,1)S(1)}, u32[]{:S(2)}, u32[]{:S(2)}) collective-permute-start(bf16[2,3,1024]{2,1,0:T(4,128)(2,1)S(1)} %copy.7), channel_id=1, source_target_pairs={{0,4},{4,8},{8,12},{12,16},{16,20},{20,24},{24,28},{28,32},{32,36}... | collective-permute-start | bytes 36872 | tf_op jit(solution)/shard_map/ppermute | solution.py:270
  5.3 0.8 collective-permute-done.edge_ref
  6.2 0.0 copy-start.1
  6.2 1.4 %copy-done.1 = bf16[256,3,1024]{2,0,1:T(8,128)(2,1)S(1)} copy-done((bf16[256,3,1024]{2,0,1:T(8,128)(2,1)S(1)}, bf16[256,3,1024]{2,0,1:T(8,128)(2,1)}, u32[]{:S(2)}) %copy-start.1) | copy-done | bytes 1572888
  7.6 0.0 copy-start.4
  7.6 0.8 copy-done.4
  8.4 0.0 copy-start.6
  8.4 0.7 copy-done.6
  9.1 3.4 %shard_map.56 = bf16[1024,256]{1,0:T(8,128)(2,1)} custom-call(s32[8]{0:T(128)S(1)} %copy-done.6, bf16[3,256,1024]{2,1,0:T(8,128)(2,1)S(1)} %bitcast.7, bf16[2,3,1024]{2,1,0:T(4,128)(2,1)S(1)} %collective-permute-done.edge_ref, f32[3,3,1024]{2,1,0:T(4,128)S(1)} %copy-done.4), custom_call_target="tpu_custom_call" | custom-call | flops 5242880 | bytes 4194304 | tf_op jit(solution)/shard_map/pallas_call | solution.py:72
  12.5 8.3 %all-to-all-start = ((bf16[32,32,256]{2,1,0:T(8,128)(2,1)}), bf16[32,32,256]{2,1,0:T(8,128)(2,1)S(1)}, u32[]{:S(2)}, u32[]{:S(2)}) async-start(bf16[32,32,256]{2,1,0:T(8,128)(2,1)} %bitcast.1), calls=%async_computation | async-start | bytes 1048576 | tf_op jit(solution)/shard_map/all_to_all | solution.py:275
  20.8 0.0 copy-start.3
  20.8 0.9 copy-done.3
  21.7 0.0 copy-start.7
  21.7 5.1 %shard_map.57.toep_ref = bf16[32,2176,128]{2,1,0:T(8,128)(2,1)S(1)} custom-call(f32[32,2048]{1,0:T(8,128)S(1)} %bitcast.10), custom_call_target="tpu_custom_call" | custom-call | flops 71303168 | bytes 17825792 | tf_op jit(solution)/shard_map/pallas_call | solution.py:102
  26.8 0.0 copy-start
  26.8 6.1 %copy-done = bf16[32,2176,128]{2,1,0:T(8,128)(2,1)} copy-done((bf16[32,2176,128]{2,1,0:T(8,128)(2,1)}, bf16[32,2176,128]{2,1,0:T(8,128)(2,1)S(1)}, u32[]{:S(2)}) %copy-start) | copy-done | bytes 17825816
  32.9 0.0 copy-start.2
  33.0 0.0 copy-start.5
  33.0 0.0 all-to-all-done.signal_ref
  33.0 0.0 copy-done.7
  33.0 18.6 %shard_map.58 = bf16[32,32,256]{2,1,0:T(8,128)(2,1)} custom-call(s32[8]{0:T(128)S(1)} %copy-done.7, bf16[32,32,256]{2,1,0:T(8,128)(2,1)S(1)} %all-to-all-done.signal_ref, bf16[32,2176,128]{2,1,0:T(8,128)(2,1)} %copy-done), custom_call_target="tpu_custom_call" | custom-call | flops 1283457024 | bytes 17825792 | tf_op jit(solution)/shard_map/pallas_call | solution.py:200
  51.5 7.4 %all-to-all-start.1 = ((bf16[32,32,256]{2,1,0:T(8,128)(2,1)}), bf16[32,32,256]{2,1,0:T(8,128)(2,1)S(1)}, u32[]{:S(2)}, u32[]{:S(2)}) async-start(bf16[32,32,256]{2,1,0:T(8,128)(2,1)} %shard_map.58), calls=%async_computation.1 | async-start | bytes 1048576 | tf_op jit(solution)/shard_map/all_to_all | solution.py:277
  58.9 0.0 copy-done.2
  58.9 0.0 copy-done.5
  58.9 2.2 %shard_map.55.query_ref = bf16[256,1024]{1,0:T(8,128)(2,1)S(1)} custom-call(s32[8]{0:T(128)S(1)} %copy-done.7, bf16[3,256,1024]{2,1,0:T(8,128)(2,1)S(1)} %bitcast.8, bf16[2,3,1024]{2,1,0:T(4,128)(2,1)S(1)} %collective-permute-done.edge_ref, f32[3,3,1024]{2,1,0:T(4,128)S(1)} %copy-done.5), custom_call_target="tpu_custom_call" | custom-call | flops 5242880 | bytes 4194304 | tf_op jit(solution)/shard_map/pallas_call | solution.py:72
  61.1 9.3 %all-to-all-done.1 = bf16[32,32,256]{2,1,0:T(8,128)(2,1)S(1)} async-done(((bf16[32,32,256]{2,1,0:T(8,128)(2,1)}), bf16[32,32,256]{2,1,0:T(8,128)(2,1)S(1)}, u32[]{:S(2)}, u32[]{:S(2)}) %all-to-all-start.1) | async-done | bytes 524320 | tf_op jit(solution)/shard_map/all_to_all | solution.py:277
  70.5 0.6 shard_map.59
  71.1 1.7 %collective-permute-start.1 = (bf16[256,1024]{1,0:T(8,128)(2,1)S(1)}, bf16[256,1024]{1,0:T(8,128)(2,1)S(1)}, u32[]{:S(2)}, u32[]{:S(2)}) collective-permute-start(bf16[256,1024]{1,0:T(8,128)(2,1)S(1)} %shard_map.59), channel_id=1, source_target_pairs={{0,1},{1,2},{2,3},{3,0},{4,5},{5,6},{6,7},{7,4},{8,9},{9,10},{10,1... | collective-permute-start | bytes 1572872 | tf_op jit(solution)/shard_map/ppermute | solution.py:247
  72.8 2.2 %collective-permute-start.2 = (bf16[256,1024]{1,0:T(8,128)(2,1)S(1)}, bf16[256,1024]{1,0:T(8,128)(2,1)S(1)}, u32[]{:S(2)}, u32[]{:S(2)}) collective-permute-start(bf16[256,1024]{1,0:T(8,128)(2,1)S(1)} %shard_map.59), channel_id=1, source_target_pairs={{0,3},{1,0},{2,1},{3,2},{4,7},{5,4},{6,5},{7,6},{8,11},{9,8},{10,9... | collective-permute-start | bytes 1572872 | tf_op jit(solution)/shard_map/ppermute | solution.py:247
  75.0 11.8 %collective-permute-done.1 = bf16[256,1024]{1,0:T(8,128)(2,1)S(1)} collective-permute-done((bf16[256,1024]{1,0:T(8,128)(2,1)S(1)}, bf16[256,1024]{1,0:T(8,128)(2,1)S(1)}, u32[]{:S(2)}, u32[]{:S(2)}) %collective-permute-start.1) | collective-permute-done | bytes 524320 | tf_op jit(solution)/shard_map/ppermute | solution.py:247
  86.8 0.1 collective-permute-start.3
  86.9 0.0 collective-permute-done.2
  86.9 2.7 %collective-permute-start.4 = (bf16[128,1024]{1,0:T(8,128)(2,1)S(1)}, bf16[128,1024]{1,0:T(8,128)(2,1)S(1)}, u32[]{:S(2)}, u32[]{:S(2)}) collective-permute-start(bf16[128,1024]{1,0:T(8,128)(2,1)S(1)} %slice.13), channel_id=1, source_target_pairs={{0,3},{1,0},{2,1},{3,2},{4,7},{5,4},{6,5},{7,6},{8,11},{9,8},{10,9... | collective-permute-start | bytes 786440 | tf_op jit(solution)/shard_map/ppermute | solution.py:247
  89.7 2.3 %fusion.2 = f32[256,1024]{1,0:T(8,128)S(1)} fusion(bf16[256,1024]{1,0:T(8,128)(2,1)S(1)} %collective-permute-done.2, bf16[4096,1024]{1,0:T(8,128)(2,1)} %param.9, s32[]{:T(128)S(6)} %select_n.36), kind=kOutput, calls=%fused_computation.2 | convolution fusion | flops 536870912 | bytes 3670020 | tf_op jit(solution)/shard_map/dot_general | solution.py:257
  92.0 2.3 %fusion.4 = f32[256,1024]{1,0:T(8,128)S(1)} fusion(bf16[256,1024]{1,0:T(8,128)(2,1)S(1)} %collective-permute-done.1, bf16[4096,1024]{1,0:T(8,128)(2,1)} %param.9, s32[]{:T(128)S(6)} %select_n.34), kind=kOutput, calls=%fused_computation.4 | convolution fusion | flops 536870912 | bytes 3670020 | tf_op jit(solution)/shard_map/dot_general | solution.py:257
  94.3 0.7 collective-permute-done.3
  94.9 0.0 collective-permute-done.4
  94.9 2.3 %fusion = f32[256,1024]{1,0:T(8,128)S(1)} fusion(bf16[4096,1024]{1,0:T(8,128)(2,1)} %param.9, s32[]{:T(128)S(6)} %select_n.38, bf16[128,1024]{1,0:T(8,128)(2,1)S(1)} %collective-permute-done.4, bf16[128,1024]{1,0:T(8,128)(2,1)S(1)} %collective-permute-done.3), kind=kOutput, calls=%fused_computation | convolution fusion | flops 537919488 | bytes 3670020 | tf_op jit(solution)/shard_map/dot_general | solution.py:257
  97.3 3.2 %fusion.17 = bf16[256,1024]{1,0:T(8,128)(2,1)} fusion(f32[256,1024]{1,0:T(8,128)S(1)} %fusion, f32[256,1024]{1,0:T(8,128)S(1)} %fusion.2, f32[256,1024]{1,0:T(8,128)S(1)} %fusion.4, bf16[256,1024]{1,0:T(8,128)(2,1)S(1)} %shard_map.59, bf16[4096,1024]{1,0:T(8,128)(2,1)} %param.9, s32[]{:T(128)S(6)} %select_n.32), kind=kOutput, calls=%fused_computation.11 | convolution fusion | flops 537919488 | bytes 6291460 | tf_op jit(solution)/shard_map/dot_general | solution.py:257
  (3 shorter events, 0.0 us)
Async XLA Ops:
  0.8 5.4 %collective-permute-start = (bf16[2,3,1024]{2,1,0:T(4,128)(2,1)S(1)}, bf16[2,3,1024]{2,1,0:T(4,128)(2,1)S(1)}, u32[]{:S(2)}, u32[]{:S(2)}) collective-permute-start(bf16[2,3,1024]{2,1,0:T(4,128)(2,1)S(1)} %copy.7), channel_id=1, source_target_pairs={{0,4},{4,8},{8,12},{12,16},{16,20},{20,24},{24,28},{28,32},{32,36}... | collective-permute-start | bytes 36872 | tf_op jit(solution)/shard_map/ppermute | solution.py:270
  6.2 1.4 %copy-start.1 = (bf16[256,3,1024]{2,0,1:T(8,128)(2,1)S(1)}, bf16[256,3,1024]{2,0,1:T(8,128)(2,1)}, u32[]{:S(2)}) copy-start(bf16[256,3,1024]{2,0,1:T(8,128)(2,1)} %param.5) | copy-start | bytes 4718596
  7.6 0.8 copy-start.4
  8.4 0.7 copy-start.6
  12.5 20.5 %all-to-all-start = ((bf16[32,32,256]{2,1,0:T(8,128)(2,1)}), bf16[32,32,256]{2,1,0:T(8,128)(2,1)S(1)}, u32[]{:S(2)}, u32[]{:S(2)}) async-start(bf16[32,32,256]{2,1,0:T(8,128)(2,1)} %bitcast.1), calls=%async_computation | async-start | bytes 1048576 | tf_op jit(solution)/shard_map/all_to_all | solution.py:275
  20.8 1.0 copy-start.3
  21.7 11.2 %copy-start.7 = (s32[8]{0:T(128)S(1)}, s32[8]{0:T(128)}, u32[]{:S(2)}) copy-start(s32[8]{0:T(128)} %lengths_ref.5) | copy-start | bytes 100
  26.8 6.1 %copy-start = (bf16[32,2176,128]{2,1,0:T(8,128)(2,1)}, bf16[32,2176,128]{2,1,0:T(8,128)(2,1)S(1)}, u32[]{:S(2)}) copy-start(bf16[32,2176,128]{2,1,0:T(8,128)(2,1)S(1)} %shard_map.57.toep_ref) | copy-start | bytes 53477380
  32.9 26.0 %copy-start.2 = (bf16[256,3,1024]{2,0,1:T(8,128)(2,1)S(1)}, bf16[256,3,1024]{2,0,1:T(8,128)(2,1)}, u32[]{:S(2)}) copy-start(bf16[256,3,1024]{2,0,1:T(8,128)(2,1)} %param.5) | copy-start | bytes 4718596
  33.0 26.0 %copy-start.5 = (f32[3,3,1024]{2,1,0:T(4,128)S(1)}, f32[3,3,1024]{2,1,0:T(4,128)}, u32[]{:S(2)}) copy-start(f32[3,3,1024]{2,1,0:T(4,128)} %taps_ref.3) | copy-start | bytes 110596
  51.5 18.9 %all-to-all-start.1 = ((bf16[32,32,256]{2,1,0:T(8,128)(2,1)}), bf16[32,32,256]{2,1,0:T(8,128)(2,1)S(1)}, u32[]{:S(2)}, u32[]{:S(2)}) async-start(bf16[32,32,256]{2,1,0:T(8,128)(2,1)} %shard_map.58), calls=%async_computation.1 | async-start | bytes 1048576 | tf_op jit(solution)/shard_map/all_to_all | solution.py:277
  71.1 15.7 %collective-permute-start.1 = (bf16[256,1024]{1,0:T(8,128)(2,1)S(1)}, bf16[256,1024]{1,0:T(8,128)(2,1)S(1)}, u32[]{:S(2)}, u32[]{:S(2)}) collective-permute-start(bf16[256,1024]{1,0:T(8,128)(2,1)S(1)} %shard_map.59), channel_id=1, source_target_pairs={{0,1},{1,2},{2,3},{3,0},{4,5},{5,6},{6,7},{7,4},{8,9},{9,10},{10,1... | collective-permute-start | bytes 1572872 | tf_op jit(solution)/shard_map/ppermute | solution.py:247
  72.8 14.1 %collective-permute-start.2 = (bf16[256,1024]{1,0:T(8,128)(2,1)S(1)}, bf16[256,1024]{1,0:T(8,128)(2,1)S(1)}, u32[]{:S(2)}, u32[]{:S(2)}) collective-permute-start(bf16[256,1024]{1,0:T(8,128)(2,1)S(1)} %shard_map.59), channel_id=1, source_target_pairs={{0,3},{1,0},{2,1},{3,2},{4,7},{5,4},{6,5},{7,6},{8,11},{9,8},{10,9... | collective-permute-start | bytes 1572872 | tf_op jit(solution)/shard_map/ppermute | solution.py:247
  86.8 8.1 %collective-permute-start.3 = (bf16[128,1024]{1,0:T(8,128)(2,1)S(1)}, bf16[128,1024]{1,0:T(8,128)(2,1)S(1)}, u32[]{:S(2)}, u32[]{:S(2)}) collective-permute-start(bf16[128,1024]{1,0:T(8,128)(2,1)S(1)} %slice.12), channel_id=1, source_target_pairs={{0,1},{1,2},{2,3},{3,0},{4,5},{5,6},{6,7},{7,4},{8,9},{9,10},{10,1... | collective-permute-start | bytes 786440 | tf_op jit(solution)/shard_map/ppermute | solution.py:247
  86.9 8.0 %collective-permute-start.4 = (bf16[128,1024]{1,0:T(8,128)(2,1)S(1)}, bf16[128,1024]{1,0:T(8,128)(2,1)S(1)}, u32[]{:S(2)}, u32[]{:S(2)}) collective-permute-start(bf16[128,1024]{1,0:T(8,128)(2,1)S(1)} %slice.13), channel_id=1, source_target_pairs={{0,3},{1,0},{2,1},{3,2},{4,7},{5,4},{6,5},{7,6},{8,11},{9,8},{10,9... | collective-permute-start | bytes 786440 | tf_op jit(solution)/shard_map/ppermute | solution.py:247
where the time goes:
time: 102 us; the launch traced here: 100 us
  Pallas kernels  29.9 us (29%)
  starting transfers between devices  26.9 us (26%)
  waiting for transfers between devices  22.7 us (22%)
  local copies, waits for them, and re-layouts  10.8 us (11%)
  matrix products  10.1 us (10%)
    pallas_call x1, Pallas kernels, long_conv(): pl.pallas_call(functools.partial(conv_kernel, rows=rows, rows_b=rows_b, l...  18.6 us
    ppermute x4, waiting for transfers between devices, shift(): lax.ppermute(array, axis, [(i, (i + by) % length) for i in range(length)])  12.5 us
    dot_general x4, matrix products, part(): return jnp.dot(block, rows, preferred_element_type=jnp.float32)  10.1 us
    unnamed x17, local copies, waits for them, and re-layouts  9.93 us
    all_to_all x1, waiting for transfers between devices, per_device(): lax.all_to_all(conv, 'seq', 0, 0, tiled=True).reshape(width, tok_rows)  9.32 us
    all_to_all x1, starting transfers between devices, per_device(): lax.all_to_all(product_t.reshape(seq, width // seq, tok_rows), 'seq', 0,...  8.28 us
    all_to_all x1, starting transfers between devices, per_device(): lax.all_to_all(conv, 'seq', 0, 0, tiled=True).reshape(width, tok_rows)  7.38 us
    ppermute x4, starting transfers between devices, shift(): lax.ppermute(array, axis, [(i, (i + by) % length) for i in range(length)])  6.7 us
  transfers between devices with their start and end apart: 7, of which 4 were waited for; matrix products, arithmetic and copies ran while one was open for 5% of the time, Pallas kernels for 7%

commit v1 on v0

v1 whole, which is shorter than its diff:
```python
import functools

import jax
import jax.numpy as jnp
from jax import lax
from jax.experimental import pallas as pl
from jax.experimental.pallas import tpu as pltpu
from jax.sharding import PartitionSpec as P

TAPS = 3
BLK = 256
TILE = 128
PAD = 8
GRANT = 24
MIB = 1 << 20


def params(mib):
    return pltpu.CompilerParams(vmem_limit_bytes=mib * MIB)


def short_filter(scr, taps_ref, which, keeps_ref, lanes):
    tok_rows = scr.shape[0] - 8
    total = taps_ref[0, which : which + 1, lanes] * scr[8 : 8 + tok_rows, lanes]
    for tap in range(1, TAPS):
        window = scr[8 - tap : 8 - tap + tok_rows, lanes] * keeps_ref[tap - 1]
        total = total + taps_ref[tap, which : which + 1, lanes] * window
    return total


def fill(scr, edge, values):
    scr[6:8, :] = edge.astype(jnp.float32)
    scr[8:, :] = values.astype(jnp.float32)


def fill_keeps(lengths_ref, keeps_ref):
    @pl.when(pl.program_id(0) == 0)
    def _():
        _, tok_rows, width = keeps_ref.shape
        place = lax.axis_index("seq") * tok_rows
        positions = place + lax.broadcasted_iota(jnp.int32, (tok_rows, width), 0)
        starts = jnp.zeros((tok_rows, width), jnp.int32)
        offset = jnp.int32(0)
        for prompt in range(lengths_ref.shape[0]):
            starts = jnp.where(positions >= offset, offset, starts)
            offset = offset + lengths_ref[prompt]
        for tap in range(1, TAPS):
            keeps_ref[tap - 1] = (positions - tap >= starts).astype(jnp.float32)


def lane_parts(width):
    return [slice(i, i + TILE) for i in range(0, width, TILE)]


def product_kernel(lengths_ref, k_ref, v_ref, edge_ref, taps_ref, out_ref, keeps_ref, scr_k, scr_v):
    fill_keeps(lengths_ref, keeps_ref)
    fill(scr_k, edge_ref[:, 1, :], k_ref[...])
    fill(scr_v, edge_ref[:, 2, :], v_ref[...])
    for lanes in lane_parts(k_ref.shape[1]):
        product = short_filter(scr_k, taps_ref, 1, keeps_ref, lanes) * short_filter(
            scr_v, taps_ref, 2, keeps_ref, lanes
        )
        out_ref[lanes, :] = product.T.astype(jnp.bfloat16)


def query_kernel(lengths_ref, q_ref, edge_ref, taps_ref, out_ref, keeps_ref, scr_q):
    fill_keeps(lengths_ref, keeps_ref)
    fill(scr_q, edge_ref[:, 0, :], q_ref[...])
    for lanes in lane_parts(q_ref.shape[1]):
        out_ref[:, lanes] = short_filter(scr_q, taps_ref, 0, keeps_ref, lanes).astype(jnp.bfloat16)


def short_call(kernel, lengths, by_kind, edge, taps, kinds, transposed, width=256):
    _, tok_rows, channels = by_kind.shape
    if transposed:
        shape, spec = (channels, tok_rows), pl.BlockSpec((width, tok_rows), lambda i: (i, 0))
    else:
        shape, spec = (tok_rows, channels), pl.BlockSpec((tok_rows, width), lambda i: (0, i))
    return pl.pallas_call(
        kernel,
        grid=(channels // width,),
        out_shape=jax.ShapeDtypeStruct(shape, jnp.bfloat16),
        in_specs=[pl.BlockSpec(memory_space=pltpu.SMEM)]
        + [pl.BlockSpec((None, tok_rows, width), lambda i, kind=kind: (kind, 0, i)) for kind in kinds]
        + [
            pl.BlockSpec((TAPS - 1, 3, width), lambda i: (0, 0, i)),
            pl.BlockSpec((TAPS, 3, width), lambda i: (0, 0, i)),
        ],
        out_specs=spec,
        scratch_shapes=[pltpu.VMEM((TAPS - 1, tok_rows, TILE), jnp.float32)]
        + [pltpu.VMEM((tok_rows + 8, width), jnp.float32)] * len(kinds),
        compiler_params=params(GRANT),
        cost_estimate=pl.CostEstimate(flops=20 * tok_rows * channels, bytes_accessed=2 * MIB, transcendentals=0),
    )(lengths, *([by_kind] * len(kinds)), edge, taps)


def over_rows(lengths_ref, body):
    def prompt_step(prompt, carry):
        offset, row = carry
        end = offset + lengths_ref[prompt]
        first, last = offset // BLK, (end - 1) // BLK

        def block_step(block, _):
            body(row + block - first, block, offset, end)
            return 0

        lax.fori_loop(first, last + 1, block_step, 0)
        return end, row + last - first + 1

    lax.fori_loop(0, lengths_ref.shape[0], prompt_step, (jnp.int32(0), jnp.int32(0)))


def rows_before(lengths_ref, rows):
    row_ids = lax.broadcasted_iota(jnp.int32, (rows, TILE), 0)
    firsts = jnp.zeros((rows, TILE), jnp.int32)
    offset, row = jnp.int32(0), jnp.int32(0)
    for prompt in range(lengths_ref.shape[0]):
        firsts = jnp.where(row_ids >= row, row, firsts)
        end = offset + lengths_ref[prompt]
        row = row + (end - 1) // BLK - offset // BLK + 1
        offset = end
    return row_ids - firsts


def lanes_of(block, start, end, rows):
    positions = block * BLK + lax.broadcasted_iota(jnp.int32, (rows, BLK), 1)
    return (positions >= start) & (positions < end)


def conv_kernel(lengths_ref, signal_ref, taps_ref, out_ref, spread, result, before, toep, *, rows, rows_b):
    step = pl.program_id(0)
    devices, channels, _ = signal_ref.shape
    group, span = taps_ref.shape
    lags = span // BLK + 1
    tiles = span // TILE + 1
    pitch = PAD + rows_b

    @pl.when(step == 0)
    def _():
        def place(row, block, start, end):
            slab = jnp.where(lanes_of(block, start, end, channels), signal_ref[block].astype(jnp.float32), 0.0)
            for h in range(2):
                spread[h, pl.ds(PAD + row, channels, stride=pitch), :] = slab[:, h * TILE : (h + 1) * TILE]

        over_rows(lengths_ref, place)
        before[...] = rows_before(lengths_ref, rows_b)

    views = spread.reshape(2, channels, pitch, TILE)
    zero = jnp.zeros((TILE, TILE), jnp.bfloat16)
    behind = before[...]

    def tile(g, t):
        return toep[g, t * TILE : (t + 1) * TILE, :] if 0 <= t < tiles else zero

    for g in range(group):
        channel = step * group + g
        row = jnp.concatenate([taps_ref[g : g + 1, :], jnp.zeros((1, TILE), jnp.float32)], 1)
        sheared = pltpu.roll(jnp.broadcast_to(row, (TILE, span + TILE)), 0, 1, stride=1, stride_axis=0)
        for t in range(tiles):
            toep[g, t * TILE : (t + 1) * TILE, :] = sheared[:, t * TILE : (t + 1) * TILE].astype(jnp.bfloat16)
        total = None
        for lag in range(lags):
            kept = behind >= lag
            left = jnp.concatenate(
                [
                    jnp.where(kept, views[h, channel, PAD - lag : PAD - lag + rows_b, :], 0.0).astype(jnp.bfloat16)
                    for h in range(2)
                ],
                1,
            )
            t = 2 * lag
            right = jnp.concatenate(
                [
                    jnp.concatenate([tile(g, t), tile(g, t + 1)], 1),
                    jnp.concatenate([tile(g, t - 1), tile(g, t)], 1),
                ],
                0,
            )
            term = jnp.dot(left, right, preferred_element_type=jnp.float32)
            total = term if total is None else total + term
        for h in range(2):
            result[h, pl.ds(channel * rows, rows), :] = total[:rows, h * TILE : (h + 1) * TILE]

    @pl.when(step == pl.num_programs(0) - 1)
    def _():
        def collect(row, block, start, end):
            slab = jnp.concatenate([result[h, pl.ds(row, channels, stride=rows), :] for h in range(2)], 1)
            old = out_ref[block].astype(jnp.float32)
            out_ref[block] = jnp.where(lanes_of(block, start, end, channels), slab, old).astype(jnp.bfloat16)

        over_rows(lengths_ref, collect)


def long_conv(lengths, signal, taps, group=16):
    devices, channels, _ = signal.shape
    span = taps.shape[1]
    rows = -(-(devices + lengths.shape[0] - 1) // 8) * 8
    rows_b = -(-rows // 16) * 16
    return pl.pallas_call(
        functools.partial(conv_kernel, rows=rows, rows_b=rows_b),
        grid=(channels // group,),
        out_shape=jax.ShapeDtypeStruct(signal.shape, jnp.bfloat16),
        in_specs=[
            pl.BlockSpec(memory_space=pltpu.SMEM),
            pl.BlockSpec(signal.shape, lambda i: (0, 0, 0)),
            pl.BlockSpec((group, span), lambda i: (i, 0)),
        ],
        out_specs=pl.BlockSpec(signal.shape, lambda i: (0, 0, 0)),
        scratch_shapes=[
            pltpu.VMEM((2, channels * (PAD + rows_b), TILE), jnp.float32),
            pltpu.VMEM((2, channels * rows, TILE), jnp.float32),
            pltpu.VMEM((rows_b, TILE), jnp.int32),
            pltpu.VMEM((group, span + TILE, TILE), jnp.bfloat16),
        ],
        compiler_params=params(GRANT),
        cost_estimate=pl.CostEstimate(
            flops=2 * channels * rows * (span + BLK) * BLK, bytes_accessed=2 * MIB, transcendentals=0
        ),
    )(lengths, signal, taps)


def gate_kernel(query_ref, conv_ref, *out_refs):
    conv = conv_ref[...].astype(jnp.float32).T
    gated = (query_ref[...].astype(jnp.float32) * conv).astype(jnp.bfloat16)
    rows = gated.shape[0] // len(out_refs)
    for i, out_ref in enumerate(out_refs):
        out_ref[...] = gated[i * rows : (i + 1) * rows]


def gate(query, conv_t, pieces=2, width=256):
    tok_rows, channels = query.shape
    rows = tok_rows // pieces
    return pl.pallas_call(
        gate_kernel,
        grid=(channels // width,),
        out_shape=[jax.ShapeDtypeStruct((rows, channels), jnp.bfloat16)] * pieces,
        in_specs=[
            pl.BlockSpec((tok_rows, width), lambda i: (0, i)),
            pl.BlockSpec((width, tok_rows), lambda i: (i, 0)),
        ],
        out_specs=[pl.BlockSpec((rows, width), lambda i: (0, i))] * pieces,
        compiler_params=params(GRANT),
        cost_estimate=pl.CostEstimate(flops=tok_rows * channels, bytes_accessed=2 * MIB, transcendentals=0),
    )(query, conv_t)


def shift(array, axis, by):
    length = lax.axis_size(axis)
    return lax.ppermute(array, axis, [(i, (i + by) % length) for i in range(length)])


def project_kernel(*refs, count, pieces, has_total):
    blocks, weights = refs[: count * pieces], refs[count * pieces : count * (pieces + 1)]
    out_ref = refs[-1]
    total = refs[count * (pieces + 1)][...] if has_total else None
    for i in range(count):
        block = jnp.concatenate([ref[...] for ref in blocks[i * pieces : (i + 1) * pieces]], 0)
        term = jnp.dot(block, weights[i][...], preferred_element_type=jnp.float32)
        total = term if total is None else total + term
    out_ref[...] = total.astype(out_ref.dtype)


def project_part(blocks, weights, total, kind):
    count, pieces = len(blocks), len(blocks[0])
    rows, depth = blocks[0][0].shape
    columns = weights[0].shape[1]
    tok_rows = rows * pieces
    operands = [piece for block in blocks for piece in block] + weights + ([] if total is None else [total])
    return pl.pallas_call(
        functools.partial(project_kernel, count=count, pieces=pieces, has_total=total is not None),
        out_shape=jax.ShapeDtypeStruct((tok_rows, columns), kind),
        compiler_params=params(GRANT),
        cost_estimate=pl.CostEstimate(
            flops=2 * count * tok_rows * depth * columns,
            bytes_accessed=2 * count * depth * columns,
            transcendentals=0,
        ),
    )(*operands)


def project(pieces, w_out):
    size = lax.axis_size("ch")
    place = lax.axis_index("ch")
    depth = pieces[0].shape[1]
    own, after, far_rows, before = (
        lax.dynamic_slice_in_dim(w_out, (place + i) % size * depth, depth, 0) for i in range(size)
    )
    up, down = pieces
    right_up, left_down = shift(up, "ch", 1), shift(down, "ch", -1)
    right_down, left_up = shift(down, "ch", 1), shift(up, "ch", -1)
    far_up, far_down = shift(right_up, "ch", 1), shift(left_down, "ch", -1)
    total = project_part([(up, down)], [own], None, jnp.float32)
    near = [(right_up, right_down), (left_up, left_down)]
    total = project_part(near, [before, after], total, jnp.float32)
    return project_part([(far_up, far_down)], [far_rows], total, jnp.bfloat16)


def per_device(qkv, short_taps, lengths, filter_taps, w_out):
    tok_rows, _, width = qkv.shape
    lead = TAPS - 1
    seq = lax.axis_size("seq")
    edge = lax.ppermute(qkv[tok_rows - lead :], "seq", [(i, i + 1) for i in range(seq - 1)])
    by_kind = qkv.transpose(1, 0, 2)
    product_t = short_call(product_kernel, lengths, by_kind, edge, short_taps, (1, 2), True)
    query = short_call(query_kernel, lengths, by_kind, edge, short_taps, (0,), False)
    signal = lax.all_to_all(product_t.reshape(seq, width // seq, tok_rows), "seq", 0, 0, tiled=True)
    conv = long_conv(lengths, signal, filter_taps[0])
    conv_t = lax.all_to_all(conv, "seq", 0, 0, tiled=True).reshape(width, tok_rows)
    return project(gate(query, conv_t), w_out)


def solution(mesh):
    placed = (P("seq", None, "ch"), P(None, None, "ch"), P(), P("ch", "seq", None), P(None, "ch"))
    return jax.shard_map(
        per_device, mesh=mesh, in_specs=placed, out_specs=P("seq", "ch"), check_vma=False
    )
```

time: 102 us -> 80.4 us (0.79); the launches traced: 100 us -> 80 us
  blocking collectives: 0 us -> 19.6 us
  Pallas kernels: 29.9 us -> 17.8 us
  matrix products: 10.1 us -> 0 us
  starting transfers between devices: 26.9 us -> 17.8 us
  waiting for transfers between devices: 22.7 us -> 16.5 us
  local copies, waits for them, and re-layouts: 10.8 us -> 8.14 us
    all_to_all x0 -> x1, blocking collectives: none -> 19.6 us  [per_device(): lax.all_to_all(product_t.reshape(seq, width // seq, tok_rows), 'seq', 0,...]
    pallas_call x3 -> x5, Pallas kernels: 24.2 us -> 14 us  [the longest x1 9.9 us: long_conv(): pl.pallas_call(functools.partial(conv_kernel, rows=rows, rows_b=rows_b),...]
    dot_general x4 -> x0, matrix products: 10.1 us -> none  [part(): return jnp.dot(block, rows, preferred_element_type=jnp.float32)]
    all_to_all x1 -> x0, starting transfers between devices: 8.28 us -> none  [per_device(): lax.all_to_all(product_t.reshape(seq, width // seq, tok_rows), 'seq', 0,...]
    unnamed x17 -> x15, local copies, waits for them, and re-layouts: 9.93 us -> 2.88 us
    ppermute x4 -> x6, waiting for transfers between devices: 12.5 us -> 5.63 us  [shift(): lax.ppermute(array, axis, [(i, (i + by) % length) for i in range(length)])]
    dynamic_slice x0 -> x1, local copies, waits for them, and re-layouts: none -> 4.45 us  [project(): lax.dynamic_slice_in_dim(w_out, (place + i) % size * depth, depth, 0)]
    all_to_all x1, starting transfers between devices: 7.38 us -> 3.99 us  [per_device(): lax.all_to_all(conv, 'seq', 0, 0, tiled=True).reshape(width, tok_rows)]
  transfers between devices with their start and end apart: 7 -> 8, of which waited for: 4 -> 4; matrix products, arithmetic and copies ran while one was open for 5% -> 6% of each run, Pallas kernels for 7% -> 4%
where the time goes in v1:
time: 80.4 us; the launch traced here: 80 us
  blocking collectives  19.6 us (24%)
  starting transfers between devices  17.8 us (22%)
  Pallas kernels  17.8 us (22%)
  waiting for transfers between devices  16.5 us (21%)
  local copies, waits for them, and re-layouts  8.14 us (10%)
    all_to_all x1, blocking collectives, per_device(): lax.all_to_all(product_t.reshape(seq, width // seq, tok_rows), 'seq', 0,...  19.6 us
    all_to_all x1, waiting for transfers between devices, per_device(): lax.all_to_all(conv, 'seq', 0, 0, tiled=True).reshape(width, tok_rows)  10.1 us
    pallas_call x1, Pallas kernels, long_conv(): pl.pallas_call(functools.partial(conv_kernel, rows=rows, rows_b=rows_b),...  9.9 us
    ppermute x6, starting transfers between devices, shift(): lax.ppermute(array, axis, [(i, (i + by) % length) for i in range(length)])  9.26 us
    ppermute x6, waiting for transfers between devices, shift(): lax.ppermute(array, axis, [(i, (i + by) % length) for i in range(length)])  5.63 us
    ppermute x1, starting transfers between devices, per_device(): lax.ppermute(qkv[tok_rows - lead:], 'seq', [(i, i + 1) for i in range(seq...  4.51 us
    dynamic_slice x1, local copies, waits for them, and re-layouts, project(): lax.dynamic_slice_in_dim(w_out, (place + i) % size * depth, depth, 0)  4.45 us
    all_to_all x1, starting transfers between devices, per_device(): lax.all_to_all(conv, 'seq', 0, 0, tiled=True).reshape(width, tok_rows)  3.99 us
  transfers between devices with their start and end apart: 8, of which 4 were waited for; matrix products, arithmetic and copies ran while one was open for 6% of the time, Pallas kernels for 4%

profile of v1, /device:TPU:1, one launch (start us, length us, event | category | flops | bytes accessed | tf_op | source)
XLA Modules:
  0.0 80.0 jit_solution(6272438886668828420)
XLA Ops:
  0.0 0.8 %slice.3 = bf16[2,3,1024]{2,0,1:T(2,128)(2,1)S(1)} slice(bf16[256,3,1024]{2,0,1:T(8,128)(2,1)} %param.5), slice={[254:256], [0:3], [0:1024]} | slice | bytes 24576 | tf_op jit(solution)/shard_map/slice | solution.py:302
  0.8 4.5 %collective-permute-start = (bf16[2,3,1024]{2,1,0:T(4,128)(2,1)S(1)}, bf16[2,3,1024]{2,1,0:T(4,128)(2,1)S(1)}, u32[]{:S(2)}, u32[]{:S(2)}) collective-permute-start(bf16[2,3,1024]{2,1,0:T(4,128)(2,1)S(1)} %copy.7), channel_id=1, source_target_pairs={{0,4},{4,8},{8,12},{12,16},{16,20},{20,24},{24,28},{28,32},{32,36}... | collective-permute-start | bytes 36872 | tf_op jit(solution)/shard_map/ppermute | solution.py:302
  5.3 0.8 %collective-permute-done.edge_ref = bf16[2,3,1024]{2,1,0:T(4,128)(2,1)S(1)} collective-permute-done((bf16[2,3,1024]{2,1,0:T(4,128)(2,1)S(1)}, bf16[2,3,1024]{2,1,0:T(4,128)(2,1)S(1)}, u32[]{:S(2)}, u32[]{:S(2)}) %collective-permute-start) | collective-permute-done | bytes 12320 | tf_op jit(solution)/shard_map/ppermute | solution.py:302
  6.2 0.0 copy-start
  6.2 1.4 %copy-done = bf16[256,3,1024]{2,0,1:T(8,128)(2,1)S(1)} copy-done((bf16[256,3,1024]{2,0,1:T(8,128)(2,1)S(1)}, bf16[256,3,1024]{2,0,1:T(8,128)(2,1)}, u32[]{:S(2)}) %copy-start) | copy-done | bytes 1572888
  7.6 0.0 copy-start.2
  7.6 0.8 copy-done.2
  8.4 0.0 copy-start.4
  8.4 0.7 copy-done.4
  9.1 0.0 copy-start.6
  9.1 2.3 %shard_map.56 = bf16[1024,256]{1,0:T(8,128)(2,1)S(1)} custom-call(s32[8]{0:T(128)S(1)} %copy-done.4, bf16[3,256,1024]{2,1,0:T(8,128)(2,1)S(1)} %bitcast.4, bf16[3,256,1024]{2,1,0:T(8,128)(2,1)S(1)} %bitcast.5, bf16[2,3,1024]{2,1,0:T(4,128)(2,1)S(1)} %collective-permute-done.edge_ref, f32[3,3,1024]{2,1,0:T(4,128)S(1)} %copy-done.2), custom_call_target="tpu_custom_call" | custom-call | flops 5242880 | bytes 2097152 | tf_op jit(solution)/shard_map/pallas_call | solution.py:79
  11.3 19.6 %all_to_all.10.signal_ref = bf16[32,32,256]{2,1,0:T(8,128)(2,1)S(1)} all-to-all(bf16[32,32,256]{2,1,0:T(8,128)(2,1)S(1)} %bitcast.8), channel_id=1, replica_groups=mesh['seq'=32,'ch'=4] {'seq'}, dimensions={0} | all-to-all | bytes 1048576 | tf_op jit(solution)/shard_map/all_to_all | solution.py:306
  31.0 0.0 copy-done.6
  31.0 0.0 copy-start.1
  31.0 0.0 copy-start.3
  31.0 0.0 copy-start.5
  31.0 9.9 %shard_map.57 = bf16[32,32,256]{2,1,0:T(8,128)(2,1)} custom-call(s32[8]{0:T(128)S(1)} %copy-done.4, bf16[32,32,256]{2,1,0:T(8,128)(2,1)S(1)} %all_to_all.10.signal_ref, f32[32,2048]{1,0:T(8,128)S(1)} %bitcast.9), custom_call_target="tpu_custom_call" | custom-call | flops 1509949440 | bytes 2097152 | tf_op jit(solution)/shard_map/pallas_call | solution.py:199
  40.9 4.0 %all-to-all-start.1 = ((bf16[32,32,256]{2,1,0:T(8,128)(2,1)}), bf16[32,32,256]{2,1,0:T(8,128)(2,1)S(1)}, u32[]{:S(2)}, u32[]{:S(2)}) async-start(bf16[32,32,256]{2,1,0:T(8,128)(2,1)} %shard_map.57), calls=%async_computation.1 | async-start | bytes 1048576 | tf_op jit(solution)/shard_map/all_to_all | solution.py:308
  44.9 0.0 copy-done.1
  44.9 0.0 copy-done.3
  44.9 0.0 copy-done.5
  44.9 1.6 %shard_map.55.query_ref = bf16[256,1024]{1,0:T(8,128)(2,1)S(1)} custom-call(s32[8]{0:T(128)S(1)} %copy-done.5, bf16[3,256,1024]{2,1,0:T(8,128)(2,1)S(1)} %bitcast.6, bf16[2,3,1024]{2,1,0:T(4,128)(2,1)S(1)} %collective-permute-done.edge_ref, f32[3,3,1024]{2,1,0:T(4,128)S(1)} %copy-done.3), custom_call_target="tpu_custom_call" | custom-call | flops 5242880 | bytes 2097152 | tf_op jit(solution)/shard_map/pallas_call | solution.py:79
  46.5 10.1 %all-to-all-done.1 = bf16[32,32,256]{2,1,0:T(8,128)(2,1)S(1)} async-done(((bf16[32,32,256]{2,1,0:T(8,128)(2,1)}), bf16[32,32,256]{2,1,0:T(8,128)(2,1)S(1)}, u32[]{:S(2)}, u32[]{:S(2)}) %all-to-all-start.1) | async-done | bytes 524320 | tf_op jit(solution)/shard_map/all_to_all | solution.py:308
  56.5 0.6 shard_map.58
  57.2 1.7 %collective-permute-start.1 = (bf16[128,1024]{1,0:T(8,128)(2,1)S(1)}, bf16[128,1024]{1,0:T(8,128)(2,1)S(1)}, u32[]{:S(2)}, u32[]{:S(2)}) collective-permute-start(bf16[128,1024]{1,0:T(8,128)(2,1)S(1)} %get-tuple-element.7.refs_0_), channel_id=1, source_target_pairs={{0,1},{1,2},{2,3},{3,0},{4,5},{5,6},{6,7},{7,4},{8,9},{9,10},{10,1... | collective-permute-start | bytes 786440 | tf_op jit(solution)/shard_map/ppermute | solution.py:249
  58.9 2.2 %collective-permute-start.3 = (bf16[128,1024]{1,0:T(8,128)(2,1)S(1)}, bf16[128,1024]{1,0:T(8,128)(2,1)S(1)}, u32[]{:S(2)}, u32[]{:S(2)}) collective-permute-start(bf16[128,1024]{1,0:T(8,128)(2,1)S(1)} %get-tuple-element.8.refs_1_), channel_id=1, source_target_pairs={{0,3},{1,0},{2,1},{3,2},{4,7},{5,4},{6,5},{7,6},{8,11},{9,8},{10,9... | collective-permute-start | bytes 786440 | tf_op jit(solution)/shard_map/ppermute | solution.py:249
  61.1 0.0 collective-permute-start.5
  61.1 2.7 %collective-permute-start.6 = (bf16[128,1024]{1,0:T(8,128)(2,1)S(1)}, bf16[128,1024]{1,0:T(8,128)(2,1)S(1)}, u32[]{:S(2)}, u32[]{:S(2)}) collective-permute-start(bf16[128,1024]{1,0:T(8,128)(2,1)S(1)} %get-tuple-element.7.refs_0_), channel_id=1, source_target_pairs={{0,3},{1,0},{2,1},{3,2},{4,7},{5,4},{6,5},{7,6},{8,11},{9,8},{10,9... | collective-permute-start | bytes 786440 | tf_op jit(solution)/shard_map/ppermute | solution.py:249
  63.8 3.5 %collective-permute-done.1.refs_0_ = bf16[128,1024]{1,0:T(8,128)(2,1)S(1)} collective-permute-done((bf16[128,1024]{1,0:T(8,128)(2,1)S(1)}, bf16[128,1024]{1,0:T(8,128)(2,1)S(1)}, u32[]{:S(2)}, u32[]{:S(2)}) %collective-permute-start.1) | collective-permute-done | bytes 262176 | tf_op jit(solution)/shard_map/ppermute | solution.py:249
  67.3 0.0 collective-permute-start.2
  67.3 0.0 collective-permute-done.3.refs_3_
  67.3 2.7 %collective-permute-start.4 = (bf16[128,1024]{1,0:T(8,128)(2,1)S(1)}, bf16[128,1024]{1,0:T(8,128)(2,1)S(1)}, u32[]{:S(2)}, u32[]{:S(2)}) collective-permute-start(bf16[128,1024]{1,0:T(8,128)(2,1)S(1)} %collective-permute-done.3.refs_3_), channel_id=1, source_target_pairs={{0,3},{1,0},{2,1},{3,2},{4,7},{5,4},{6,5},{7,6},{8,11},{9,8},{10,9... | collective-permute-start | bytes 786440 | tf_op jit(solution)/shard_map/ppermute | solution.py:249
  70.0 4.4 %constant_dynamic-slice_fusion = (bf16[1024,1024]{1,0:T(8,128)(2,1)S(1)}, bf16[1024,1024]{1,0:T(8,128)(2,1)S(1)}, bf16[1024,1024]{1,0:T(8,128)(2,1)S(1)}, bf16[1024,1024]{1,0:T(8,128)(2,1)S(1)}) fusion(bf16[4096,1024]{1,0:T(8,128)(2,1)} %param.9, s32[]{:T(128)S(6)} %select_n.38, s32[]{:T(128)S(6)} %select_n.34, s32[]{:T(128)S(6)} %select_n.32, s32[]{:T(128)S(6)} %select_n.36), kind=kLoop, calls=%fused_computation | loop fusion | bytes 16777232 | tf_op jit(solution)/shard_map/dynamic_slice | solution.py:286
  74.4 0.7 shard_map.59.refs_6_
  75.1 0.0 collective-permute-done.5.refs_1_
  75.1 0.0 collective-permute-done.6.refs_2_
  75.2 1.3 %shard_map.60.refs_3_ = f32[256,1024]{1,0:T(8,128)S(1)} custom-call(bf16[128,1024]{1,0:T(8,128)(2,1)S(1)} %collective-permute-done.1.refs_0_, bf16[128,1024]{1,0:T(8,128)(2,1)S(1)} %collective-permute-done.5.refs_1_, bf16[128,1024]{1,0:T(8,128)(2,1)S(1)} %collective-permute-done.6.refs_2_, bf16[128,1024]{1,0:T(8,128)(2,1)S(1)} %collective-permute-done.3.refs_3_, ...), custom_call_target="tpu_custom_call" | custom-call | flops 1073741824 | bytes 4194304 | tf_op jit(solution)/shard_map/pallas_call | solution.py:269
  76.4 2.1 %collective-permute-done.2.refs_0_ = bf16[128,1024]{1,0:T(8,128)(2,1)S(1)} collective-permute-done((bf16[128,1024]{1,0:T(8,128)(2,1)S(1)}, bf16[128,1024]{1,0:T(8,128)(2,1)S(1)}, u32[]{:S(2)}, u32[]{:S(2)}) %collective-permute-start.2) | collective-permute-done | bytes 262176 | tf_op jit(solution)/shard_map/ppermute | solution.py:249
  78.5 0.0 collective-permute-done.4.refs_1_
  78.5 1.5 %shard_map.61 = bf16[256,1024]{1,0:T(8,128)(2,1)} custom-call(bf16[128,1024]{1,0:T(8,128)(2,1)S(1)} %collective-permute-done.2.refs_0_, bf16[128,1024]{1,0:T(8,128)(2,1)S(1)} %collective-permute-done.4.refs_1_, bf16[1024,1024]{1,0:T(8,128)(2,1)S(1)} %get-tuple-element.11.refs_2_, f32[256,1024]{1,0:T(8,128)S(1)} %shard_map.60.refs_3_), custom_call_target="tpu_custom_call" | custom-call | flops 536870912 | bytes 2097152 | tf_op jit(solution)/shard_map/pallas_call | solution.py:269
  (1 shorter events, 0.0 us)
Async XLA Ops:
  0.8 5.4 %collective-permute-start = (bf16[2,3,1024]{2,1,0:T(4,128)(2,1)S(1)}, bf16[2,3,1024]{2,1,0:T(4,128)(2,1)S(1)}, u32[]{:S(2)}, u32[]{:S(2)}) collective-permute-start(bf16[2,3,1024]{2,1,0:T(4,128)(2,1)S(1)} %copy.7), channel_id=1, source_target_pairs={{0,4},{4,8},{8,12},{12,16},{16,20},{20,24},{24,28},{28,32},{32,36}... | collective-permute-start | bytes 36872 | tf_op jit(solution)/shard_map/ppermute | solution.py:302
  6.2 1.4 %copy-start = (bf16[256,3,1024]{2,0,1:T(8,128)(2,1)S(1)}, bf16[256,3,1024]{2,0,1:T(8,128)(2,1)}, u32[]{:S(2)}) copy-start(bf16[256,3,1024]{2,0,1:T(8,128)(2,1)} %param.5) | copy-start | bytes 4718596
  7.6 0.8 copy-start.2
  8.4 0.7 copy-start.4
  9.1 21.9 %copy-start.6 = (f32[1,32,2048]{2,1,0:T(8,128)S(1)}, f32[1,32,2048]{2,1,0:T(8,128)}, u32[]{:S(2)}) copy-start(f32[1,32,2048]{2,1,0:T(8,128)} %param.8) | copy-start | bytes 786436
  31.0 13.9 %copy-start.1 = (bf16[256,3,1024]{2,0,1:T(8,128)(2,1)S(1)}, bf16[256,3,1024]{2,0,1:T(8,128)(2,1)}, u32[]{:S(2)}) copy-start(bf16[256,3,1024]{2,0,1:T(8,128)(2,1)} %param.5) | copy-start | bytes 4718596
  31.0 13.9 %copy-start.3 = (f32[3,3,1024]{2,1,0:T(4,128)S(1)}, f32[3,3,1024]{2,1,0:T(4,128)}, u32[]{:S(2)}) copy-start(f32[3,3,1024]{2,1,0:T(4,128)} %taps_ref.3) | copy-start | bytes 110596
  31.0 13.9 %copy-start.5 = (s32[8]{0:T(128)S(1)}, s32[8]{0:T(128)}, u32[]{:S(2)}) copy-start(s32[8]{0:T(128)} %lengths_ref.5) | copy-start | bytes 100
  40.9 15.7 %all-to-all-start.1 = ((bf16[32,32,256]{2,1,0:T(8,128)(2,1)}), bf16[32,32,256]{2,1,0:T(8,128)(2,1)S(1)}, u32[]{:S(2)}, u32[]{:S(2)}) async-start(bf16[32,32,256]{2,1,0:T(8,128)(2,1)} %shard_map.57), calls=%async_computation.1 | async-start | bytes 1048576 | tf_op jit(solution)/shard_map/all_to_all | solution.py:308
  57.2 10.1 %collective-permute-start.1 = (bf16[128,1024]{1,0:T(8,128)(2,1)S(1)}, bf16[128,1024]{1,0:T(8,128)(2,1)S(1)}, u32[]{:S(2)}, u32[]{:S(2)}) collective-permute-start(bf16[128,1024]{1,0:T(8,128)(2,1)S(1)} %get-tuple-element.7.refs_0_), channel_id=1, source_target_pairs={{0,1},{1,2},{2,3},{3,0},{4,5},{5,6},{6,7},{7,4},{8,9},{9,10},{10,1... | collective-permute-start | bytes 786440 | tf_op jit(solution)/shard_map/ppermute | solution.py:249
  58.9 8.4 %collective-permute-start.3 = (bf16[128,1024]{1,0:T(8,128)(2,1)S(1)}, bf16[128,1024]{1,0:T(8,128)(2,1)S(1)}, u32[]{:S(2)}, u32[]{:S(2)}) collective-permute-start(bf16[128,1024]{1,0:T(8,128)(2,1)S(1)} %get-tuple-element.8.refs_1_), channel_id=1, source_target_pairs={{0,3},{1,0},{2,1},{3,2},{4,7},{5,4},{6,5},{7,6},{8,11},{9,8},{10,9... | collective-permute-start | bytes 786440 | tf_op jit(solution)/shard_map/ppermute | solution.py:249
  61.1 14.1 %collective-permute-start.5 = (bf16[128,1024]{1,0:T(8,128)(2,1)S(1)}, bf16[128,1024]{1,0:T(8,128)(2,1)S(1)}, u32[]{:S(2)}, u32[]{:S(2)}) collective-permute-start(bf16[128,1024]{1,0:T(8,128)(2,1)S(1)} %get-tuple-element.8.refs_1_), channel_id=1, source_target_pairs={{0,1},{1,2},{2,3},{3,0},{4,5},{5,6},{6,7},{7,4},{8,9},{9,10},{10,1... | collective-permute-start | bytes 786440 | tf_op jit(solution)/shard_map/ppermute | solution.py:249
  61.1 14.1 %collective-permute-start.6 = (bf16[128,1024]{1,0:T(8,128)(2,1)S(1)}, bf16[128,1024]{1,0:T(8,128)(2,1)S(1)}, u32[]{:S(2)}, u32[]{:S(2)}) collective-permute-start(bf16[128,1024]{1,0:T(8,128)(2,1)S(1)} %get-tuple-element.7.refs_0_), channel_id=1, source_target_pairs={{0,3},{1,0},{2,1},{3,2},{4,7},{5,4},{6,5},{7,6},{8,11},{9,8},{10,9... | collective-permute-start | bytes 786440 | tf_op jit(solution)/shard_map/ppermute | solution.py:249
  67.3 11.2 %collective-permute-start.2 = (bf16[128,1024]{1,0:T(8,128)(2,1)S(1)}, bf16[128,1024]{1,0:T(8,128)(2,1)S(1)}, u32[]{:S(2)}, u32[]{:S(2)}) collective-permute-start(bf16[128,1024]{1,0:T(8,128)(2,1)S(1)} %collective-permute-done.1.refs_0_), channel_id=1, source_target_pairs={{0,1},{1,2},{2,3},{3,0},{4,5},{5,6},{6,7},{7,4},{8,9},{9,10},{10,1... | collective-permute-start | bytes 786440 | tf_op jit(solution)/shard_map/ppermute | solution.py:249
  67.3 11.2 %collective-permute-start.4 = (bf16[128,1024]{1,0:T(8,128)(2,1)S(1)}, bf16[128,1024]{1,0:T(8,128)(2,1)S(1)}, u32[]{:S(2)}, u32[]{:S(2)}) collective-permute-start(bf16[128,1024]{1,0:T(8,128)(2,1)S(1)} %collective-permute-done.3.refs_3_), channel_id=1, source_target_pairs={{0,3},{1,0},{2,1},{3,2},{4,7},{5,4},{6,5},{7,6},{8,11},{9,8},{10,9... | collective-permute-start | bytes 786440 | tf_op jit(solution)/shard_map/ppermute | solution.py:249

commit v2 on v1

--- a/solution.py
+++ b/solution.py
@@ -12,6 +12,7 @@
 TILE = 128
 PAD = 8
 GRANT = 24
+START_GRANT = 60
 MIB = 1 << 20
 
 
@@ -70,7 +71,7 @@
         out_ref[:, lanes] = short_filter(scr_q, taps_ref, 0, keeps_ref, lanes).astype(jnp.bfloat16)
 
 
-def short_call(kernel, lengths, by_kind, edge, taps, kinds, transposed, width=256):
+def short_call(kernel, lengths, by_kind, edge, taps, kinds, transposed, grant, width=512):
     _, tok_rows, channels = by_kind.shape
     if transposed:
         shape, spec = (channels, tok_rows), pl.BlockSpec((width, tok_rows), lambda i: (i, 0))
@@ -89,25 +90,36 @@
         out_specs=spec,
         scratch_shapes=[pltpu.VMEM((TAPS - 1, tok_rows, TILE), jnp.float32)]
         + [pltpu.VMEM((tok_rows + 8, width), jnp.float32)] * len(kinds),
-        compiler_params=params(GRANT),
+        compiler_params=params(grant),
         cost_estimate=pl.CostEstimate(flops=20 * tok_rows * channels, bytes_accessed=2 * MIB, transcendentals=0),
     )(lengths, *([by_kind] * len(kinds)), edge, taps)
 
 
-def over_rows(lengths_ref, body):
-    def prompt_step(prompt, carry):
-        offset, row = carry
+def list_rows(lengths_ref, table, heads, rows):
+    for row in range(rows - lengths_ref.shape[0], rows):
+        for i in range(3):
+            table[i, row] = jnp.int32(0)
+    offset, row = jnp.int32(0), jnp.int32(0)
+    for prompt in range(lengths_ref.shape[0]):
         end = offset + lengths_ref[prompt]
         first, last = offset // BLK, (end - 1) // BLK
-
-        def block_step(block, _):
-            body(row + block - first, block, offset, end)
+        heads[1, prompt] = row
+
+        def note(block, _, row=row, first=first, offset=offset, end=end):
+            at = row + block - first
+            table[0, at] = block
+            table[1, at] = offset
+            table[2, at] = end
+
+            @pl.when(block * BLK >= offset)
+            def _():
+                heads[0, block] = at
+
             return 0
 
-        lax.fori_loop(first, last + 1, block_step, 0)
-        return end, row + last - first + 1
-
-    lax.fori_loop(0, lengths_ref.shape[0], prompt_step, (jnp.int32(0), jnp.int32(0)))
+        lax.fori_loop(first, last + 1, note, 0)
+        row = row + last - first + 1
+        offset = end
 
 
 def rows_before(lengths_ref, rows):
@@ -122,12 +134,16 @@
     return row_ids - firsts
 
 
-def lanes_of(block, start, end, rows):
-    positions = block * BLK + lax.broadcasted_iota(jnp.int32, (rows, BLK), 1)
-    return (positions >= start) & (positions < end)
-
-
-def conv_kernel(lengths_ref, signal_ref, taps_ref, out_ref, spread, result, before, toep, *, rows, rows_b):
+def only_lanes(table, row, values, others):
+    block, start, end = (table[i, row] for i in range(3))
+    positions = block * BLK + lax.broadcasted_iota(jnp.int32, (8, BLK), 1)
+    inside = (positions >= start) & (positions < end)
+    shape = (values.shape[0] // 8, 8, BLK)
+    others = others if isinstance(others, float) else others.reshape(shape)
+    return jnp.where(inside[None], values.reshape(shape), others).reshape(values.shape)
+
+
+def conv_kernel(lengths_ref, signal_ref, taps_ref, out_ref, table, heads, spread, result, before, toep, *, rows, rows_b):
     step = pl.program_id(0)
     devices, channels, _ = signal_ref.shape
     group, span = taps_ref.shape
@@ -137,12 +153,11 @@
 
     @pl.when(step == 0)
     def _():
-        def place(row, block, start, end):
-            slab = jnp.where(lanes_of(block, start, end, channels), signal_ref[block].astype(jnp.float32), 0.0)
+        list_rows(lengths_ref, table, heads, rows)
+        for row in range(rows):
+            slab = only_lanes(table, row, signal_ref[table[0, row]].astype(jnp.float32), 0.0)
             for h in range(2):
                 spread[h, pl.ds(PAD + row, channels, stride=pitch), :] = slab[:, h * TILE : (h + 1) * TILE]
-
-        over_rows(lengths_ref, place)
         before[...] = rows_before(lengths_ref, rows_b)
 
     views = spread.reshape(2, channels, pitch, TILE)
@@ -183,15 +198,19 @@
 
     @pl.when(step == pl.num_programs(0) - 1)
     def _():
-        def collect(row, block, start, end):
-            slab = jnp.concatenate([result[h, pl.ds(row, channels, stride=rows), :] for h in range(2)], 1)
+        def slab_of(row):
+            return jnp.concatenate([result[h, pl.ds(row, channels, stride=rows), :] for h in range(2)], 1)
+
+        for block in range(devices):
+            out_ref[block] = slab_of(heads[0, block]).astype(jnp.bfloat16)
+        for prompt in range(lengths_ref.shape[0]):
+            row = heads[1, prompt]
+            block = table[0, row]
             old = out_ref[block].astype(jnp.float32)
-            out_ref[block] = jnp.where(lanes_of(block, start, end, channels), slab, old).astype(jnp.bfloat16)
-
-        over_rows(lengths_ref, collect)
-
-
-def long_conv(lengths, signal, taps, group=16):
+            out_ref[block] = only_lanes(table, row, slab_of(row), old).astype(jnp.bfloat16)
+
+
+def long_conv(lengths, signal, taps, group=32):
     devices, channels, _ = signal.shape
     span = taps.shape[1]
     rows = -(-(devices + lengths.shape[0] - 1) // 8) * 8
@@ -207,6 +226,8 @@
         ],
         out_specs=pl.BlockSpec(signal.shape, lambda i: (0, 0, 0)),
         scratch_shapes=[
+            pltpu.SMEM((3, rows), jnp.int32),
+            pltpu.SMEM((2, devices), jnp.int32),
             pltpu.VMEM((2, channels * (PAD + rows_b), TILE), jnp.float32),
             pltpu.VMEM((2, channels * rows, TILE), jnp.float32),
             pltpu.VMEM((rows_b, TILE), jnp.int32),
@@ -301,8 +322,8 @@
     seq = lax.axis_size("seq")
     edge = lax.ppermute(qkv[tok_rows - lead :], "seq", [(i, i + 1) for i in range(seq - 1)])
     by_kind = qkv.transpose(1, 0, 2)
-    product_t = short_call(product_kernel, lengths, by_kind, edge, short_taps, (1, 2), True)
-    query = short_call(query_kernel, lengths, by_kind, edge, short_taps, (0,), False)
+    product_t = short_call(product_kernel, lengths, by_kind, edge, short_taps, (1, 2), True, START_GRANT)
+    query = short_call(query_kernel, lengths, by_kind, edge, short_taps, (0,), False, GRANT)
     signal = lax.all_to_all(product_t.reshape(seq, width // seq, tok_rows), "seq", 0, 0, tiled=True)
     conv = long_conv(lengths, signal, filter_taps[0])
     conv_t = lax.all_to_all(conv, "seq", 0, 0, tiled=True).reshape(width, tok_rows)

time: 80.4 us -> 78.6 us (0.978)
  local copies, waits for them, and re-layouts: 8.14 us -> 5.88 us
    unnamed x15 -> x13, local copies, waits for them, and re-layouts: 2.88 us -> 0.62 us
    pallas_call x2, Pallas kernels: 3.81 us -> 4.75 us  [short_call(): pl.pallas_call(kernel, grid=(channels // width,), out_shape=jax.ShapeDtyp...]
  transfers between devices with their start and end apart: 8 -> 8, of which waited for: 4 -> 4; matrix products, arithmetic and copies ran while one was open for 6% -> 6% of each run, Pallas kernels for 4% -> 5%
where the time goes in v2:
time: 78.6 us; the launch traced here: 78.2 us
  blocking collectives  19.8 us (25%)
  Pallas kernels  18 us (23%)
  starting transfers between devices  17.8 us (23%)
  waiting for transfers between devices  16.6 us (21%)
  local copies, waits for them, and re-layouts  5.88 us (7%)
    all_to_all x1, blocking collectives, per_device(): lax.all_to_all(product_t.reshape(seq, width // seq, tok_rows), 'seq', 0,...  19.8 us
    all_to_all x1, waiting for transfers between devices, per_device(): lax.all_to_all(conv, 'seq', 0, 0, tiled=True).reshape(width, tok_rows)  10.1 us
    ppermute x6, starting transfers between devices, shift(): lax.ppermute(array, axis, [(i, (i + by) % length) for i in range(length)])  9.26 us
    pallas_call x1, Pallas kernels, long_conv(): pl.pallas_call(functools.partial(conv_kernel, rows=rows, rows_b=rows_b),...  9.18 us
    ppermute x6, waiting for transfers between devices, shift(): lax.ppermute(array, axis, [(i, (i + by) % length) for i in range(length)])  5.63 us
    pallas_call x2, Pallas kernels, short_call(): pl.pallas_call(kernel, grid=(channels // width,), out_shape=jax.ShapeDtyp...  4.75 us
    ppermute x1, starting transfers between devices, per_device(): lax.ppermute(qkv[tok_rows - lead:], 'seq', [(i, i + 1) for i in range(seq...  4.51 us
    dynamic_slice x1, local copies, waits for them, and re-layouts, project(): lax.dynamic_slice_in_dim(w_out, (place + i) % size * depth, depth, 0)  4.45 us
  transfers between devices with their start and end apart: 8, of which 4 were waited for; matrix products, arithmetic and copies ran while one was open for 6% of the time, Pallas kernels for 5%

profile of v2, /device:TPU:1, one launch (start us, length us, event | category | flops | bytes accessed | tf_op | source)
XLA Modules:
  0.0 78.2 jit_solution(8155799073193828765)
XLA Ops:
  0.0 0.8 %slice.3 = bf16[2,3,1024]{2,0,1:T(2,128)(2,1)S(1)} slice(bf16[256,3,1024]{2,0,1:T(8,128)(2,1)} %param.5), slice={[254:256], [0:3], [0:1024]} | slice | bytes 24576 | tf_op jit(solution)/shard_map/slice | solution.py:323
  0.8 4.5 %collective-permute-start = (bf16[2,3,1024]{2,1,0:T(4,128)(2,1)S(1)}, bf16[2,3,1024]{2,1,0:T(4,128)(2,1)S(1)}, u32[]{:S(2)}, u32[]{:S(2)}) collective-permute-start(bf16[2,3,1024]{2,1,0:T(4,128)(2,1)S(1)} %copy.7), channel_id=1, source_target_pairs={{0,4},{4,8},{8,12},{12,16},{16,20},{20,24},{24,28},{28,32},{32,36}... | collective-permute-start | bytes 36872 | tf_op jit(solution)/shard_map/ppermute | solution.py:323
  5.3 0.8 %collective-permute-done.edge_ref = bf16[2,3,1024]{2,1,0:T(4,128)(2,1)S(1)} collective-permute-done((bf16[2,3,1024]{2,1,0:T(4,128)(2,1)S(1)}, bf16[2,3,1024]{2,1,0:T(4,128)(2,1)S(1)}, u32[]{:S(2)}, u32[]{:S(2)}) %collective-permute-start) | collective-permute-done | bytes 12320 | tf_op jit(solution)/shard_map/ppermute | solution.py:323
  6.2 0.0 copy-start.2
  6.2 0.6 copy-done.2
  6.8 0.0 copy-start.4
  6.8 0.0 copy-start.5
  6.8 3.2 %shard_map.56 = bf16[1024,256]{1,0:T(8,128)(2,1)} custom-call(s32[8]{0:T(128)} %lengths_ref.5, bf16[3,256,1024]{2,1,0:T(8,128)(2,1)} %bitcast.4, bf16[3,256,1024]{2,1,0:T(8,128)(2,1)} %bitcast.5, bf16[2,3,1024]{2,1,0:T(4,128)(2,1)} %copy-done.2, f32[3,3,1024]{2,1,0:T(4,128)} %taps_ref.3), custom_call_target="tpu_custom_call" | custom-call | flops 5242880 | bytes 2097152 | tf_op jit(solution)/shard_map/pallas_call | solution.py:80
  10.0 19.8 %all_to_all.10.signal_ref = bf16[32,32,256]{2,1,0:T(8,128)(2,1)S(1)} all-to-all(bf16[32,32,256]{2,1,0:T(8,128)(2,1)} %bitcast.9), channel_id=1, replica_groups=mesh['seq'=32,'ch'=4] {'seq'}, dimensions={0} | all-to-all | bytes 1048576 | tf_op jit(solution)/shard_map/all_to_all | solution.py:327
  29.8 0.0 copy-done.4
  29.8 0.0 copy-done.5
  29.8 0.0 copy-start
  29.8 0.0 copy-start.1
  29.8 0.0 copy-start.3
  29.8 9.2 %shard_map.57 = bf16[32,32,256]{2,1,0:T(8,128)(2,1)} custom-call(s32[8]{0:T(128)S(1)} %copy-done.4, bf16[32,32,256]{2,1,0:T(8,128)(2,1)S(1)} %all_to_all.10.signal_ref, f32[32,2048]{1,0:T(8,128)S(1)} %bitcast.8), custom_call_target="tpu_custom_call" | custom-call | flops 1509949440 | bytes 2097152 | tf_op jit(solution)/shard_map/pallas_call | solution.py:218
  39.0 4.0 %all-to-all-start.1 = ((bf16[32,32,256]{2,1,0:T(8,128)(2,1)}), bf16[32,32,256]{2,1,0:T(8,128)(2,1)S(1)}, u32[]{:S(2)}, u32[]{:S(2)}) async-start(bf16[32,32,256]{2,1,0:T(8,128)(2,1)} %shard_map.57), calls=%async_computation.1 | async-start | bytes 1048576 | tf_op jit(solution)/shard_map/all_to_all | solution.py:329
  43.0 0.0 copy-done
  43.0 0.0 copy-done.1
  43.0 0.0 copy-done.3
  43.1 1.6 %shard_map.55.query_ref = bf16[256,1024]{1,0:T(8,128)(2,1)S(1)} custom-call(s32[8]{0:T(128)S(1)} %copy-done.4, bf16[3,256,1024]{2,1,0:T(8,128)(2,1)S(1)} %bitcast.6, bf16[2,3,1024]{2,1,0:T(4,128)(2,1)S(1)} %copy-done.3, f32[3,3,1024]{2,1,0:T(4,128)S(1)} %copy-done.1), custom_call_target="tpu_custom_call" | custom-call | flops 5242880 | bytes 2097152 | tf_op jit(solution)/shard_map/pallas_call | solution.py:80
  44.6 10.1 %all-to-all-done.1 = bf16[32,32,256]{2,1,0:T(8,128)(2,1)S(1)} async-done(((bf16[32,32,256]{2,1,0:T(8,128)(2,1)}), bf16[32,32,256]{2,1,0:T(8,128)(2,1)S(1)}, u32[]{:S(2)}, u32[]{:S(2)}) %all-to-all-start.1) | async-done | bytes 524320 | tf_op jit(solution)/shard_map/all_to_all | solution.py:329
  54.7 0.6 shard_map.58
  55.3 1.7 %collective-permute-start.1 = (bf16[128,1024]{1,0:T(8,128)(2,1)S(1)}, bf16[128,1024]{1,0:T(8,128)(2,1)S(1)}, u32[]{:S(2)}, u32[]{:S(2)}) collective-permute-start(bf16[128,1024]{1,0:T(8,128)(2,1)S(1)} %get-tuple-element.7.refs_0_), channel_id=1, source_target_pairs={{0,1},{1,2},{2,3},{3,0},{4,5},{5,6},{6,7},{7,4},{8,9},{9,10},{10,1... | collective-permute-start | bytes 786440 | tf_op jit(solution)/shard_map/ppermute | solution.py:270
  57.0 2.2 %collective-permute-start.3 = (bf16[128,1024]{1,0:T(8,128)(2,1)S(1)}, bf16[128,1024]{1,0:T(8,128)(2,1)S(1)}, u32[]{:S(2)}, u32[]{:S(2)}) collective-permute-start(bf16[128,1024]{1,0:T(8,128)(2,1)S(1)} %get-tuple-element.8.refs_1_), channel_id=1, source_target_pairs={{0,3},{1,0},{2,1},{3,2},{4,7},{5,4},{6,5},{7,6},{8,11},{9,8},{10,9... | collective-permute-start | bytes 786440 | tf_op jit(solution)/shard_map/ppermute | solution.py:270
  59.2 0.0 collective-permute-start.5
  59.2 2.7 %collective-permute-start.6 = (bf16[128,1024]{1,0:T(8,128)(2,1)S(1)}, bf16[128,1024]{1,0:T(8,128)(2,1)S(1)}, u32[]{:S(2)}, u32[]{:S(2)}) collective-permute-start(bf16[128,1024]{1,0:T(8,128)(2,1)S(1)} %get-tuple-element.7.refs_0_), channel_id=1, source_target_pairs={{0,3},{1,0},{2,1},{3,2},{4,7},{5,4},{6,5},{7,6},{8,11},{9,8},{10,9... | collective-permute-start | bytes 786440 | tf_op jit(solution)/shard_map/ppermute | solution.py:270
  61.9 3.5 %collective-permute-done.1.refs_0_ = bf16[128,1024]{1,0:T(8,128)(2,1)S(1)} collective-permute-done((bf16[128,1024]{1,0:T(8,128)(2,1)S(1)}, bf16[128,1024]{1,0:T(8,128)(2,1)S(1)}, u32[]{:S(2)}, u32[]{:S(2)}) %collective-permute-start.1) | collective-permute-done | bytes 262176 | tf_op jit(solution)/shard_map/ppermute | solution.py:270
  65.4 0.0 collective-permute-start.2
  65.4 0.0 collective-permute-done.3.refs_3_
  65.4 2.7 %collective-permute-start.4 = (bf16[128,1024]{1,0:T(8,128)(2,1)S(1)}, bf16[128,1024]{1,0:T(8,128)(2,1)S(1)}, u32[]{:S(2)}, u32[]{:S(2)}) collective-permute-start(bf16[128,1024]{1,0:T(8,128)(2,1)S(1)} %collective-permute-done.3.refs_3_), channel_id=1, source_target_pairs={{0,3},{1,0},{2,1},{3,2},{4,7},{5,4},{6,5},{7,6},{8,11},{9,8},{10,9... | collective-permute-start | bytes 786440 | tf_op jit(solution)/shard_map/ppermute | solution.py:270
  68.1 4.4 %constant_dynamic-slice_fusion = (bf16[1024,1024]{1,0:T(8,128)(2,1)S(1)}, bf16[1024,1024]{1,0:T(8,128)(2,1)S(1)}, bf16[1024,1024]{1,0:T(8,128)(2,1)S(1)}, bf16[1024,1024]{1,0:T(8,128)(2,1)S(1)}) fusion(bf16[4096,1024]{1,0:T(8,128)(2,1)} %param.9, s32[]{:T(128)S(6)} %select_n.38, s32[]{:T(128)S(6)} %select_n.34, s32[]{:T(128)S(6)} %select_n.32, s32[]{:T(128)S(6)} %select_n.36), kind=kLoop, calls=%fused_computation | loop fusion | bytes 16777232 | tf_op jit(solution)/shard_map/dynamic_slice | solution.py:307
  72.6 0.7 shard_map.59.refs_6_
  73.3 0.0 collective-permute-done.5.refs_1_
  73.3 0.0 collective-permute-done.6.refs_2_
  73.3 1.3 %shard_map.60.refs_3_ = f32[256,1024]{1,0:T(8,128)S(1)} custom-call(bf16[128,1024]{1,0:T(8,128)(2,1)S(1)} %collective-permute-done.1.refs_0_, bf16[128,1024]{1,0:T(8,128)(2,1)S(1)} %collective-permute-done.5.refs_1_, bf16[128,1024]{1,0:T(8,128)(2,1)S(1)} %collective-permute-done.6.refs_2_, bf16[128,1024]{1,0:T(8,128)(2,1)S(1)} %collective-permute-done.3.refs_3_, ...), custom_call_target="tpu_custom_call" | custom-call | flops 1073741824 | bytes 4194304 | tf_op jit(solution)/shard_map/pallas_call | solution.py:290
  74.6 2.1 %collective-permute-done.2.refs_0_ = bf16[128,1024]{1,0:T(8,128)(2,1)S(1)} collective-permute-done((bf16[128,1024]{1,0:T(8,128)(2,1)S(1)}, bf16[128,1024]{1,0:T(8,128)(2,1)S(1)}, u32[]{:S(2)}, u32[]{:S(2)}) %collective-permute-start.2) | collective-permute-done | bytes 262176 | tf_op jit(solution)/shard_map/ppermute | solution.py:270
  76.7 0.0 collective-permute-done.4.refs_1_
  76.7 1.5 %shard_map.61 = bf16[256,1024]{1,0:T(8,128)(2,1)} custom-call(bf16[128,1024]{1,0:T(8,128)(2,1)S(1)} %collective-permute-done.2.refs_0_, bf16[128,1024]{1,0:T(8,128)(2,1)S(1)} %collective-permute-done.4.refs_1_, bf16[1024,1024]{1,0:T(8,128)(2,1)S(1)} %get-tuple-element.11.refs_2_, f32[256,1024]{1,0:T(8,128)S(1)} %shard_map.60.refs_3_), custom_call_target="tpu_custom_call" | custom-call | flops 536870912 | bytes 2097152 | tf_op jit(solution)/shard_map/pallas_call | solution.py:290
  (1 shorter events, 0.0 us)
Async XLA Ops:
  0.8 5.4 %collective-permute-start = (bf16[2,3,1024]{2,1,0:T(4,128)(2,1)S(1)}, bf16[2,3,1024]{2,1,0:T(4,128)(2,1)S(1)}, u32[]{:S(2)}, u32[]{:S(2)}) collective-permute-start(bf16[2,3,1024]{2,1,0:T(4,128)(2,1)S(1)} %copy.7), channel_id=1, source_target_pairs={{0,4},{4,8},{8,12},{12,16},{16,20},{20,24},{24,28},{28,32},{32,36}... | collective-permute-start | bytes 36872 | tf_op jit(solution)/shard_map/ppermute | solution.py:323
  6.2 0.6 copy-start.2
  6.8 23.0 %copy-start.4 = (s32[8]{0:T(128)S(1)}, s32[8]{0:T(128)}, u32[]{:S(2)}) copy-start(s32[8]{0:T(128)} %lengths_ref.5) | copy-start | bytes 100
  6.8 23.0 %copy-start.5 = (f32[1,32,2048]{2,1,0:T(8,128)S(1)}, f32[1,32,2048]{2,1,0:T(8,128)}, u32[]{:S(2)}) copy-start(f32[1,32,2048]{2,1,0:T(8,128)} %param.8) | copy-start | bytes 786436
  29.8 13.2 %copy-start = (bf16[256,3,1024]{2,0,1:T(8,128)(2,1)S(1)}, bf16[256,3,1024]{2,0,1:T(8,128)(2,1)}, u32[]{:S(2)}) copy-start(bf16[256,3,1024]{2,0,1:T(8,128)(2,1)} %param.5) | copy-start | bytes 4718596
  29.8 13.2 %copy-start.1 = (f32[3,3,1024]{2,1,0:T(4,128)S(1)}, f32[3,3,1024]{2,1,0:T(4,128)}, u32[]{:S(2)}) copy-start(f32[3,3,1024]{2,1,0:T(4,128)} %taps_ref.3) | copy-start | bytes 110596
  29.8 13.2 %copy-start.3 = (bf16[2,3,1024]{2,1,0:T(4,128)(2,1)S(1)}, bf16[2,3,1024]{2,1,0:T(4,128)(2,1)}, u32[]{:S(2)}) copy-start(bf16[2,3,1024]{2,1,0:T(4,128)(2,1)} %copy-done.2) | copy-start | bytes 36868
  39.0 15.7 %all-to-all-start.1 = ((bf16[32,32,256]{2,1,0:T(8,128)(2,1)}), bf16[32,32,256]{2,1,0:T(8,128)(2,1)S(1)}, u32[]{:S(2)}, u32[]{:S(2)}) async-start(bf16[32,32,256]{2,1,0:T(8,128)(2,1)} %shard_map.57), calls=%async_computation.1 | async-start | bytes 1048576 | tf_op jit(solution)/shard_map/all_to_all | solution.py:329
  55.3 10.1 %collective-permute-start.1 = (bf16[128,1024]{1,0:T(8,128)(2,1)S(1)}, bf16[128,1024]{1,0:T(8,128)(2,1)S(1)}, u32[]{:S(2)}, u32[]{:S(2)}) collective-permute-start(bf16[128,1024]{1,0:T(8,128)(2,1)S(1)} %get-tuple-element.7.refs_0_), channel_id=1, source_target_pairs={{0,1},{1,2},{2,3},{3,0},{4,5},{5,6},{6,7},{7,4},{8,9},{9,10},{10,1... | collective-permute-start | bytes 786440 | tf_op jit(solution)/shard_map/ppermute | solution.py:270
  57.0 8.4 %collective-permute-start.3 = (bf16[128,1024]{1,0:T(8,128)(2,1)S(1)}, bf16[128,1024]{1,0:T(8,128)(2,1)S(1)}, u32[]{:S(2)}, u32[]{:S(2)}) collective-permute-start(bf16[128,1024]{1,0:T(8,128)(2,1)S(1)} %get-tuple-element.8.refs_1_), channel_id=1, source_target_pairs={{0,3},{1,0},{2,1},{3,2},{4,7},{5,4},{6,5},{7,6},{8,11},{9,8},{10,9... | collective-permute-start | bytes 786440 | tf_op jit(solution)/shard_map/ppermute | solution.py:270
  59.2 14.1 %collective-permute-start.5 = (bf16[128,1024]{1,0:T(8,128)(2,1)S(1)}, bf16[128,1024]{1,0:T(8,128)(2,1)S(1)}, u32[]{:S(2)}, u32[]{:S(2)}) collective-permute-start(bf16[128,1024]{1,0:T(8,128)(2,1)S(1)} %get-tuple-element.8.refs_1_), channel_id=1, source_target_pairs={{0,1},{1,2},{2,3},{3,0},{4,5},{5,6},{6,7},{7,4},{8,9},{9,10},{10,1... | collective-permute-start | bytes 786440 | tf_op jit(solution)/shard_map/ppermute | solution.py:270
  59.2 14.1 %collective-permute-start.6 = (bf16[128,1024]{1,0:T(8,128)(2,1)S(1)}, bf16[128,1024]{1,0:T(8,128)(2,1)S(1)}, u32[]{:S(2)}, u32[]{:S(2)}) collective-permute-start(bf16[128,1024]{1,0:T(8,128)(2,1)S(1)} %get-tuple-element.7.refs_0_), channel_id=1, source_target_pairs={{0,3},{1,0},{2,1},{3,2},{4,7},{5,4},{6,5},{7,6},{8,11},{9,8},{10,9... | collective-permute-start | bytes 786440 | tf_op jit(solution)/shard_map/ppermute | solution.py:270
  65.4 11.2 %collective-permute-start.2 = (bf16[128,1024]{1,0:T(8,128)(2,1)S(1)}, bf16[128,1024]{1,0:T(8,128)(2,1)S(1)}, u32[]{:S(2)}, u32[]{:S(2)}) collective-permute-start(bf16[128,1024]{1,0:T(8,128)(2,1)S(1)} %collective-permute-done.1.refs_0_), channel_id=1, source_target_pairs={{0,1},{1,2},{2,3},{3,0},{4,5},{5,6},{6,7},{7,4},{8,9},{9,10},{10,1... | collective-permute-start | bytes 786440 | tf_op jit(solution)/shard_map/ppermute | solution.py:270
  65.4 11.2 %collective-permute-start.4 = (bf16[128,1024]{1,0:T(8,128)(2,1)S(1)}, bf16[128,1024]{1,0:T(8,128)(2,1)S(1)}, u32[]{:S(2)}, u32[]{:S(2)}) collective-permute-start(bf16[128,1024]{1,0:T(8,128)(2,1)S(1)} %collective-permute-done.3.refs_3_), channel_id=1, source_target_pairs={{0,3},{1,0},{2,1},{3,2},{4,7},{5,4},{6,5},{7,6},{8,11},{9,8},{10,9... | collective-permute-start | bytes 786440 | tf_op jit(solution)/shard_map/ppermute | solution.py:270

commit v3 on v2

--- a/solution.py
+++ b/solution.py
@@ -13,6 +13,7 @@
 PAD = 8
 GRANT = 24
 START_GRANT = 60
+EDGES = 8
 MIB = 1 << 20
 
 
@@ -29,8 +30,10 @@
     return total
 
 
-def fill(scr, edge, values):
-    scr[6:8, :] = edge.astype(jnp.float32)
+def fill(scr, values, edge=None):
+    scr[:8, :] = jnp.zeros((8, scr.shape[1]), jnp.float32)
+    if edge is not None:
+        scr[6:8, :] = edge.astype(jnp.float32)
     scr[8:, :] = values.astype(jnp.float32)
 
 
@@ -53,46 +56,64 @@
     return [slice(i, i + TILE) for i in range(0, width, TILE)]
 
 
-def product_kernel(lengths_ref, k_ref, v_ref, edge_ref, taps_ref, out_ref, keeps_ref, scr_k, scr_v):
+def product_kernel(lengths_ref, k_ref, v_ref, taps_ref, out_ref, keeps_ref, scr_k, scr_v):
     fill_keeps(lengths_ref, keeps_ref)
-    fill(scr_k, edge_ref[:, 1, :], k_ref[...])
-    fill(scr_v, edge_ref[:, 2, :], v_ref[...])
-    for lanes in lane_parts(k_ref.shape[1]):
+    fill(scr_k, k_ref[...])
+    fill(scr_v, v_ref[...])
+    held = out_ref.shape[1] - EDGES
+    tok_rows, width = k_ref.shape
+    for lanes in lane_parts(width):
         product = short_filter(scr_k, taps_ref, 1, keeps_ref, lanes) * short_filter(
             scr_v, taps_ref, 2, keeps_ref, lanes
         )
-        out_ref[lanes, :] = product.T.astype(jnp.bfloat16)
+        product = product.T
+        outer = [scr[8 + t : 10 + t, lanes] for scr in (scr_k, scr_v) for t in (0, tok_rows - 2)]
+        outer = jnp.concatenate(outer, 0)
+        for i in range(TILE // held):
+            mine = outer if i == 0 else pltpu.roll(outer, TILE - i * held, 1)
+            mine = jnp.concatenate([mine, jnp.zeros((EDGES, tok_rows - TILE), jnp.float32)], 1)
+            rows = jnp.concatenate([product[i * held : (i + 1) * held], mine], 0)
+            out_ref[lanes.start // held + i] = rows.astype(jnp.bfloat16)
 
 
 def query_kernel(lengths_ref, q_ref, edge_ref, taps_ref, out_ref, keeps_ref, scr_q):
     fill_keeps(lengths_ref, keeps_ref)
-    fill(scr_q, edge_ref[:, 0, :], q_ref[...])
+    fill(scr_q, q_ref[...], edge_ref[...])
     for lanes in lane_parts(q_ref.shape[1]):
         out_ref[:, lanes] = short_filter(scr_q, taps_ref, 0, keeps_ref, lanes).astype(jnp.bfloat16)
 
 
-def short_call(kernel, lengths, by_kind, edge, taps, kinds, transposed, grant, width=512):
+def short_call(kernel, lengths, by_kind, edge, taps, kinds, shape, block, grant, width=512):
     _, tok_rows, channels = by_kind.shape
-    if transposed:
-        shape, spec = (channels, tok_rows), pl.BlockSpec((width, tok_rows), lambda i: (i, 0))
-    else:
-        shape, spec = (tok_rows, channels), pl.BlockSpec((tok_rows, width), lambda i: (0, i))
+    steps = channels // width
     return pl.pallas_call(
         kernel,
-        grid=(channels // width,),
+        grid=(steps,),
         out_shape=jax.ShapeDtypeStruct(shape, jnp.bfloat16),
         in_specs=[pl.BlockSpec(memory_space=pltpu.SMEM)]
         + [pl.BlockSpec((None, tok_rows, width), lambda i, kind=kind: (kind, 0, i)) for kind in kinds]
-        + [
-            pl.BlockSpec((TAPS - 1, 3, width), lambda i: (0, 0, i)),
-            pl.BlockSpec((TAPS, 3, width), lambda i: (0, 0, i)),
-        ],
-        out_specs=spec,
+        + [pl.BlockSpec((TAPS - 1, width), lambda i: (0, i))] * (edge is not None)
+        + [pl.BlockSpec((TAPS, 3, width), lambda i: (0, 0, i))],
+        out_specs=block,
         scratch_shapes=[pltpu.VMEM((TAPS - 1, tok_rows, TILE), jnp.float32)]
         + [pltpu.VMEM((tok_rows + 8, width), jnp.float32)] * len(kinds),
         compiler_params=params(grant),
         cost_estimate=pl.CostEstimate(flops=20 * tok_rows * channels, bytes_accessed=2 * MIB, transcendentals=0),
-    )(lengths, *([by_kind] * len(kinds)), edge, taps)
+    )(lengths, *([by_kind] * len(kinds)), *([] if edge is None else [edge]), taps)
+
+
+def products(lengths, by_kind, taps, devices, width=512):
+    _, tok_rows, channels = by_kind.shape
+    held = channels // devices
+    shape = (devices, held + EDGES, tok_rows)
+    block = pl.BlockSpec((width // held,) + shape[1:], lambda i: (i, 0, 0))
+    return short_call(product_kernel, lengths, by_kind, None, taps, (1, 2), shape, block, START_GRANT, width)
+
+
+def queries(lengths, by_kind, edge, taps, width=512):
+    _, tok_rows, channels = by_kind.shape
+    block = pl.BlockSpec((tok_rows, width), lambda i: (0, i))
+    return short_call(query_kernel, lengths, by_kind, edge, taps, (0,), (tok_rows, channels), block, GRANT, width)
 
 
 def list_rows(lengths_ref, table, heads, rows):
@@ -143,9 +164,40 @@
     return jnp.where(inside[None], values.reshape(shape), others).reshape(values.shape)
 
 
-def conv_kernel(lengths_ref, signal_ref, taps_ref, out_ref, table, heads, spread, result, before, toep, *, rows, rows_b):
+def first_products(lengths_ref, edges, short_ref, channels):
+    count = edges.shape[0]
+    place = lax.axis_index("seq") * channels
+    here = pl.ds(pl.multiple_of(place // TILE * TILE, TILE), TILE)
+    rows = [short_ref[tap, which : which + 1, here] for which in (1, 2) for tap in range(TAPS)]
+    rows = jnp.concatenate(rows + [jnp.zeros((2, TILE), jnp.float32)], 0)
+    rows = pltpu.roll(rows, TILE - place % TILE, 1)
+    columns = jnp.concatenate([rows, jnp.zeros((TILE - 8, TILE), jnp.float32)], 0).T[:channels]
+    own = edges.T[:channels]
+    lane = lax.broadcasted_iota(jnp.int32, (channels, count), 1)
+    positions = lane // EDGES * BLK + lane % EDGES
+    starts = jnp.zeros((channels, count), jnp.int32)
+    offset = jnp.int32(0)
+    for prompt in range(lengths_ref.shape[0]):
+        starts = jnp.where(positions >= offset, offset, starts)
+        offset = offset + lengths_ref[prompt]
+    product = None
+    for i in range(2):
+        now = own if i == 0 else pltpu.roll(own, count - 4, 1)
+        one = jnp.where(lane % EDGES == 0, pltpu.roll(now, 5, 1), pltpu.roll(now, 1, 1))
+        two = pltpu.roll(now, 6, 1)
+        total = columns[:, 3 * i : 3 * i + 1] * now
+        for tap, value in ((1, one), (2, two)):
+            keep = (positions - tap >= starts).astype(jnp.float32)
+            total = total + columns[:, 3 * i + tap : 3 * i + tap + 1] * (value * keep)
+        product = total if product is None else product * total
+    return product.astype(jnp.bfloat16).astype(jnp.float32)
+
+
+def conv_kernel(
+    lengths_ref, signal_ref, taps_ref, short_ref, out_ref, table, heads, blocks, edges, spread, result, before, toep, *, rows, rows_b
+):
     step = pl.program_id(0)
-    devices, channels, _ = signal_ref.shape
+    devices, channels, _ = out_ref.shape
     group, span = taps_ref.shape
     lags = span // BLK + 1
     tiles = span // TILE + 1
@@ -154,8 +206,19 @@
     @pl.when(step == 0)
     def _():
         list_rows(lengths_ref, table, heads, rows)
+        for device in range(devices):
+            arrived = signal_ref[device].astype(jnp.float32)
+            blocks[device] = arrived[:channels]
+            edges[device * EDGES : (device + 1) * EDGES, :] = arrived[channels:, :TILE]
+        firsts = first_products(lengths_ref, edges[...], short_ref, channels)
+        is_first = lax.broadcasted_iota(jnp.int32, (channels, TILE), 1) < TAPS - 1
+        for device in range(devices):
+            at = device * EDGES
+            mine = firsts[:, at // TILE * TILE : (at // TILE + 1) * TILE]
+            mine = mine if at % TILE == 0 else pltpu.roll(mine, TILE - at % TILE, 1)
+            blocks[device, :, :TILE] = jnp.where(is_first, mine, blocks[device, :, :TILE])
         for row in range(rows):
-            slab = only_lanes(table, row, signal_ref[table[0, row]].astype(jnp.float32), 0.0)
+            slab = only_lanes(table, row, blocks[table[0, row]], 0.0)
             for h in range(2):
                 spread[h, pl.ds(PAD + row, channels, stride=pitch), :] = slab[:, h * TILE : (h + 1) * TILE]
         before[...] = rows_before(lengths_ref, rows_b)
@@ -210,24 +273,29 @@
             out_ref[block] = only_lanes(table, row, slab_of(row), old).astype(jnp.bfloat16)
 
 
-def long_conv(lengths, signal, taps, group=32):
-    devices, channels, _ = signal.shape
+def long_conv(lengths, signal, taps, short_taps, group=32):
+    devices, _, tok_rows = signal.shape
+    channels = taps.shape[0]
+    shape = (devices, channels, tok_rows)
     span = taps.shape[1]
     rows = -(-(devices + lengths.shape[0] - 1) // 8) * 8
     rows_b = -(-rows // 16) * 16
     return pl.pallas_call(
         functools.partial(conv_kernel, rows=rows, rows_b=rows_b),
         grid=(channels // group,),
-        out_shape=jax.ShapeDtypeStruct(signal.shape, jnp.bfloat16),
+        out_shape=jax.ShapeDtypeStruct(shape, jnp.bfloat16),
         in_specs=[
             pl.BlockSpec(memory_space=pltpu.SMEM),
             pl.BlockSpec(signal.shape, lambda i: (0, 0, 0)),
             pl.BlockSpec((group, span), lambda i: (i, 0)),
+            pl.BlockSpec(short_taps.shape, lambda i: (0, 0, 0)),
         ],
-        out_specs=pl.BlockSpec(signal.shape, lambda i: (0, 0, 0)),
+        out_specs=pl.BlockSpec(shape, lambda i: (0, 0, 0)),
         scratch_shapes=[
             pltpu.SMEM((3, rows), jnp.int32),
             pltpu.SMEM((2, devices), jnp.int32),
+            pltpu.VMEM(shape, jnp.float32),
+            pltpu.VMEM((devices * EDGES, TILE), jnp.float32),
             pltpu.VMEM((2, channels * (PAD + rows_b), TILE), jnp.float32),
             pltpu.VMEM((2, channels * rows, TILE), jnp.float32),
             pltpu.VMEM((rows_b, TILE), jnp.int32),
@@ -237,7 +305,7 @@
         cost_estimate=pl.CostEstimate(
             flops=2 * channels * rows * (span + BLK) * BLK, bytes_accessed=2 * MIB, transcendentals=0
         ),
-    )(lengths, signal, taps)
+    )(lengths, signal, taps, short_taps)
 
 
 def gate_kernel(query_ref, conv_ref, *out_refs):
@@ -320,12 +388,13 @@
     tok_rows, _, width = qkv.shape
     lead = TAPS - 1
     seq = lax.axis_size("seq")
-    edge = lax.ppermute(qkv[tok_rows - lead :], "seq", [(i, i + 1) for i in range(seq - 1)])
     by_kind = qkv.transpose(1, 0, 2)
-    product_t = short_call(product_kernel, lengths, by_kind, edge, short_taps, (1, 2), True, START_GRANT)
-    query = short_call(query_kernel, lengths, by_kind, edge, short_taps, (0,), False, GRANT)
-    signal = lax.all_to_all(product_t.reshape(seq, width // seq, tok_rows), "seq", 0, 0, tiled=True)
-    conv = long_conv(lengths, signal, filter_taps[0])
+    sent = products(lengths, by_kind, short_taps, seq)
+    signal = lax.all_to_all(sent, "seq", 0, 0, tiled=True)
+    conv = long_conv(lengths, signal, filter_taps[0], short_taps)
+    late, conv = lax.optimization_barrier((by_kind, conv))
+    edge = lax.ppermute(late[0, tok_rows - lead :], "seq", [(i, i + 1) for i in range(seq - 1)])
+    query = queries(lengths, late, edge, short_taps)
     conv_t = lax.all_to_all(conv, "seq", 0, 0, tiled=True).reshape(width, tok_rows)
     return project(gate(query, conv_t), w_out)
 

time: 78.6 us -> 74.6 us (0.949)
  waiting for transfers between devices: 16.6 us -> 12.2 us
  blocking collectives: 19.8 us -> 21.5 us
  local copies, waits for them, and re-layouts: 5.88 us -> 4.47 us
  Pallas kernels: 18 us -> 19.1 us
  starting transfers between devices: 17.8 us -> 16.9 us
    all_to_all x1, waiting for transfers between devices: 10.1 us -> 4.12 us  [per_device(): lax.all_to_all(conv, 'seq', 0, 0, tiled=True).reshape(width, tok_rows)]
    all_to_all x1, blocking collectives: 19.8 us -> 21.5 us  [per_device(): signal = lax.all_to_all(sent, 'seq', 0, 0, tiled=True)]
    ppermute x1, waiting for transfers between devices: 0.85 us -> 2.42 us  [per_device(): lax.ppermute(late[0, tok_rows - lead:], 'seq', [(i, i + 1) for i in range...]
    pallas_call x1, Pallas kernels: 9.18 us -> 10.2 us  [long_conv(): pl.pallas_call(functools.partial(conv_kernel, rows=rows, rows_b=rows_b),...]
    ppermute x1, starting transfers between devices: 4.51 us -> 3.55 us  [per_device(): lax.ppermute(late[0, tok_rows - lead:], 'seq', [(i, i + 1) for i in range...]
    slice x1 -> x0, local copies, waits for them, and re-layouts: 0.81 us -> none  [per_device(): qkv[tok_rows - lead:]]
where the time goes in v3:
time: 74.6 us; the launch traced here: 74.2 us
  blocking collectives  21.5 us (29%)
  Pallas kernels  19.1 us (26%)
  starting transfers between devices  16.9 us (23%)
  waiting for transfers between devices  12.2 us (16%)
  local copies, waits for them, and re-layouts  4.47 us (6%)
    all_to_all x1, blocking collectives, per_device(): signal = lax.all_to_all(sent, 'seq', 0, 0, tiled=True)  21.5 us
    pallas_call x1, Pallas kernels, long_conv(): pl.pallas_call(functools.partial(conv_kernel, rows=rows, rows_b=rows_b),...  10.2 us
    ppermute x6, starting transfers between devices, shift(): lax.ppermute(array, axis, [(i, (i + by) % length) for i in range(length)])  9.26 us
    ppermute x6, waiting for transfers between devices, shift(): lax.ppermute(array, axis, [(i, (i + by) % length) for i in range(length)])  5.63 us
    pallas_call x2, Pallas kernels, short_call(): pl.pallas_call(kernel, grid=(steps,), out_shape=jax.ShapeDtypeStruct(shap...  4.81 us
    dynamic_slice x1, local copies, waits for them, and re-layouts, project(): lax.dynamic_slice_in_dim(w_out, (place + i) % size * depth, depth, 0)  4.45 us
    all_to_all x1, waiting for transfers between devices, per_device(): lax.all_to_all(conv, 'seq', 0, 0, tiled=True).reshape(width, tok_rows)  4.12 us
    all_to_all x1, starting transfers between devices, per_device(): lax.all_to_all(conv, 'seq', 0, 0, tiled=True).reshape(width, tok_rows)  4.09 us
  transfers between devices with their start and end apart: 8, of which 4 were waited for; matrix products, arithmetic and copies ran while one was open for 6% of the time, Pallas kernels for 5%

profile of v3, /device:TPU:1, one launch (start us, length us, event | category | flops | bytes accessed | tf_op | source)
XLA Modules:
  0.0 74.2 jit_solution(16621258713965531261)
XLA Ops:
  0.0 0.0 copy-start.1
  0.0 0.0 copy-start.2
  0.0 0.0 copy-start.3
  0.0 3.3 %shard_map.55 = bf16[32,40,256]{2,1,0:T(8,128)(2,1)} custom-call(s32[8]{0:T(128)} %lengths_ref.5, bf16[3,256,1024]{2,1,0:T(8,128)(2,1)} %bitcast.5, bf16[3,256,1024]{2,1,0:T(8,128)(2,1)} %bitcast.6, f32[3,3,1024]{2,1,0:T(4,128)} %taps_ref.3), custom_call_target="tpu_custom_call" | custom-call | flops 5242880 | bytes 2097152 | tf_op jit(solution)/shard_map/pallas_call | solution.py:89
  3.3 21.5 %all_to_all.10.signal_ref = bf16[32,40,256]{2,1,0:T(8,128)(2,1)S(1)} all-to-all(bf16[32,40,256]{2,1,0:T(8,128)(2,1)} %shard_map.55), channel_id=1, replica_groups=mesh['seq'=32,'ch'=4] {'seq'}, dimensions={0} | all-to-all | bytes 1310720 | tf_op jit(solution)/shard_map/all_to_all | solution.py:393
  24.8 0.0 copy-done.1
  24.8 0.0 copy-done.2
  24.8 0.0 copy-done.3
  24.8 0.0 copy-start
  24.8 10.2 %shard_map.56 = bf16[32,32,256]{2,1,0:T(8,128)(2,1)} custom-call(s32[8]{0:T(128)S(1)} %copy-done.2, bf16[32,40,256]{2,1,0:T(8,128)(2,1)S(1)} %all_to_all.10.signal_ref, f32[32,2048]{1,0:T(8,128)S(1)} %bitcast.10, f32[3,3,1024]{2,1,0:T(4,128)S(1)} %copy-done.1), custom_call_target="tpu_custom_call" | custom-call | flops 1509949440 | bytes 2097152 | tf_op jit(solution)/shard_map/pallas_call | solution.py:283
  35.0 4.1 %all-to-all-start.1 = ((bf16[32,32,256]{2,1,0:T(8,128)(2,1)}), bf16[32,32,256]{2,1,0:T(8,128)(2,1)S(1)}, u32[]{:S(2)}, u32[]{:S(2)}) async-start(bf16[32,32,256]{2,1,0:T(8,128)(2,1)} %shard_map.56), calls=%async_computation.1 | async-start | bytes 1048576 | tf_op jit(solution)/shard_map/all_to_all | solution.py:398
  39.1 0.0 copy-done
  39.1 3.5 %collective-permute-start = (bf16[2,1024]{1,0:T(2,128)(2,1)S(1)}, bf16[2,1024]{1,0:T(2,128)(2,1)S(1)}, u32[]{:S(2)}, u32[]{:S(2)}) collective-permute-start(bf16[2,1024]{1,0:T(2,128)(2,1)S(1)} %slice_bitcast_fusion), channel_id=1, source_target_pairs={{0,4},{4,8},{8,12},{12,16},{16,20},{20,24},{24,28},{28,32},{32,36}... | collective-permute-start | bytes 12296 | tf_op jit(solution)/shard_map/ppermute | solution.py:396
  42.6 2.4 %collective-permute-done.edge_ref = bf16[2,1024]{1,0:T(2,128)(2,1)S(1)} collective-permute-done((bf16[2,1024]{1,0:T(2,128)(2,1)S(1)}, bf16[2,1024]{1,0:T(2,128)(2,1)S(1)}, u32[]{:S(2)}, u32[]{:S(2)}) %collective-permute-start) | collective-permute-done | bytes 4128 | tf_op jit(solution)/shard_map/ppermute | solution.py:396
  45.0 1.5 %shard_map.57.query_ref = bf16[256,1024]{1,0:T(8,128)(2,1)S(1)} custom-call(s32[8]{0:T(128)S(1)} %copy-done.2, bf16[3,256,1024]{2,1,0:T(8,128)(2,1)S(1)} %bitcast.8, bf16[2,1024]{1,0:T(2,128)(2,1)S(1)} %collective-permute-done.edge_ref, f32[3,3,1024]{2,1,0:T(4,128)S(1)} %copy-done.1), custom_call_target="tpu_custom_call" | custom-call | flops 5242880 | bytes 2097152 | tf_op jit(solution)/shard_map/pallas_call | solution.py:89
  46.6 4.1 %all-to-all-done.1 = bf16[32,32,256]{2,1,0:T(8,128)(2,1)S(1)} async-done(((bf16[32,32,256]{2,1,0:T(8,128)(2,1)}), bf16[32,32,256]{2,1,0:T(8,128)(2,1)S(1)}, u32[]{:S(2)}, u32[]{:S(2)}) %all-to-all-start.1) | async-done | bytes 524320 | tf_op jit(solution)/shard_map/all_to_all | solution.py:398
  50.7 0.6 shard_map.58
  51.3 1.7 %collective-permute-start.1 = (bf16[128,1024]{1,0:T(8,128)(2,1)S(1)}, bf16[128,1024]{1,0:T(8,128)(2,1)S(1)}, u32[]{:S(2)}, u32[]{:S(2)}) collective-permute-start(bf16[128,1024]{1,0:T(8,128)(2,1)S(1)} %get-tuple-element.11.refs_0_), channel_id=1, source_target_pairs={{0,1},{1,2},{2,3},{3,0},{4,5},{5,6},{6,7},{7,4},{8,9},{9,10},{10,1... | collective-permute-start | bytes 786440 | tf_op jit(solution)/shard_map/ppermute | solution.py:338
  53.1 2.2 %collective-permute-start.3 = (bf16[128,1024]{1,0:T(8,128)(2,1)S(1)}, bf16[128,1024]{1,0:T(8,128)(2,1)S(1)}, u32[]{:S(2)}, u32[]{:S(2)}) collective-permute-start(bf16[128,1024]{1,0:T(8,128)(2,1)S(1)} %get-tuple-element.12.refs_1_), channel_id=1, source_target_pairs={{0,3},{1,0},{2,1},{3,2},{4,7},{5,4},{6,5},{7,6},{8,11},{9,8},{10,9... | collective-permute-start | bytes 786440 | tf_op jit(solution)/shard_map/ppermute | solution.py:338
  55.3 0.0 collective-permute-start.5
  55.3 2.7 %collective-permute-start.6 = (bf16[128,1024]{1,0:T(8,128)(2,1)S(1)}, bf16[128,1024]{1,0:T(8,128)(2,1)S(1)}, u32[]{:S(2)}, u32[]{:S(2)}) collective-permute-start(bf16[128,1024]{1,0:T(8,128)(2,1)S(1)} %get-tuple-element.11.refs_0_), channel_id=1, source_target_pairs={{0,3},{1,0},{2,1},{3,2},{4,7},{5,4},{6,5},{7,6},{8,11},{9,8},{10,9... | collective-permute-start | bytes 786440 | tf_op jit(solution)/shard_map/ppermute | solution.py:338
  57.9 3.5 %collective-permute-done.1.refs_0_ = bf16[128,1024]{1,0:T(8,128)(2,1)S(1)} collective-permute-done((bf16[128,1024]{1,0:T(8,128)(2,1)S(1)}, bf16[128,1024]{1,0:T(8,128)(2,1)S(1)}, u32[]{:S(2)}, u32[]{:S(2)}) %collective-permute-start.1) | collective-permute-done | bytes 262176 | tf_op jit(solution)/shard_map/ppermute | solution.py:338
  61.5 0.0 collective-permute-start.2
  61.5 0.0 collective-permute-done.3.refs_3_
  61.5 2.7 %collective-permute-start.4 = (bf16[128,1024]{1,0:T(8,128)(2,1)S(1)}, bf16[128,1024]{1,0:T(8,128)(2,1)S(1)}, u32[]{:S(2)}, u32[]{:S(2)}) collective-permute-start(bf16[128,1024]{1,0:T(8,128)(2,1)S(1)} %collective-permute-done.3.refs_3_), channel_id=1, source_target_pairs={{0,3},{1,0},{2,1},{3,2},{4,7},{5,4},{6,5},{7,6},{8,11},{9,8},{10,9... | collective-permute-start | bytes 786440 | tf_op jit(solution)/shard_map/ppermute | solution.py:338
  64.1 4.4 %constant_dynamic-slice_fusion = (bf16[1024,1024]{1,0:T(8,128)(2,1)S(1)}, bf16[1024,1024]{1,0:T(8,128)(2,1)S(1)}, bf16[1024,1024]{1,0:T(8,128)(2,1)S(1)}, bf16[1024,1024]{1,0:T(8,128)(2,1)S(1)}) fusion(bf16[4096,1024]{1,0:T(8,128)(2,1)} %param.9, s32[]{:T(128)S(6)} %select_n.38, s32[]{:T(128)S(6)} %select_n.34, s32[]{:T(128)S(6)} %select_n.32, s32[]{:T(128)S(6)} %select_n.36), kind=kLoop, calls=%fused_computation.1 | loop fusion | bytes 16777232 | tf_op jit(solution)/shard_map/dynamic_slice | solution.py:375
  68.6 0.7 shard_map.59.refs_6_
  69.3 0.0 collective-permute-done.5.refs_1_
  69.3 0.0 collective-permute-done.6.refs_2_
  69.3 1.3 %shard_map.60.refs_3_ = f32[256,1024]{1,0:T(8,128)S(1)} custom-call(bf16[128,1024]{1,0:T(8,128)(2,1)S(1)} %collective-permute-done.1.refs_0_, bf16[128,1024]{1,0:T(8,128)(2,1)S(1)} %collective-permute-done.5.refs_1_, bf16[128,1024]{1,0:T(8,128)(2,1)S(1)} %collective-permute-done.6.refs_2_, bf16[128,1024]{1,0:T(8,128)(2,1)S(1)} %collective-permute-done.3.refs_3_, ...), custom_call_target="tpu_custom_call" | custom-call | flops 1073741824 | bytes 4194304 | tf_op jit(solution)/shard_map/pallas_call | solution.py:358
  70.6 2.1 %collective-permute-done.2.refs_0_ = bf16[128,1024]{1,0:T(8,128)(2,1)S(1)} collective-permute-done((bf16[128,1024]{1,0:T(8,128)(2,1)S(1)}, bf16[128,1024]{1,0:T(8,128)(2,1)S(1)}, u32[]{:S(2)}, u32[]{:S(2)}) %collective-permute-start.2) | collective-permute-done | bytes 262176 | tf_op jit(solution)/shard_map/ppermute | solution.py:338
  72.7 0.0 collective-permute-done.4.refs_1_
  72.7 1.5 %shard_map.61 = bf16[256,1024]{1,0:T(8,128)(2,1)} custom-call(bf16[128,1024]{1,0:T(8,128)(2,1)S(1)} %collective-permute-done.2.refs_0_, bf16[128,1024]{1,0:T(8,128)(2,1)S(1)} %collective-permute-done.4.refs_1_, bf16[1024,1024]{1,0:T(8,128)(2,1)S(1)} %get-tuple-element.15.refs_2_, f32[256,1024]{1,0:T(8,128)S(1)} %shard_map.60.refs_3_), custom_call_target="tpu_custom_call" | custom-call | flops 536870912 | bytes 2097152 | tf_op jit(solution)/shard_map/pallas_call | solution.py:358
  (1 shorter events, 0.0 us)
Async XLA Ops:
  0.0 24.8 %copy-start.1 = (f32[3,3,1024]{2,1,0:T(4,128)S(1)}, f32[3,3,1024]{2,1,0:T(4,128)}, u32[]{:S(2)}) copy-start(f32[3,3,1024]{2,1,0:T(4,128)} %taps_ref.3) | copy-start | bytes 110596
  0.0 24.8 %copy-start.2 = (s32[8]{0:T(128)S(1)}, s32[8]{0:T(128)}, u32[]{:S(2)}) copy-start(s32[8]{0:T(128)} %lengths_ref.5) | copy-start | bytes 100
  0.0 24.8 %copy-start.3 = (f32[1,32,2048]{2,1,0:T(8,128)S(1)}, f32[1,32,2048]{2,1,0:T(8,128)}, u32[]{:S(2)}) copy-start(f32[1,32,2048]{2,1,0:T(8,128)} %param.8) | copy-start | bytes 786436
  24.8 14.3 %copy-start = (bf16[256,3,1024]{2,0,1:T(8,128)(2,1)S(1)}, bf16[256,3,1024]{2,0,1:T(8,128)(2,1)}, u32[]{:S(2)}) copy-start(bf16[256,3,1024]{2,0,1:T(8,128)(2,1)} %param.5) | copy-start | bytes 4718596
  35.0 15.8 %all-to-all-start.1 = ((bf16[32,32,256]{2,1,0:T(8,128)(2,1)}), bf16[32,32,256]{2,1,0:T(8,128)(2,1)S(1)}, u32[]{:S(2)}, u32[]{:S(2)}) async-start(bf16[32,32,256]{2,1,0:T(8,128)(2,1)} %shard_map.56), calls=%async_computation.1 | async-start | bytes 1048576 | tf_op jit(solution)/shard_map/all_to_all | solution.py:398
  39.1 6.0 %collective-permute-start = (bf16[2,1024]{1,0:T(2,128)(2,1)S(1)}, bf16[2,1024]{1,0:T(2,128)(2,1)S(1)}, u32[]{:S(2)}, u32[]{:S(2)}) collective-permute-start(bf16[2,1024]{1,0:T(2,128)(2,1)S(1)} %slice_bitcast_fusion), channel_id=1, source_target_pairs={{0,4},{4,8},{8,12},{12,16},{16,20},{20,24},{24,28},{28,32},{32,36}... | collective-permute-start | bytes 12296 | tf_op jit(solution)/shard_map/ppermute | solution.py:396
  51.3 10.1 %collective-permute-start.1 = (bf16[128,1024]{1,0:T(8,128)(2,1)S(1)}, bf16[128,1024]{1,0:T(8,128)(2,1)S(1)}, u32[]{:S(2)}, u32[]{:S(2)}) collective-permute-start(bf16[128,1024]{1,0:T(8,128)(2,1)S(1)} %get-tuple-element.11.refs_0_), channel_id=1, source_target_pairs={{0,1},{1,2},{2,3},{3,0},{4,5},{5,6},{6,7},{7,4},{8,9},{9,10},{10,1... | collective-permute-start | bytes 786440 | tf_op jit(solution)/shard_map/ppermute | solution.py:338
  53.1 8.4 %collective-permute-start.3 = (bf16[128,1024]{1,0:T(8,128)(2,1)S(1)}, bf16[128,1024]{1,0:T(8,128)(2,1)S(1)}, u32[]{:S(2)}, u32[]{:S(2)}) collective-permute-start(bf16[128,1024]{1,0:T(8,128)(2,1)S(1)} %get-tuple-element.12.refs_1_), channel_id=1, source_target_pairs={{0,3},{1,0},{2,1},{3,2},{4,7},{5,4},{6,5},{7,6},{8,11},{9,8},{10,9... | collective-permute-start | bytes 786440 | tf_op jit(solution)/shard_map/ppermute | solution.py:338
  55.3 14.1 %collective-permute-start.5 = (bf16[128,1024]{1,0:T(8,128)(2,1)S(1)}, bf16[128,1024]{1,0:T(8,128)(2,1)S(1)}, u32[]{:S(2)}, u32[]{:S(2)}) collective-permute-start(bf16[128,1024]{1,0:T(8,128)(2,1)S(1)} %get-tuple-element.12.refs_1_), channel_id=1, source_target_pairs={{0,1},{1,2},{2,3},{3,0},{4,5},{5,6},{6,7},{7,4},{8,9},{9,10},{10,1... | collective-permute-start | bytes 786440 | tf_op jit(solution)/shard_map/ppermute | solution.py:338
  55.3 14.1 %collective-permute-start.6 = (bf16[128,1024]{1,0:T(8,128)(2,1)S(1)}, bf16[128,1024]{1,0:T(8,128)(2,1)S(1)}, u32[]{:S(2)}, u32[]{:S(2)}) collective-permute-start(bf16[128,1024]{1,0:T(8,128)(2,1)S(1)} %get-tuple-element.11.refs_0_), channel_id=1, source_target_pairs={{0,3},{1,0},{2,1},{3,2},{4,7},{5,4},{6,5},{7,6},{8,11},{9,8},{10,9... | collective-permute-start | bytes 786440 | tf_op jit(solution)/shard_map/ppermute | solution.py:338
  61.5 11.2 %collective-permute-start.2 = (bf16[128,1024]{1,0:T(8,128)(2,1)S(1)}, bf16[128,1024]{1,0:T(8,128)(2,1)S(1)}, u32[]{:S(2)}, u32[]{:S(2)}) collective-permute-start(bf16[128,1024]{1,0:T(8,128)(2,1)S(1)} %collective-permute-done.1.refs_0_), channel_id=1, source_target_pairs={{0,1},{1,2},{2,3},{3,0},{4,5},{5,6},{6,7},{7,4},{8,9},{9,10},{10,1... | collective-permute-start | bytes 786440 | tf_op jit(solution)/shard_map/ppermute | solution.py:338
  61.5 11.2 %collective-permute-start.4 = (bf16[128,1024]{1,0:T(8,128)(2,1)S(1)}, bf16[128,1024]{1,0:T(8,128)(2,1)S(1)}, u32[]{:S(2)}, u32[]{:S(2)}) collective-permute-start(bf16[128,1024]{1,0:T(8,128)(2,1)S(1)} %collective-permute-done.3.refs_3_), channel_id=1, source_target_pairs={{0,3},{1,0},{2,1},{3,2},{4,7},{5,4},{6,5},{7,6},{8,11},{9,8},{10,9... | collective-permute-start | bytes 786440 | tf_op jit(solution)/shard_map/ppermute | solution.py:338

commit v4 on v3

--- a/solution.py
+++ b/solution.py
@@ -60,19 +60,19 @@
     fill_keeps(lengths_ref, keeps_ref)
     fill(scr_k, k_ref[...])
     fill(scr_v, v_ref[...])
-    held = out_ref.shape[1] - EDGES
     tok_rows, width = k_ref.shape
+    held = (out_ref.shape[1] - EDGES) * TILE // tok_rows
     for lanes in lane_parts(width):
         product = short_filter(scr_k, taps_ref, 1, keeps_ref, lanes) * short_filter(
             scr_v, taps_ref, 2, keeps_ref, lanes
         )
         product = product.T
+        halves = [product[:, at : at + TILE] for at in range(0, tok_rows, TILE)]
         outer = [scr[8 + t : 10 + t, lanes] for scr in (scr_k, scr_v) for t in (0, tok_rows - 2)]
         outer = jnp.concatenate(outer, 0)
         for i in range(TILE // held):
             mine = outer if i == 0 else pltpu.roll(outer, TILE - i * held, 1)
-            mine = jnp.concatenate([mine, jnp.zeros((EDGES, tok_rows - TILE), jnp.float32)], 1)
-            rows = jnp.concatenate([product[i * held : (i + 1) * held], mine], 0)
+            rows = jnp.concatenate([half[i * held : (i + 1) * held] for half in halves] + [mine], 0)
             out_ref[lanes.start // held + i] = rows.astype(jnp.bfloat16)
 
 
@@ -105,7 +105,7 @@
 def products(lengths, by_kind, taps, devices, width=512):
     _, tok_rows, channels = by_kind.shape
     held = channels // devices
-    shape = (devices, held + EDGES, tok_rows)
+    shape = (devices, held * tok_rows // TILE + EDGES, TILE)
     block = pl.BlockSpec((width // held,) + shape[1:], lambda i: (i, 0, 0))
     return short_call(product_kernel, lengths, by_kind, None, taps, (1, 2), shape, block, START_GRANT, width)
 
@@ -208,8 +208,9 @@
         list_rows(lengths_ref, table, heads, rows)
         for device in range(devices):
             arrived = signal_ref[device].astype(jnp.float32)
-            blocks[device] = arrived[:channels]
-            edges[device * EDGES : (device + 1) * EDGES, :] = arrived[channels:, :TILE]
+            for h in range(2):
+                blocks[device, :, h * TILE : (h + 1) * TILE] = arrived[h * channels : (h + 1) * channels]
+            edges[device * EDGES : (device + 1) * EDGES, :] = arrived[2 * channels :]
         firsts = first_products(lengths_ref, edges[...], short_ref, channels)
         is_first = lax.broadcasted_iota(jnp.int32, (channels, TILE), 1) < TAPS - 1
         for device in range(devices):
@@ -274,7 +275,7 @@
 
 
 def long_conv(lengths, signal, taps, short_taps, group=32):
-    devices, _, tok_rows = signal.shape
+    devices, tok_rows = signal.shape[0], BLK
     channels = taps.shape[0]
     shape = (devices, channels, tok_rows)
     span = taps.shape[1]
@@ -316,8 +317,9 @@
         out_ref[...] = gated[i * rows : (i + 1) * rows]
 
 
-def gate(query, conv_t, pieces=2, width=256):
+def gate(query, conv_t, pieces=2, width=1024):
     tok_rows, channels = query.shape
+    width = min(width, channels)
     rows = tok_rows // pieces
     return pl.pallas_call(
         gate_kernel,

time: 74.6 us -> 73.4 us (0.984)
  no operation moved by 1% of the time
where the time goes in v4:
time: 73.4 us; the launch traced here: 73.1 us
  blocking collectives  20.8 us (28%)
  Pallas kernels  18.6 us (25%)
  starting transfers between devices  16.9 us (23%)
  waiting for transfers between devices  12.2 us (17%)
  local copies, waits for them, and re-layouts  4.47 us (6%)
    all_to_all x1, blocking collectives, per_device(): signal = lax.all_to_all(sent, 'seq', 0, 0, tiled=True)  20.8 us
    pallas_call x1, Pallas kernels, long_conv(): pl.pallas_call(functools.partial(conv_kernel, rows=rows, rows_b=rows_b),...  10.2 us
    ppermute x6, starting transfers between devices, shift(): lax.ppermute(array, axis, [(i, (i + by) % length) for i in range(length)])  9.27 us
    ppermute x6, waiting for transfers between devices, shift(): lax.ppermute(array, axis, [(i, (i + by) % length) for i in range(length)])  5.63 us
    pallas_call x2, Pallas kernels, short_call(): pl.pallas_call(kernel, grid=(steps,), out_shape=jax.ShapeDtypeStruct(shap...  4.77 us
    dynamic_slice x1, local copies, waits for them, and re-layouts, project(): lax.dynamic_slice_in_dim(w_out, (place + i) % size * depth, depth, 0)  4.45 us
    all_to_all x1, waiting for transfers between devices, per_device(): lax.all_to_all(conv, 'seq', 0, 0, tiled=True).reshape(width, tok_rows)  4.12 us
    all_to_all x1, starting transfers between devices, per_device(): lax.all_to_all(conv, 'seq', 0, 0, tiled=True).reshape(width, tok_rows)  4.06 us
  transfers between devices with their start and end apart: 8, of which 4 were waited for; matrix products, arithmetic and copies ran while one was open for 6% of the time, Pallas kernels for 5%

profile of v4, /device:TPU:1, one launch (start us, length us, event | category | flops | bytes accessed | tf_op | source)
XLA Modules:
  0.0 73.1 jit_solution(11820363917159681447)
XLA Ops:
  0.0 0.0 copy-start.1
  0.0 0.0 copy-start.2
  0.0 0.0 copy-start.3
  0.0 3.2 %shard_map.55 = bf16[32,72,128]{2,1,0:T(8,128)(2,1)} custom-call(s32[8]{0:T(128)} %lengths_ref.5, bf16[3,256,1024]{2,1,0:T(8,128)(2,1)} %bitcast.5, bf16[3,256,1024]{2,1,0:T(8,128)(2,1)} %bitcast.6, f32[3,3,1024]{2,1,0:T(4,128)} %taps_ref.3), custom_call_target="tpu_custom_call" | custom-call | flops 5242880 | bytes 2097152 | tf_op jit(solution)/shard_map/pallas_call | solution.py:89
  3.2 20.8 %all_to_all.10.signal_ref = bf16[32,72,128]{2,1,0:T(8,128)(2,1)S(1)} all-to-all(bf16[32,72,128]{2,1,0:T(8,128)(2,1)} %shard_map.55), channel_id=1, replica_groups=mesh['seq'=32,'ch'=4] {'seq'}, dimensions={0} | all-to-all | bytes 1179648 | tf_op jit(solution)/shard_map/all_to_all | solution.py:395
  24.1 0.0 copy-done.1
  24.1 0.0 copy-done.2
  24.1 0.0 copy-done.3
  24.1 0.0 copy-start
  24.1 10.2 %shard_map.56 = bf16[32,32,256]{2,1,0:T(8,128)(2,1)} custom-call(s32[8]{0:T(128)S(1)} %copy-done.2, bf16[32,72,128]{2,1,0:T(8,128)(2,1)S(1)} %all_to_all.10.signal_ref, f32[32,2048]{1,0:T(8,128)S(1)} %bitcast.10, f32[3,3,1024]{2,1,0:T(4,128)S(1)} %copy-done.1), custom_call_target="tpu_custom_call" | custom-call | flops 1509949440 | bytes 2097152 | tf_op jit(solution)/shard_map/pallas_call | solution.py:284
  34.2 4.1 %all-to-all-start.1 = ((bf16[32,32,256]{2,1,0:T(8,128)(2,1)}), bf16[32,32,256]{2,1,0:T(8,128)(2,1)S(1)}, u32[]{:S(2)}, u32[]{:S(2)}) async-start(bf16[32,32,256]{2,1,0:T(8,128)(2,1)} %shard_map.56), calls=%async_computation.1 | async-start | bytes 1048576 | tf_op jit(solution)/shard_map/all_to_all | solution.py:400
  38.3 0.0 copy-done
  38.3 3.5 %collective-permute-start = (bf16[2,1024]{1,0:T(2,128)(2,1)S(1)}, bf16[2,1024]{1,0:T(2,128)(2,1)S(1)}, u32[]{:S(2)}, u32[]{:S(2)}) collective-permute-start(bf16[2,1024]{1,0:T(2,128)(2,1)S(1)} %slice_bitcast_fusion), channel_id=1, source_target_pairs={{0,4},{4,8},{8,12},{12,16},{16,20},{20,24},{24,28},{28,32},{32,36}... | collective-permute-start | bytes 12296 | tf_op jit(solution)/shard_map/ppermute | solution.py:398
  41.9 2.4 %collective-permute-done.edge_ref = bf16[2,1024]{1,0:T(2,128)(2,1)S(1)} collective-permute-done((bf16[2,1024]{1,0:T(2,128)(2,1)S(1)}, bf16[2,1024]{1,0:T(2,128)(2,1)S(1)}, u32[]{:S(2)}, u32[]{:S(2)}) %collective-permute-start) | collective-permute-done | bytes 4128 | tf_op jit(solution)/shard_map/ppermute | solution.py:398
  44.3 1.5 %shard_map.57.query_ref = bf16[256,1024]{1,0:T(8,128)(2,1)S(1)} custom-call(s32[8]{0:T(128)S(1)} %copy-done.2, bf16[3,256,1024]{2,1,0:T(8,128)(2,1)S(1)} %bitcast.8, bf16[2,1024]{1,0:T(2,128)(2,1)S(1)} %collective-permute-done.edge_ref, f32[3,3,1024]{2,1,0:T(4,128)S(1)} %copy-done.1), custom_call_target="tpu_custom_call" | custom-call | flops 5242880 | bytes 2097152 | tf_op jit(solution)/shard_map/pallas_call | solution.py:89
  45.9 4.1 %all-to-all-done.1 = bf16[32,32,256]{2,1,0:T(8,128)(2,1)S(1)} async-done(((bf16[32,32,256]{2,1,0:T(8,128)(2,1)}), bf16[32,32,256]{2,1,0:T(8,128)(2,1)S(1)}, u32[]{:S(2)}, u32[]{:S(2)}) %all-to-all-start.1) | async-done | bytes 524320 | tf_op jit(solution)/shard_map/all_to_all | solution.py:400
  50.0 0.2 shard_map.58
  50.2 1.7 %collective-permute-start.1 = (bf16[128,1024]{1,0:T(8,128)(2,1)S(1)}, bf16[128,1024]{1,0:T(8,128)(2,1)S(1)}, u32[]{:S(2)}, u32[]{:S(2)}) collective-permute-start(bf16[128,1024]{1,0:T(8,128)(2,1)S(1)} %get-tuple-element.11.refs_0_), channel_id=1, source_target_pairs={{0,1},{1,2},{2,3},{3,0},{4,5},{5,6},{6,7},{7,4},{8,9},{9,10},{10,1... | collective-permute-start | bytes 786440 | tf_op jit(solution)/shard_map/ppermute | solution.py:340
  51.9 2.2 %collective-permute-start.3 = (bf16[128,1024]{1,0:T(8,128)(2,1)S(1)}, bf16[128,1024]{1,0:T(8,128)(2,1)S(1)}, u32[]{:S(2)}, u32[]{:S(2)}) collective-permute-start(bf16[128,1024]{1,0:T(8,128)(2,1)S(1)} %get-tuple-element.12.refs_1_), channel_id=1, source_target_pairs={{0,3},{1,0},{2,1},{3,2},{4,7},{5,4},{6,5},{7,6},{8,11},{9,8},{10,9... | collective-permute-start | bytes 786440 | tf_op jit(solution)/shard_map/ppermute | solution.py:340
  54.1 0.0 collective-permute-start.5
  54.1 2.7 %collective-permute-start.6 = (bf16[128,1024]{1,0:T(8,128)(2,1)S(1)}, bf16[128,1024]{1,0:T(8,128)(2,1)S(1)}, u32[]{:S(2)}, u32[]{:S(2)}) collective-permute-start(bf16[128,1024]{1,0:T(8,128)(2,1)S(1)} %get-tuple-element.11.refs_0_), channel_id=1, source_target_pairs={{0,3},{1,0},{2,1},{3,2},{4,7},{5,4},{6,5},{7,6},{8,11},{9,8},{10,9... | collective-permute-start | bytes 786440 | tf_op jit(solution)/shard_map/ppermute | solution.py:340
  56.8 3.5 %collective-permute-done.1.refs_0_ = bf16[128,1024]{1,0:T(8,128)(2,1)S(1)} collective-permute-done((bf16[128,1024]{1,0:T(8,128)(2,1)S(1)}, bf16[128,1024]{1,0:T(8,128)(2,1)S(1)}, u32[]{:S(2)}, u32[]{:S(2)}) %collective-permute-start.1) | collective-permute-done | bytes 262176 | tf_op jit(solution)/shard_map/ppermute | solution.py:340
  60.3 0.0 collective-permute-start.2
  60.3 0.0 collective-permute-done.3.refs_3_
  60.3 2.7 %collective-permute-start.4 = (bf16[128,1024]{1,0:T(8,128)(2,1)S(1)}, bf16[128,1024]{1,0:T(8,128)(2,1)S(1)}, u32[]{:S(2)}, u32[]{:S(2)}) collective-permute-start(bf16[128,1024]{1,0:T(8,128)(2,1)S(1)} %collective-permute-done.3.refs_3_), channel_id=1, source_target_pairs={{0,3},{1,0},{2,1},{3,2},{4,7},{5,4},{6,5},{7,6},{8,11},{9,8},{10,9... | collective-permute-start | bytes 786440 | tf_op jit(solution)/shard_map/ppermute | solution.py:340
  63.0 4.4 %constant_dynamic-slice_fusion = (bf16[1024,1024]{1,0:T(8,128)(2,1)S(1)}, bf16[1024,1024]{1,0:T(8,128)(2,1)S(1)}, bf16[1024,1024]{1,0:T(8,128)(2,1)S(1)}, bf16[1024,1024]{1,0:T(8,128)(2,1)S(1)}) fusion(bf16[4096,1024]{1,0:T(8,128)(2,1)} %param.9, s32[]{:T(128)S(6)} %select_n.38, s32[]{:T(128)S(6)} %select_n.34, s32[]{:T(128)S(6)} %select_n.32, s32[]{:T(128)S(6)} %select_n.36), kind=kLoop, calls=%fused_computation.1 | loop fusion | bytes 16777232 | tf_op jit(solution)/shard_map/dynamic_slice | solution.py:377
  67.4 0.7 shard_map.59.refs_6_
  68.2 0.0 collective-permute-done.5.refs_1_
  68.2 0.0 collective-permute-done.6.refs_2_
  68.2 1.3 %shard_map.60.refs_3_ = f32[256,1024]{1,0:T(8,128)S(1)} custom-call(bf16[128,1024]{1,0:T(8,128)(2,1)S(1)} %collective-permute-done.1.refs_0_, bf16[128,1024]{1,0:T(8,128)(2,1)S(1)} %collective-permute-done.5.refs_1_, bf16[128,1024]{1,0:T(8,128)(2,1)S(1)} %collective-permute-done.6.refs_2_, bf16[128,1024]{1,0:T(8,128)(2,1)S(1)} %collective-permute-done.3.refs_3_, ...), custom_call_target="tpu_custom_call" | custom-call | flops 1073741824 | bytes 4194304 | tf_op jit(solution)/shard_map/pallas_call | solution.py:360
  69.5 2.1 %collective-permute-done.2.refs_0_ = bf16[128,1024]{1,0:T(8,128)(2,1)S(1)} collective-permute-done((bf16[128,1024]{1,0:T(8,128)(2,1)S(1)}, bf16[128,1024]{1,0:T(8,128)(2,1)S(1)}, u32[]{:S(2)}, u32[]{:S(2)}) %collective-permute-start.2) | collective-permute-done | bytes 262176 | tf_op jit(solution)/shard_map/ppermute | solution.py:340
  71.5 0.0 collective-permute-done.4.refs_1_
  71.5 1.5 %shard_map.61 = bf16[256,1024]{1,0:T(8,128)(2,1)} custom-call(bf16[128,1024]{1,0:T(8,128)(2,1)S(1)} %collective-permute-done.2.refs_0_, bf16[128,1024]{1,0:T(8,128)(2,1)S(1)} %collective-permute-done.4.refs_1_, bf16[1024,1024]{1,0:T(8,128)(2,1)S(1)} %get-tuple-element.15.refs_2_, f32[256,1024]{1,0:T(8,128)S(1)} %shard_map.60.refs_3_), custom_call_target="tpu_custom_call" | custom-call | flops 536870912 | bytes 2097152 | tf_op jit(solution)/shard_map/pallas_call | solution.py:360
  (1 shorter events, 0.0 us)
Async XLA Ops:
  0.0 24.1 %copy-start.1 = (f32[3,3,1024]{2,1,0:T(4,128)S(1)}, f32[3,3,1024]{2,1,0:T(4,128)}, u32[]{:S(2)}) copy-start(f32[3,3,1024]{2,1,0:T(4,128)} %taps_ref.3) | copy-start | bytes 110596
  0.0 24.1 %copy-start.2 = (s32[8]{0:T(128)S(1)}, s32[8]{0:T(128)}, u32[]{:S(2)}) copy-start(s32[8]{0:T(128)} %lengths_ref.5) | copy-start | bytes 100
  0.0 24.1 %copy-start.3 = (f32[1,32,2048]{2,1,0:T(8,128)S(1)}, f32[1,32,2048]{2,1,0:T(8,128)}, u32[]{:S(2)}) copy-start(f32[1,32,2048]{2,1,0:T(8,128)} %param.8) | copy-start | bytes 786436
  24.1 14.2 %copy-start = (bf16[256,3,1024]{2,0,1:T(8,128)(2,1)S(1)}, bf16[256,3,1024]{2,0,1:T(8,128)(2,1)}, u32[]{:S(2)}) copy-start(bf16[256,3,1024]{2,0,1:T(8,128)(2,1)} %param.5) | copy-start | bytes 4718596
  34.2 15.7 %all-to-all-start.1 = ((bf16[32,32,256]{2,1,0:T(8,128)(2,1)}), bf16[32,32,256]{2,1,0:T(8,128)(2,1)S(1)}, u32[]{:S(2)}, u32[]{:S(2)}) async-start(bf16[32,32,256]{2,1,0:T(8,128)(2,1)} %shard_map.56), calls=%async_computation.1 | async-start | bytes 1048576 | tf_op jit(solution)/shard_map/all_to_all | solution.py:400
  38.3 6.0 %collective-permute-start = (bf16[2,1024]{1,0:T(2,128)(2,1)S(1)}, bf16[2,1024]{1,0:T(2,128)(2,1)S(1)}, u32[]{:S(2)}, u32[]{:S(2)}) collective-permute-start(bf16[2,1024]{1,0:T(2,128)(2,1)S(1)} %slice_bitcast_fusion), channel_id=1, source_target_pairs={{0,4},{4,8},{8,12},{12,16},{16,20},{20,24},{24,28},{28,32},{32,36}... | collective-permute-start | bytes 12296 | tf_op jit(solution)/shard_map/ppermute | solution.py:398
  50.2 10.1 %collective-permute-start.1 = (bf16[128,1024]{1,0:T(8,128)(2,1)S(1)}, bf16[128,1024]{1,0:T(8,128)(2,1)S(1)}, u32[]{:S(2)}, u32[]{:S(2)}) collective-permute-start(bf16[128,1024]{1,0:T(8,128)(2,1)S(1)} %get-tuple-element.11.refs_0_), channel_id=1, source_target_pairs={{0,1},{1,2},{2,3},{3,0},{4,5},{5,6},{6,7},{7,4},{8,9},{9,10},{10,1... | collective-permute-start | bytes 786440 | tf_op jit(solution)/shard_map/ppermute | solution.py:340
  51.9 8.4 %collective-permute-start.3 = (bf16[128,1024]{1,0:T(8,128)(2,1)S(1)}, bf16[128,1024]{1,0:T(8,128)(2,1)S(1)}, u32[]{:S(2)}, u32[]{:S(2)}) collective-permute-start(bf16[128,1024]{1,0:T(8,128)(2,1)S(1)} %get-tuple-element.12.refs_1_), channel_id=1, source_target_pairs={{0,3},{1,0},{2,1},{3,2},{4,7},{5,4},{6,5},{7,6},{8,11},{9,8},{10,9... | collective-permute-start | bytes 786440 | tf_op jit(solution)/shard_map/ppermute | solution.py:340
  54.1 14.1 %collective-permute-start.5 = (bf16[128,1024]{1,0:T(8,128)(2,1)S(1)}, bf16[128,1024]{1,0:T(8,128)(2,1)S(1)}, u32[]{:S(2)}, u32[]{:S(2)}) collective-permute-start(bf16[128,1024]{1,0:T(8,128)(2,1)S(1)} %get-tuple-element.12.refs_1_), channel_id=1, source_target_pairs={{0,1},{1,2},{2,3},{3,0},{4,5},{5,6},{6,7},{7,4},{8,9},{9,10},{10,1... | collective-permute-start | bytes 786440 | tf_op jit(solution)/shard_map/ppermute | solution.py:340
  54.1 14.1 %collective-permute-start.6 = (bf16[128,1024]{1,0:T(8,128)(2,1)S(1)}, bf16[128,1024]{1,0:T(8,128)(2,1)S(1)}, u32[]{:S(2)}, u32[]{:S(2)}) collective-permute-start(bf16[128,1024]{1,0:T(8,128)(2,1)S(1)} %get-tuple-element.11.refs_0_), channel_id=1, source_target_pairs={{0,3},{1,0},{2,1},{3,2},{4,7},{5,4},{6,5},{7,6},{8,11},{9,8},{10,9... | collective-permute-start | bytes 786440 | tf_op jit(solution)/shard_map/ppermute | solution.py:340
  60.3 11.2 %collective-permute-start.2 = (bf16[128,1024]{1,0:T(8,128)(2,1)S(1)}, bf16[128,1024]{1,0:T(8,128)(2,1)S(1)}, u32[]{:S(2)}, u32[]{:S(2)}) collective-permute-start(bf16[128,1024]{1,0:T(8,128)(2,1)S(1)} %collective-permute-done.1.refs_0_), channel_id=1, source_target_pairs={{0,1},{1,2},{2,3},{3,0},{4,5},{5,6},{6,7},{7,4},{8,9},{9,10},{10,1... | collective-permute-start | bytes 786440 | tf_op jit(solution)/shard_map/ppermute | solution.py:340
  60.3 11.2 %collective-permute-start.4 = (bf16[128,1024]{1,0:T(8,128)(2,1)S(1)}, bf16[128,1024]{1,0:T(8,128)(2,1)S(1)}, u32[]{:S(2)}, u32[]{:S(2)}) collective-permute-start(bf16[128,1024]{1,0:T(8,128)(2,1)S(1)} %collective-permute-done.3.refs_3_), channel_id=1, source_target_pairs={{0,3},{1,0},{2,1},{3,2},{4,7},{5,4},{6,5},{7,6},{8,11},{9,8},{10,9... | collective-permute-start | bytes 786440 | tf_op jit(solution)/shard_map/ppermute | solution.py:340

commit v5 on v4

--- a/solution.py
+++ b/solution.py
@@ -193,46 +193,46 @@
     return product.astype(jnp.bfloat16).astype(jnp.float32)
 
 
+def pitch_of(rows):
+    return rows | 1
+
+
 def conv_kernel(
     lengths_ref, signal_ref, taps_ref, short_ref, out_ref, table, heads, blocks, edges, spread, result, before, toep, *, rows, rows_b
 ):
-    step = pl.program_id(0)
     devices, channels, _ = out_ref.shape
-    group, span = taps_ref.shape
+    span = taps_ref.shape[1]
     lags = span // BLK + 1
     tiles = span // TILE + 1
-    pitch = PAD + rows_b
-
-    @pl.when(step == 0)
-    def _():
-        list_rows(lengths_ref, table, heads, rows)
-        for device in range(devices):
-            arrived = signal_ref[device].astype(jnp.float32)
-            for h in range(2):
-                blocks[device, :, h * TILE : (h + 1) * TILE] = arrived[h * channels : (h + 1) * channels]
-            edges[device * EDGES : (device + 1) * EDGES, :] = arrived[2 * channels :]
-        firsts = first_products(lengths_ref, edges[...], short_ref, channels)
-        is_first = lax.broadcasted_iota(jnp.int32, (channels, TILE), 1) < TAPS - 1
-        for device in range(devices):
-            at = device * EDGES
-            mine = firsts[:, at // TILE * TILE : (at // TILE + 1) * TILE]
-            mine = mine if at % TILE == 0 else pltpu.roll(mine, TILE - at % TILE, 1)
-            blocks[device, :, :TILE] = jnp.where(is_first, mine, blocks[device, :, :TILE])
-        for row in range(rows):
-            slab = only_lanes(table, row, blocks[table[0, row]], 0.0)
-            for h in range(2):
-                spread[h, pl.ds(PAD + row, channels, stride=pitch), :] = slab[:, h * TILE : (h + 1) * TILE]
-        before[...] = rows_before(lengths_ref, rows_b)
-
-    views = spread.reshape(2, channels, pitch, TILE)
+    pitch, held = pitch_of(PAD + rows_b), pitch_of(rows)
+
+    list_rows(lengths_ref, table, heads, rows)
+    for device in range(devices):
+        arrived = signal_ref[device].astype(jnp.float32)
+        for h in range(2):
+            blocks[device, :, h * TILE : (h + 1) * TILE] = arrived[h * channels : (h + 1) * channels]
+        edges[device * EDGES : (device + 1) * EDGES, :] = arrived[2 * channels :]
+    firsts = first_products(lengths_ref, edges[...], short_ref, channels)
+    is_first = lax.broadcasted_iota(jnp.int32, (channels, TILE), 1) < TAPS - 1
+    for device in range(devices):
+        at = device * EDGES
+        mine = firsts[:, at // TILE * TILE : (at // TILE + 1) * TILE]
+        mine = mine if at % TILE == 0 else pltpu.roll(mine, TILE - at % TILE, 1)
+        blocks[device, :, :TILE] = jnp.where(is_first, mine, blocks[device, :, :TILE])
+    for row in range(rows):
+        slab = only_lanes(table, row, blocks[table[0, row]], 0.0)
+        for h in range(2):
+            spread[h, pl.ds(PAD + row, channels, stride=pitch), :] = slab[:, h * TILE : (h + 1) * TILE]
+    before[...] = rows_before(lengths_ref, rows_b)
+
     zero = jnp.zeros((TILE, TILE), jnp.bfloat16)
     behind = before[...]
 
     def tile(g, t):
         return toep[g, t * TILE : (t + 1) * TILE, :] if 0 <= t < tiles else zero
 
-    for g in range(group):
-        channel = step * group + g
+    for g in range(channels):
+        base = g * pitch + PAD
         row = jnp.concatenate([taps_ref[g : g + 1, :], jnp.zeros((1, TILE), jnp.float32)], 1)
         sheared = pltpu.roll(jnp.broadcast_to(row, (TILE, span + TILE)), 0, 1, stride=1, stride_axis=0)
         for t in range(tiles):
@@ -242,7 +242,7 @@
             kept = behind >= lag
             left = jnp.concatenate(
                 [
-                    jnp.where(kept, views[h, channel, PAD - lag : PAD - lag + rows_b, :], 0.0).astype(jnp.bfloat16)
+                    jnp.where(kept, spread[h, base - lag : base - lag + rows_b, :], 0.0).astype(jnp.bfloat16)
                     for h in range(2)
                 ],
                 1,
@@ -258,37 +258,39 @@
             term = jnp.dot(left, right, preferred_element_type=jnp.float32)
             total = term if total is None else total + term
         for h in range(2):
-            result[h, pl.ds(channel * rows, rows), :] = total[:rows, h * TILE : (h + 1) * TILE]
-
-    @pl.when(step == pl.num_programs(0) - 1)
-    def _():
-        def slab_of(row):
-            return jnp.concatenate([result[h, pl.ds(row, channels, stride=rows), :] for h in range(2)], 1)
-
-        for block in range(devices):
-            out_ref[block] = slab_of(heads[0, block]).astype(jnp.bfloat16)
-        for prompt in range(lengths_ref.shape[0]):
-            row = heads[1, prompt]
-            block = table[0, row]
-            old = out_ref[block].astype(jnp.float32)
-            out_ref[block] = only_lanes(table, row, slab_of(row), old).astype(jnp.bfloat16)
-
-
-def long_conv(lengths, signal, taps, short_taps, group=32):
+            result[h, g * held : g * held + rows, :] = total[:rows, h * TILE : (h + 1) * TILE]
+
+    def slab_of(row):
+        return jnp.concatenate([result[h, pl.ds(row, channels, stride=held), :] for h in range(2)], 1)
+
+    for block in range(devices):
+        out_ref[block] = slab_of(heads[0, block]).astype(jnp.bfloat16)
+    for prompt in range(lengths_ref.shape[0]):
+        row = heads[1, prompt]
+        block = table[0, row]
+        old = out_ref[block].astype(jnp.float32)
+        out_ref[block] = only_lanes(table, row, slab_of(row), old).astype(jnp.bfloat16)
+
+
+def round_up(value, to):
+    return -(-value // to) * to
+
+
+def long_conv(lengths, signal, taps, short_taps):
     devices, tok_rows = signal.shape[0], BLK
     channels = taps.shape[0]
     shape = (devices, channels, tok_rows)
     span = taps.shape[1]
-    rows = -(-(devices + lengths.shape[0] - 1) // 8) * 8
-    rows_b = -(-rows // 16) * 16
+    rows = round_up(devices + lengths.shape[0] - 1, 8)
+    rows_b = round_up(rows, 16)
     return pl.pallas_call(
         functools.partial(conv_kernel, rows=rows, rows_b=rows_b),
-        grid=(channels // group,),
+        grid=(1,),
         out_shape=jax.ShapeDtypeStruct(shape, jnp.bfloat16),
         in_specs=[
             pl.BlockSpec(memory_space=pltpu.SMEM),
             pl.BlockSpec(signal.shape, lambda i: (0, 0, 0)),
-            pl.BlockSpec((group, span), lambda i: (i, 0)),
+            pl.BlockSpec((channels, span), lambda i: (0, 0)),
             pl.BlockSpec(short_taps.shape, lambda i: (0, 0, 0)),
         ],
         out_specs=pl.BlockSpec(shape, lambda i: (0, 0, 0)),
@@ -297,10 +299,10 @@
             pltpu.SMEM((2, devices), jnp.int32),
             pltpu.VMEM(shape, jnp.float32),
             pltpu.VMEM((devices * EDGES, TILE), jnp.float32),
-            pltpu.VMEM((2, channels * (PAD + rows_b), TILE), jnp.float32),
-            pltpu.VMEM((2, channels * rows, TILE), jnp.float32),
+            pltpu.VMEM((2, round_up(channels * pitch_of(PAD + rows_b), 8), TILE), jnp.float32),
+            pltpu.VMEM((2, round_up(channels * pitch_of(rows), 8), TILE), jnp.float32),
             pltpu.VMEM((rows_b, TILE), jnp.int32),
-            pltpu.VMEM((group, span + TILE, TILE), jnp.bfloat16),
+            pltpu.VMEM((channels, span + TILE, TILE), jnp.bfloat16),
         ],
         compiler_params=params(GRANT),
         cost_estimate=pl.CostEstimate(

time: 73.4 us -> 73.1 us (level)
  no operation moved by 1% of the time
where the time goes in v5:
time: 73.1 us; the launch traced here: 72.8 us
  blocking collectives  20.8 us (28%)
  Pallas kernels  18.3 us (25%)
  starting transfers between devices  16.9 us (23%)
  waiting for transfers between devices  12.2 us (17%)
  local copies, waits for them, and re-layouts  4.47 us (6%)
    all_to_all x1, blocking collectives, per_device(): signal = lax.all_to_all(sent, 'seq', 0, 0, tiled=True)  20.8 us
    pallas_call x1, Pallas kernels, long_conv(): pl.pallas_call(functools.partial(conv_kernel, rows=rows, rows_b=rows_b),...  9.86 us
    ppermute x6, starting transfers between devices, shift(): lax.ppermute(array, axis, [(i, (i + by) % length) for i in range(length)])  9.26 us
    ppermute x6, waiting for transfers between devices, shift(): lax.ppermute(array, axis, [(i, (i + by) % length) for i in range(length)])  5.63 us
    pallas_call x2, Pallas kernels, short_call(): pl.pallas_call(kernel, grid=(steps,), out_shape=jax.ShapeDtypeStruct(shap...  4.77 us
    dynamic_slice x1, local copies, waits for them, and re-layouts, project(): lax.dynamic_slice_in_dim(w_out, (place + i) % size * depth, depth, 0)  4.45 us
    all_to_all x1, waiting for transfers between devices, per_device(): lax.all_to_all(conv, 'seq', 0, 0, tiled=True).reshape(width, tok_rows)  4.12 us
    all_to_all x1, starting transfers between devices, per_device(): lax.all_to_all(conv, 'seq', 0, 0, tiled=True).reshape(width, tok_rows)  4.06 us
  transfers between devices with their start and end apart: 8, of which 4 were waited for; matrix products, arithmetic and copies ran while one was open for 6% of the time, Pallas kernels for 5%

profile of v5, /device:TPU:1, one launch (start us, length us, event | category | flops | bytes accessed | tf_op | source)
XLA Modules:
  0.0 72.8 jit_solution(12585260469834354006)
XLA Ops:
  0.0 0.0 copy-start.1
  0.0 0.0 copy-start.2
  0.0 0.0 copy-start.3
  0.0 3.2 %shard_map.55 = bf16[32,72,128]{2,1,0:T(8,128)(2,1)} custom-call(s32[8]{0:T(128)} %lengths_ref.5, bf16[3,256,1024]{2,1,0:T(8,128)(2,1)} %bitcast.5, bf16[3,256,1024]{2,1,0:T(8,128)(2,1)} %bitcast.6, f32[3,3,1024]{2,1,0:T(4,128)} %taps_ref.3), custom_call_target="tpu_custom_call" | custom-call | flops 5242880 | bytes 2097152 | tf_op jit(solution)/shard_map/pallas_call | solution.py:89
  3.2 20.8 %all_to_all.10.signal_ref = bf16[32,72,128]{2,1,0:T(8,128)(2,1)S(1)} all-to-all(bf16[32,72,128]{2,1,0:T(8,128)(2,1)} %shard_map.55), channel_id=1, replica_groups=mesh['seq'=32,'ch'=4] {'seq'}, dimensions={0} | all-to-all | bytes 1179648 | tf_op jit(solution)/shard_map/all_to_all | solution.py:397
  24.1 0.0 copy-done.1
  24.1 0.0 copy-done.2
  24.1 0.0 copy-done.3
  24.1 0.0 copy-start
  24.1 9.9 %shard_map.56 = bf16[32,32,256]{2,1,0:T(8,128)(2,1)} custom-call(s32[8]{0:T(128)S(1)} %copy-done.2, bf16[32,72,128]{2,1,0:T(8,128)(2,1)S(1)} %all_to_all.10.signal_ref, f32[32,2048]{1,0:T(8,128)S(1)} %bitcast.10, f32[3,3,1024]{2,1,0:T(4,128)S(1)} %copy-done.1), custom_call_target="tpu_custom_call" | custom-call | flops 1509949440 | bytes 2097152 | tf_op jit(solution)/shard_map/pallas_call | solution.py:286
  34.0 4.1 %all-to-all-start.1 = ((bf16[32,32,256]{2,1,0:T(8,128)(2,1)}), bf16[32,32,256]{2,1,0:T(8,128)(2,1)S(1)}, u32[]{:S(2)}, u32[]{:S(2)}) async-start(bf16[32,32,256]{2,1,0:T(8,128)(2,1)} %shard_map.56), calls=%async_computation.1 | async-start | bytes 1048576 | tf_op jit(solution)/shard_map/all_to_all | solution.py:402
  38.0 0.0 copy-done
  38.0 3.5 %collective-permute-start = (bf16[2,1024]{1,0:T(2,128)(2,1)S(1)}, bf16[2,1024]{1,0:T(2,128)(2,1)S(1)}, u32[]{:S(2)}, u32[]{:S(2)}) collective-permute-start(bf16[2,1024]{1,0:T(2,128)(2,1)S(1)} %slice_bitcast_fusion), channel_id=1, source_target_pairs={{0,4},{4,8},{8,12},{12,16},{16,20},{20,24},{24,28},{28,32},{32,36}... | collective-permute-start | bytes 12296 | tf_op jit(solution)/shard_map/ppermute | solution.py:400
  41.6 2.4 %collective-permute-done.edge_ref = bf16[2,1024]{1,0:T(2,128)(2,1)S(1)} collective-permute-done((bf16[2,1024]{1,0:T(2,128)(2,1)S(1)}, bf16[2,1024]{1,0:T(2,128)(2,1)S(1)}, u32[]{:S(2)}, u32[]{:S(2)}) %collective-permute-start) | collective-permute-done | bytes 4128 | tf_op jit(solution)/shard_map/ppermute | solution.py:400
  44.0 1.5 %shard_map.57.query_ref = bf16[256,1024]{1,0:T(8,128)(2,1)S(1)} custom-call(s32[8]{0:T(128)S(1)} %copy-done.2, bf16[3,256,1024]{2,1,0:T(8,128)(2,1)S(1)} %bitcast.8, bf16[2,1024]{1,0:T(2,128)(2,1)S(1)} %collective-permute-done.edge_ref, f32[3,3,1024]{2,1,0:T(4,128)S(1)} %copy-done.1), custom_call_target="tpu_custom_call" | custom-call | flops 5242880 | bytes 2097152 | tf_op jit(solution)/shard_map/pallas_call | solution.py:89
  45.6 4.1 %all-to-all-done.1 = bf16[32,32,256]{2,1,0:T(8,128)(2,1)S(1)} async-done(((bf16[32,32,256]{2,1,0:T(8,128)(2,1)}), bf16[32,32,256]{2,1,0:T(8,128)(2,1)S(1)}, u32[]{:S(2)}, u32[]{:S(2)}) %all-to-all-start.1) | async-done | bytes 524320 | tf_op jit(solution)/shard_map/all_to_all | solution.py:402
  49.7 0.2 shard_map.58
  49.9 1.7 %collective-permute-start.1 = (bf16[128,1024]{1,0:T(8,128)(2,1)S(1)}, bf16[128,1024]{1,0:T(8,128)(2,1)S(1)}, u32[]{:S(2)}, u32[]{:S(2)}) collective-permute-start(bf16[128,1024]{1,0:T(8,128)(2,1)S(1)} %get-tuple-element.11.refs_0_), channel_id=1, source_target_pairs={{0,1},{1,2},{2,3},{3,0},{4,5},{5,6},{6,7},{7,4},{8,9},{9,10},{10,1... | collective-permute-start | bytes 786440 | tf_op jit(solution)/shard_map/ppermute | solution.py:342
  51.6 2.2 %collective-permute-start.3 = (bf16[128,1024]{1,0:T(8,128)(2,1)S(1)}, bf16[128,1024]{1,0:T(8,128)(2,1)S(1)}, u32[]{:S(2)}, u32[]{:S(2)}) collective-permute-start(bf16[128,1024]{1,0:T(8,128)(2,1)S(1)} %get-tuple-element.12.refs_1_), channel_id=1, source_target_pairs={{0,3},{1,0},{2,1},{3,2},{4,7},{5,4},{6,5},{7,6},{8,11},{9,8},{10,9... | collective-permute-start | bytes 786440 | tf_op jit(solution)/shard_map/ppermute | solution.py:342
  53.8 0.0 collective-permute-start.5
  53.8 2.7 %collective-permute-start.6 = (bf16[128,1024]{1,0:T(8,128)(2,1)S(1)}, bf16[128,1024]{1,0:T(8,128)(2,1)S(1)}, u32[]{:S(2)}, u32[]{:S(2)}) collective-permute-start(bf16[128,1024]{1,0:T(8,128)(2,1)S(1)} %get-tuple-element.11.refs_0_), channel_id=1, source_target_pairs={{0,3},{1,0},{2,1},{3,2},{4,7},{5,4},{6,5},{7,6},{8,11},{9,8},{10,9... | collective-permute-start | bytes 786440 | tf_op jit(solution)/shard_map/ppermute | solution.py:342
  56.5 3.5 %collective-permute-done.1.refs_0_ = bf16[128,1024]{1,0:T(8,128)(2,1)S(1)} collective-permute-done((bf16[128,1024]{1,0:T(8,128)(2,1)S(1)}, bf16[128,1024]{1,0:T(8,128)(2,1)S(1)}, u32[]{:S(2)}, u32[]{:S(2)}) %collective-permute-start.1) | collective-permute-done | bytes 262176 | tf_op jit(solution)/shard_map/ppermute | solution.py:342
  60.0 0.0 collective-permute-start.2
  60.0 0.0 collective-permute-done.3.refs_3_
  60.0 2.7 %collective-permute-start.4 = (bf16[128,1024]{1,0:T(8,128)(2,1)S(1)}, bf16[128,1024]{1,0:T(8,128)(2,1)S(1)}, u32[]{:S(2)}, u32[]{:S(2)}) collective-permute-start(bf16[128,1024]{1,0:T(8,128)(2,1)S(1)} %collective-permute-done.3.refs_3_), channel_id=1, source_target_pairs={{0,3},{1,0},{2,1},{3,2},{4,7},{5,4},{6,5},{7,6},{8,11},{9,8},{10,9... | collective-permute-start | bytes 786440 | tf_op jit(solution)/shard_map/ppermute | solution.py:342
  62.7 4.4 %constant_dynamic-slice_fusion = (bf16[1024,1024]{1,0:T(8,128)(2,1)S(1)}, bf16[1024,1024]{1,0:T(8,128)(2,1)S(1)}, bf16[1024,1024]{1,0:T(8,128)(2,1)S(1)}, bf16[1024,1024]{1,0:T(8,128)(2,1)S(1)}) fusion(bf16[4096,1024]{1,0:T(8,128)(2,1)} %param.9, s32[]{:T(128)S(6)} %select_n.38, s32[]{:T(128)S(6)} %select_n.34, s32[]{:T(128)S(6)} %select_n.32, s32[]{:T(128)S(6)} %select_n.36), kind=kLoop, calls=%fused_computation.1 | loop fusion | bytes 16777232 | tf_op jit(solution)/shard_map/dynamic_slice | solution.py:379
  67.1 0.7 shard_map.59.refs_6_
  67.9 0.0 collective-permute-done.5.refs_1_
  67.9 0.0 collective-permute-done.6.refs_2_
  67.9 1.3 %shard_map.60.refs_3_ = f32[256,1024]{1,0:T(8,128)S(1)} custom-call(bf16[128,1024]{1,0:T(8,128)(2,1)S(1)} %collective-permute-done.1.refs_0_, bf16[128,1024]{1,0:T(8,128)(2,1)S(1)} %collective-permute-done.5.refs_1_, bf16[128,1024]{1,0:T(8,128)(2,1)S(1)} %collective-permute-done.6.refs_2_, bf16[128,1024]{1,0:T(8,128)(2,1)S(1)} %collective-permute-done.3.refs_3_, ...), custom_call_target="tpu_custom_call" | custom-call | flops 1073741824 | bytes 4194304 | tf_op jit(solution)/shard_map/pallas_call | solution.py:362
  69.2 2.1 %collective-permute-done.2.refs_0_ = bf16[128,1024]{1,0:T(8,128)(2,1)S(1)} collective-permute-done((bf16[128,1024]{1,0:T(8,128)(2,1)S(1)}, bf16[128,1024]{1,0:T(8,128)(2,1)S(1)}, u32[]{:S(2)}, u32[]{:S(2)}) %collective-permute-start.2) | collective-permute-done | bytes 262176 | tf_op jit(solution)/shard_map/ppermute | solution.py:342
  71.2 0.0 collective-permute-done.4.refs_1_
  71.2 1.5 %shard_map.61 = bf16[256,1024]{1,0:T(8,128)(2,1)} custom-call(bf16[128,1024]{1,0:T(8,128)(2,1)S(1)} %collective-permute-done.2.refs_0_, bf16[128,1024]{1,0:T(8,128)(2,1)S(1)} %collective-permute-done.4.refs_1_, bf16[1024,1024]{1,0:T(8,128)(2,1)S(1)} %get-tuple-element.15.refs_2_, f32[256,1024]{1,0:T(8,128)S(1)} %shard_map.60.refs_3_), custom_call_target="tpu_custom_call" | custom-call | flops 536870912 | bytes 2097152 | tf_op jit(solution)/shard_map/pallas_call | solution.py:362
  (1 shorter events, 0.0 us)
Async XLA Ops:
  0.0 24.1 %copy-start.1 = (f32[3,3,1024]{2,1,0:T(4,128)S(1)}, f32[3,3,1024]{2,1,0:T(4,128)}, u32[]{:S(2)}) copy-start(f32[3,3,1024]{2,1,0:T(4,128)} %taps_ref.3) | copy-start | bytes 110596
  0.0 24.1 %copy-start.2 = (s32[8]{0:T(128)S(1)}, s32[8]{0:T(128)}, u32[]{:S(2)}) copy-start(s32[8]{0:T(128)} %lengths_ref.5) | copy-start | bytes 100
  0.0 24.1 %copy-start.3 = (f32[1,32,2048]{2,1,0:T(8,128)S(1)}, f32[1,32,2048]{2,1,0:T(8,128)}, u32[]{:S(2)}) copy-start(f32[1,32,2048]{2,1,0:T(8,128)} %param.8) | copy-start | bytes 786436
  24.1 13.9 %copy-start = (bf16[256,3,1024]{2,0,1:T(8,128)(2,1)S(1)}, bf16[256,3,1024]{2,0,1:T(8,128)(2,1)}, u32[]{:S(2)}) copy-start(bf16[256,3,1024]{2,0,1:T(8,128)(2,1)} %param.5) | copy-start | bytes 4718596
  34.0 15.7 %all-to-all-start.1 = ((bf16[32,32,256]{2,1,0:T(8,128)(2,1)}), bf16[32,32,256]{2,1,0:T(8,128)(2,1)S(1)}, u32[]{:S(2)}, u32[]{:S(2)}) async-start(bf16[32,32,256]{2,1,0:T(8,128)(2,1)} %shard_map.56), calls=%async_computation.1 | async-start | bytes 1048576 | tf_op jit(solution)/shard_map/all_to_all | solution.py:402
  38.0 6.0 %collective-permute-start = (bf16[2,1024]{1,0:T(2,128)(2,1)S(1)}, bf16[2,1024]{1,0:T(2,128)(2,1)S(1)}, u32[]{:S(2)}, u32[]{:S(2)}) collective-permute-start(bf16[2,1024]{1,0:T(2,128)(2,1)S(1)} %slice_bitcast_fusion), channel_id=1, source_target_pairs={{0,4},{4,8},{8,12},{12,16},{16,20},{20,24},{24,28},{28,32},{32,36}... | collective-permute-start | bytes 12296 | tf_op jit(solution)/shard_map/ppermute | solution.py:400
  49.9 10.1 %collective-permute-start.1 = (bf16[128,1024]{1,0:T(8,128)(2,1)S(1)}, bf16[128,1024]{1,0:T(8,128)(2,1)S(1)}, u32[]{:S(2)}, u32[]{:S(2)}) collective-permute-start(bf16[128,1024]{1,0:T(8,128)(2,1)S(1)} %get-tuple-element.11.refs_0_), channel_id=1, source_target_pairs={{0,1},{1,2},{2,3},{3,0},{4,5},{5,6},{6,7},{7,4},{8,9},{9,10},{10,1... | collective-permute-start | bytes 786440 | tf_op jit(solution)/shard_map/ppermute | solution.py:342
  51.6 8.4 %collective-permute-start.3 = (bf16[128,1024]{1,0:T(8,128)(2,1)S(1)}, bf16[128,1024]{1,0:T(8,128)(2,1)S(1)}, u32[]{:S(2)}, u32[]{:S(2)}) collective-permute-start(bf16[128,1024]{1,0:T(8,128)(2,1)S(1)} %get-tuple-element.12.refs_1_), channel_id=1, source_target_pairs={{0,3},{1,0},{2,1},{3,2},{4,7},{5,4},{6,5},{7,6},{8,11},{9,8},{10,9... | collective-permute-start | bytes 786440 | tf_op jit(solution)/shard_map/ppermute | solution.py:342
  53.8 14.1 %collective-permute-start.5 = (bf16[128,1024]{1,0:T(8,128)(2,1)S(1)}, bf16[128,1024]{1,0:T(8,128)(2,1)S(1)}, u32[]{:S(2)}, u32[]{:S(2)}) collective-permute-start(bf16[128,1024]{1,0:T(8,128)(2,1)S(1)} %get-tuple-element.12.refs_1_), channel_id=1, source_target_pairs={{0,1},{1,2},{2,3},{3,0},{4,5},{5,6},{6,7},{7,4},{8,9},{9,10},{10,1... | collective-permute-start | bytes 786440 | tf_op jit(solution)/shard_map/ppermute | solution.py:342
  53.8 14.1 %collective-permute-start.6 = (bf16[128,1024]{1,0:T(8,128)(2,1)S(1)}, bf16[128,1024]{1,0:T(8,128)(2,1)S(1)}, u32[]{:S(2)}, u32[]{:S(2)}) collective-permute-start(bf16[128,1024]{1,0:T(8,128)(2,1)S(1)} %get-tuple-element.11.refs_0_), channel_id=1, source_target_pairs={{0,3},{1,0},{2,1},{3,2},{4,7},{5,4},{6,5},{7,6},{8,11},{9,8},{10,9... | collective-permute-start | bytes 786440 | tf_op jit(solution)/shard_map/ppermute | solution.py:342
  60.0 11.2 %collective-permute-start.2 = (bf16[128,1024]{1,0:T(8,128)(2,1)S(1)}, bf16[128,1024]{1,0:T(8,128)(2,1)S(1)}, u32[]{:S(2)}, u32[]{:S(2)}) collective-permute-start(bf16[128,1024]{1,0:T(8,128)(2,1)S(1)} %collective-permute-done.1.refs_0_), channel_id=1, source_target_pairs={{0,1},{1,2},{2,3},{3,0},{4,5},{5,6},{6,7},{7,4},{8,9},{9,10},{10,1... | collective-permute-start | bytes 786440 | tf_op jit(solution)/shard_map/ppermute | solution.py:342
  60.0 11.2 %collective-permute-start.4 = (bf16[128,1024]{1,0:T(8,128)(2,1)S(1)}, bf16[128,1024]{1,0:T(8,128)(2,1)S(1)}, u32[]{:S(2)}, u32[]{:S(2)}) collective-permute-start(bf16[128,1024]{1,0:T(8,128)(2,1)S(1)} %collective-permute-done.3.refs_3_), channel_id=1, source_target_pairs={{0,3},{1,0},{2,1},{3,2},{4,7},{5,4},{6,5},{7,6},{8,11},{9,8},{10,9... | collective-permute-start | bytes 786440 | tf_op jit(solution)/shard_map/ppermute | solution.py:342

commit v6 on v5

--- a/solution.py
+++ b/solution.py
@@ -225,11 +225,10 @@
             spread[h, pl.ds(PAD + row, channels, stride=pitch), :] = slab[:, h * TILE : (h + 1) * TILE]
     before[...] = rows_before(lengths_ref, rows_b)
 
-    zero = jnp.zeros((TILE, TILE), jnp.bfloat16)
     behind = before[...]
 
     def tile(g, t):
-        return toep[g, t * TILE : (t + 1) * TILE, :] if 0 <= t < tiles else zero
+        return toep[g, t * TILE : (t + 1) * TILE, :]
 
     for g in range(channels):
         base = g * pitch + PAD
@@ -237,26 +236,29 @@
         sheared = pltpu.roll(jnp.broadcast_to(row, (TILE, span + TILE)), 0, 1, stride=1, stride_axis=0)
         for t in range(tiles):
             toep[g, t * TILE : (t + 1) * TILE, :] = sheared[:, t * TILE : (t + 1) * TILE].astype(jnp.bfloat16)
-        total = None
-        for lag in range(lags):
-            kept = behind >= lag
-            left = jnp.concatenate(
-                [
-                    jnp.where(kept, spread[h, base - lag : base - lag + rows_b, :], 0.0).astype(jnp.bfloat16)
-                    for h in range(2)
-                ],
-                1,
+        lefts = [
+            [
+                jnp.where(behind >= lag, spread[h, base - lag : base - lag + rows_b, :], 0.0).astype(jnp.bfloat16)
+                for h in range(2)
+            ]
+            for lag in range(lags)
+        ]
+        last = lags - 1
+        both = jnp.concatenate([lefts[last][0], lefts[0][1]], 0)
+        both = jnp.dot(both, jnp.concatenate([tile(g, 2 * last), tile(g, 0)], 1), preferred_element_type=jnp.float32)
+        total = jnp.concatenate([both[:rows_b, :TILE], both[rows_b:, TILE:]], 1)
+        for lag in range(last):
+            t = 2 * lag
+            if lag == 0:
+                left = [lefts[0][0], lefts[last][1]]
+                lower = [tile(g, 2 * last - 1), tile(g, 2 * last)]
+            else:
+                left = lefts[lag]
+                lower = [tile(g, t - 1), tile(g, t)]
+            right = [jnp.concatenate([tile(g, t), tile(g, t + 1)], 1), jnp.concatenate(lower, 1)]
+            total = total + jnp.dot(
+                jnp.concatenate(left, 1), jnp.concatenate(right, 0), preferred_element_type=jnp.float32
             )
-            t = 2 * lag
-            right = jnp.concatenate(
-                [
-                    jnp.concatenate([tile(g, t), tile(g, t + 1)], 1),
-                    jnp.concatenate([tile(g, t - 1), tile(g, t)], 1),
-                ],
-                0,
-            )
-            term = jnp.dot(left, right, preferred_element_type=jnp.float32)
-            total = term if total is None else total + term
         for h in range(2):
             result[h, g * held : g * held + rows, :] = total[:rows, h * TILE : (h + 1) * TILE]
 

time: 73.1 us -> 72 us (0.985)
  Pallas kernels: 18.3 us -> 17.3 us
    pallas_call x1, Pallas kernels: 9.86 us -> 8.8 us  [long_conv(): pl.pallas_call(functools.partial(conv_kernel, rows=rows, rows_b=rows_b),...]
where the time goes in v6:
time: 72 us; the launch traced here: 71.7 us
  blocking collectives  20.8 us (29%)
  Pallas kernels  17.3 us (24%)
  starting transfers between devices  16.9 us (23%)
  waiting for transfers between devices  12.2 us (17%)
  local copies, waits for them, and re-layouts  4.47 us (6%)
    all_to_all x1, blocking collectives, per_device(): signal = lax.all_to_all(sent, 'seq', 0, 0, tiled=True)  20.8 us
    ppermute x6, starting transfers between devices, shift(): lax.ppermute(array, axis, [(i, (i + by) % length) for i in range(length)])  9.26 us
    pallas_call x1, Pallas kernels, long_conv(): pl.pallas_call(functools.partial(conv_kernel, rows=rows, rows_b=rows_b),...  8.8 us
    ppermute x6, waiting for transfers between devices, shift(): lax.ppermute(array, axis, [(i, (i + by) % length) for i in range(length)])  5.63 us
    pallas_call x2, Pallas kernels, short_call(): pl.pallas_call(kernel, grid=(steps,), out_shape=jax.ShapeDtypeStruct(shap...  4.77 us
    dynamic_slice x1, local copies, waits for them, and re-layouts, project(): lax.dynamic_slice_in_dim(w_out, (place + i) % size * depth, depth, 0)  4.45 us
    all_to_all x1, waiting for transfers between devices, per_device(): lax.all_to_all(conv, 'seq', 0, 0, tiled=True).reshape(width, tok_rows)  4.12 us
    all_to_all x1, starting transfers between devices, per_device(): lax.all_to_all(conv, 'seq', 0, 0, tiled=True).reshape(width, tok_rows)  4.06 us
  transfers between devices with their start and end apart: 8, of which 4 were waited for; matrix products, arithmetic and copies ran while one was open for 6% of the time, Pallas kernels for 5%

profile of v6, /device:TPU:1, one launch (start us, length us, event | category | flops | bytes accessed | tf_op | source)
XLA Modules:
  0.0 71.7 jit_solution(11961369776891389759)
XLA Ops:
  0.0 0.0 copy-start.1
  0.0 0.0 copy-start.2
  0.0 0.0 copy-start.3
  0.0 3.2 %shard_map.55 = bf16[32,72,128]{2,1,0:T(8,128)(2,1)} custom-call(s32[8]{0:T(128)} %lengths_ref.5, bf16[3,256,1024]{2,1,0:T(8,128)(2,1)} %bitcast.5, bf16[3,256,1024]{2,1,0:T(8,128)(2,1)} %bitcast.6, f32[3,3,1024]{2,1,0:T(4,128)} %taps_ref.3), custom_call_target="tpu_custom_call" | custom-call | flops 5242880 | bytes 2097152 | tf_op jit(solution)/shard_map/pallas_call | solution.py:89
  3.2 20.8 %all_to_all.10.signal_ref = bf16[32,72,128]{2,1,0:T(8,128)(2,1)S(1)} all-to-all(bf16[32,72,128]{2,1,0:T(8,128)(2,1)} %shard_map.55), channel_id=1, replica_groups=mesh['seq'=32,'ch'=4] {'seq'}, dimensions={0} | all-to-all | bytes 1179648 | tf_op jit(solution)/shard_map/all_to_all | solution.py:399
  24.1 0.0 copy-done.1
  24.1 0.0 copy-done.2
  24.1 0.0 copy-done.3
  24.1 0.0 copy-start
  24.1 8.8 %shard_map.56 = bf16[32,32,256]{2,1,0:T(8,128)(2,1)} custom-call(s32[8]{0:T(128)S(1)} %copy-done.2, bf16[32,72,128]{2,1,0:T(8,128)(2,1)S(1)} %all_to_all.10.signal_ref, f32[32,2048]{1,0:T(8,128)S(1)} %bitcast.10, f32[3,3,1024]{2,1,0:T(4,128)S(1)} %copy-done.1), custom_call_target="tpu_custom_call" | custom-call | flops 1509949440 | bytes 2097152 | tf_op jit(solution)/shard_map/pallas_call | solution.py:288
  32.9 4.1 %all-to-all-start.1 = ((bf16[32,32,256]{2,1,0:T(8,128)(2,1)}), bf16[32,32,256]{2,1,0:T(8,128)(2,1)S(1)}, u32[]{:S(2)}, u32[]{:S(2)}) async-start(bf16[32,32,256]{2,1,0:T(8,128)(2,1)} %shard_map.56), calls=%async_computation.1 | async-start | bytes 1048576 | tf_op jit(solution)/shard_map/all_to_all | solution.py:404
  37.0 0.0 copy-done
  37.0 3.5 %collective-permute-start = (bf16[2,1024]{1,0:T(2,128)(2,1)S(1)}, bf16[2,1024]{1,0:T(2,128)(2,1)S(1)}, u32[]{:S(2)}, u32[]{:S(2)}) collective-permute-start(bf16[2,1024]{1,0:T(2,128)(2,1)S(1)} %slice_bitcast_fusion), channel_id=1, source_target_pairs={{0,4},{4,8},{8,12},{12,16},{16,20},{20,24},{24,28},{28,32},{32,36}... | collective-permute-start | bytes 12296 | tf_op jit(solution)/shard_map/ppermute | solution.py:402
  40.5 2.4 %collective-permute-done.edge_ref = bf16[2,1024]{1,0:T(2,128)(2,1)S(1)} collective-permute-done((bf16[2,1024]{1,0:T(2,128)(2,1)S(1)}, bf16[2,1024]{1,0:T(2,128)(2,1)S(1)}, u32[]{:S(2)}, u32[]{:S(2)}) %collective-permute-start) | collective-permute-done | bytes 4128 | tf_op jit(solution)/shard_map/ppermute | solution.py:402
  43.0 1.5 %shard_map.57.query_ref = bf16[256,1024]{1,0:T(8,128)(2,1)S(1)} custom-call(s32[8]{0:T(128)S(1)} %copy-done.2, bf16[3,256,1024]{2,1,0:T(8,128)(2,1)S(1)} %bitcast.8, bf16[2,1024]{1,0:T(2,128)(2,1)S(1)} %collective-permute-done.edge_ref, f32[3,3,1024]{2,1,0:T(4,128)S(1)} %copy-done.1), custom_call_target="tpu_custom_call" | custom-call | flops 5242880 | bytes 2097152 | tf_op jit(solution)/shard_map/pallas_call | solution.py:89
  44.5 4.1 %all-to-all-done.1 = bf16[32,32,256]{2,1,0:T(8,128)(2,1)S(1)} async-done(((bf16[32,32,256]{2,1,0:T(8,128)(2,1)}), bf16[32,32,256]{2,1,0:T(8,128)(2,1)S(1)}, u32[]{:S(2)}, u32[]{:S(2)}) %all-to-all-start.1) | async-done | bytes 524320 | tf_op jit(solution)/shard_map/all_to_all | solution.py:404
  48.6 0.2 shard_map.58
  48.8 1.7 %collective-permute-start.1 = (bf16[128,1024]{1,0:T(8,128)(2,1)S(1)}, bf16[128,1024]{1,0:T(8,128)(2,1)S(1)}, u32[]{:S(2)}, u32[]{:S(2)}) collective-permute-start(bf16[128,1024]{1,0:T(8,128)(2,1)S(1)} %get-tuple-element.11.refs_0_), channel_id=1, source_target_pairs={{0,1},{1,2},{2,3},{3,0},{4,5},{5,6},{6,7},{7,4},{8,9},{9,10},{10,1... | collective-permute-start | bytes 786440 | tf_op jit(solution)/shard_map/ppermute | solution.py:344
  50.5 2.2 %collective-permute-start.3 = (bf16[128,1024]{1,0:T(8,128)(2,1)S(1)}, bf16[128,1024]{1,0:T(8,128)(2,1)S(1)}, u32[]{:S(2)}, u32[]{:S(2)}) collective-permute-start(bf16[128,1024]{1,0:T(8,128)(2,1)S(1)} %get-tuple-element.12.refs_1_), channel_id=1, source_target_pairs={{0,3},{1,0},{2,1},{3,2},{4,7},{5,4},{6,5},{7,6},{8,11},{9,8},{10,9... | collective-permute-start | bytes 786440 | tf_op jit(solution)/shard_map/ppermute | solution.py:344
  52.7 0.0 collective-permute-start.5
  52.7 2.7 %collective-permute-start.6 = (bf16[128,1024]{1,0:T(8,128)(2,1)S(1)}, bf16[128,1024]{1,0:T(8,128)(2,1)S(1)}, u32[]{:S(2)}, u32[]{:S(2)}) collective-permute-start(bf16[128,1024]{1,0:T(8,128)(2,1)S(1)} %get-tuple-element.11.refs_0_), channel_id=1, source_target_pairs={{0,3},{1,0},{2,1},{3,2},{4,7},{5,4},{6,5},{7,6},{8,11},{9,8},{10,9... | collective-permute-start | bytes 786440 | tf_op jit(solution)/shard_map/ppermute | solution.py:344
  55.4 3.5 %collective-permute-done.1.refs_0_ = bf16[128,1024]{1,0:T(8,128)(2,1)S(1)} collective-permute-done((bf16[128,1024]{1,0:T(8,128)(2,1)S(1)}, bf16[128,1024]{1,0:T(8,128)(2,1)S(1)}, u32[]{:S(2)}, u32[]{:S(2)}) %collective-permute-start.1) | collective-permute-done | bytes 262176 | tf_op jit(solution)/shard_map/ppermute | solution.py:344
  59.0 0.0 collective-permute-start.2
  59.0 0.0 collective-permute-done.3.refs_3_
  59.0 2.7 %collective-permute-start.4 = (bf16[128,1024]{1,0:T(8,128)(2,1)S(1)}, bf16[128,1024]{1,0:T(8,128)(2,1)S(1)}, u32[]{:S(2)}, u32[]{:S(2)}) collective-permute-start(bf16[128,1024]{1,0:T(8,128)(2,1)S(1)} %collective-permute-done.3.refs_3_), channel_id=1, source_target_pairs={{0,3},{1,0},{2,1},{3,2},{4,7},{5,4},{6,5},{7,6},{8,11},{9,8},{10,9... | collective-permute-start | bytes 786440 | tf_op jit(solution)/shard_map/ppermute | solution.py:344
  61.6 4.4 %constant_dynamic-slice_fusion = (bf16[1024,1024]{1,0:T(8,128)(2,1)S(1)}, bf16[1024,1024]{1,0:T(8,128)(2,1)S(1)}, bf16[1024,1024]{1,0:T(8,128)(2,1)S(1)}, bf16[1024,1024]{1,0:T(8,128)(2,1)S(1)}) fusion(bf16[4096,1024]{1,0:T(8,128)(2,1)} %param.9, s32[]{:T(128)S(6)} %select_n.38, s32[]{:T(128)S(6)} %select_n.34, s32[]{:T(128)S(6)} %select_n.32, s32[]{:T(128)S(6)} %select_n.36), kind=kLoop, calls=%fused_computation.1 | loop fusion | bytes 16777232 | tf_op jit(solution)/shard_map/dynamic_slice | solution.py:381
  66.1 0.7 shard_map.59.refs_6_
  66.8 0.0 collective-permute-done.5.refs_1_
  66.8 0.0 collective-permute-done.6.refs_2_
  66.8 1.3 %shard_map.60.refs_3_ = f32[256,1024]{1,0:T(8,128)S(1)} custom-call(bf16[128,1024]{1,0:T(8,128)(2,1)S(1)} %collective-permute-done.1.refs_0_, bf16[128,1024]{1,0:T(8,128)(2,1)S(1)} %collective-permute-done.5.refs_1_, bf16[128,1024]{1,0:T(8,128)(2,1)S(1)} %collective-permute-done.6.refs_2_, bf16[128,1024]{1,0:T(8,128)(2,1)S(1)} %collective-permute-done.3.refs_3_, ...), custom_call_target="tpu_custom_call" | custom-call | flops 1073741824 | bytes 4194304 | tf_op jit(solution)/shard_map/pallas_call | solution.py:364
  68.1 2.1 %collective-permute-done.2.refs_0_ = bf16[128,1024]{1,0:T(8,128)(2,1)S(1)} collective-permute-done((bf16[128,1024]{1,0:T(8,128)(2,1)S(1)}, bf16[128,1024]{1,0:T(8,128)(2,1)S(1)}, u32[]{:S(2)}, u32[]{:S(2)}) %collective-permute-start.2) | collective-permute-done | bytes 262176 | tf_op jit(solution)/shard_map/ppermute | solution.py:344
  70.2 0.0 collective-permute-done.4.refs_1_
  70.2 1.5 %shard_map.61 = bf16[256,1024]{1,0:T(8,128)(2,1)} custom-call(bf16[128,1024]{1,0:T(8,128)(2,1)S(1)} %collective-permute-done.2.refs_0_, bf16[128,1024]{1,0:T(8,128)(2,1)S(1)} %collective-permute-done.4.refs_1_, bf16[1024,1024]{1,0:T(8,128)(2,1)S(1)} %get-tuple-element.15.refs_2_, f32[256,1024]{1,0:T(8,128)S(1)} %shard_map.60.refs_3_), custom_call_target="tpu_custom_call" | custom-call | flops 536870912 | bytes 2097152 | tf_op jit(solution)/shard_map/pallas_call | solution.py:364
  (1 shorter events, 0.0 us)
Async XLA Ops:
  0.0 24.1 %copy-start.1 = (f32[3,3,1024]{2,1,0:T(4,128)S(1)}, f32[3,3,1024]{2,1,0:T(4,128)}, u32[]{:S(2)}) copy-start(f32[3,3,1024]{2,1,0:T(4,128)} %taps_ref.3) | copy-start | bytes 110596
  0.0 24.1 %copy-start.2 = (s32[8]{0:T(128)S(1)}, s32[8]{0:T(128)}, u32[]{:S(2)}) copy-start(s32[8]{0:T(128)} %lengths_ref.5) | copy-start | bytes 100
  0.0 24.1 %copy-start.3 = (f32[1,32,2048]{2,1,0:T(8,128)S(1)}, f32[1,32,2048]{2,1,0:T(8,128)}, u32[]{:S(2)}) copy-start(f32[1,32,2048]{2,1,0:T(8,128)} %param.8) | copy-start | bytes 786436
  24.1 12.9 %copy-start = (bf16[256,3,1024]{2,0,1:T(8,128)(2,1)S(1)}, bf16[256,3,1024]{2,0,1:T(8,128)(2,1)}, u32[]{:S(2)}) copy-start(bf16[256,3,1024]{2,0,1:T(8,128)(2,1)} %param.5) | copy-start | bytes 4718596
  32.9 15.7 %all-to-all-start.1 = ((bf16[32,32,256]{2,1,0:T(8,128)(2,1)}), bf16[32,32,256]{2,1,0:T(8,128)(2,1)S(1)}, u32[]{:S(2)}, u32[]{:S(2)}) async-start(bf16[32,32,256]{2,1,0:T(8,128)(2,1)} %shard_map.56), calls=%async_computation.1 | async-start | bytes 1048576 | tf_op jit(solution)/shard_map/all_to_all | solution.py:404
  37.0 6.0 %collective-permute-start = (bf16[2,1024]{1,0:T(2,128)(2,1)S(1)}, bf16[2,1024]{1,0:T(2,128)(2,1)S(1)}, u32[]{:S(2)}, u32[]{:S(2)}) collective-permute-start(bf16[2,1024]{1,0:T(2,128)(2,1)S(1)} %slice_bitcast_fusion), channel_id=1, source_target_pairs={{0,4},{4,8},{8,12},{12,16},{16,20},{20,24},{24,28},{28,32},{32,36}... | collective-permute-start | bytes 12296 | tf_op jit(solution)/shard_map/ppermute | solution.py:402
  48.8 10.1 %collective-permute-start.1 = (bf16[128,1024]{1,0:T(8,128)(2,1)S(1)}, bf16[128,1024]{1,0:T(8,128)(2,1)S(1)}, u32[]{:S(2)}, u32[]{:S(2)}) collective-permute-start(bf16[128,1024]{1,0:T(8,128)(2,1)S(1)} %get-tuple-element.11.refs_0_), channel_id=1, source_target_pairs={{0,1},{1,2},{2,3},{3,0},{4,5},{5,6},{6,7},{7,4},{8,9},{9,10},{10,1... | collective-permute-start | bytes 786440 | tf_op jit(solution)/shard_map/ppermute | solution.py:344
  50.5 8.4 %collective-permute-start.3 = (bf16[128,1024]{1,0:T(8,128)(2,1)S(1)}, bf16[128,1024]{1,0:T(8,128)(2,1)S(1)}, u32[]{:S(2)}, u32[]{:S(2)}) collective-permute-start(bf16[128,1024]{1,0:T(8,128)(2,1)S(1)} %get-tuple-element.12.refs_1_), channel_id=1, source_target_pairs={{0,3},{1,0},{2,1},{3,2},{4,7},{5,4},{6,5},{7,6},{8,11},{9,8},{10,9... | collective-permute-start | bytes 786440 | tf_op jit(solution)/shard_map/ppermute | solution.py:344
  52.7 14.1 %collective-permute-start.5 = (bf16[128,1024]{1,0:T(8,128)(2,1)S(1)}, bf16[128,1024]{1,0:T(8,128)(2,1)S(1)}, u32[]{:S(2)}, u32[]{:S(2)}) collective-permute-start(bf16[128,1024]{1,0:T(8,128)(2,1)S(1)} %get-tuple-element.12.refs_1_), channel_id=1, source_target_pairs={{0,1},{1,2},{2,3},{3,0},{4,5},{5,6},{6,7},{7,4},{8,9},{9,10},{10,1... | collective-permute-start | bytes 786440 | tf_op jit(solution)/shard_map/ppermute | solution.py:344
  52.7 14.1 %collective-permute-start.6 = (bf16[128,1024]{1,0:T(8,128)(2,1)S(1)}, bf16[128,1024]{1,0:T(8,128)(2,1)S(1)}, u32[]{:S(2)}, u32[]{:S(2)}) collective-permute-start(bf16[128,1024]{1,0:T(8,128)(2,1)S(1)} %get-tuple-element.11.refs_0_), channel_id=1, source_target_pairs={{0,3},{1,0},{2,1},{3,2},{4,7},{5,4},{6,5},{7,6},{8,11},{9,8},{10,9... | collective-permute-start | bytes 786440 | tf_op jit(solution)/shard_map/ppermute | solution.py:344
  59.0 11.2 %collective-permute-start.2 = (bf16[128,1024]{1,0:T(8,128)(2,1)S(1)}, bf16[128,1024]{1,0:T(8,128)(2,1)S(1)}, u32[]{:S(2)}, u32[]{:S(2)}) collective-permute-start(bf16[128,1024]{1,0:T(8,128)(2,1)S(1)} %collective-permute-done.1.refs_0_), channel_id=1, source_target_pairs={{0,1},{1,2},{2,3},{3,0},{4,5},{5,6},{6,7},{7,4},{8,9},{9,10},{10,1... | collective-permute-start | bytes 786440 | tf_op jit(solution)/shard_map/ppermute | solution.py:344
  59.0 11.2 %collective-permute-start.4 = (bf16[128,1024]{1,0:T(8,128)(2,1)S(1)}, bf16[128,1024]{1,0:T(8,128)(2,1)S(1)}, u32[]{:S(2)}, u32[]{:S(2)}) collective-permute-start(bf16[128,1024]{1,0:T(8,128)(2,1)S(1)} %collective-permute-done.3.refs_3_), channel_id=1, source_target_pairs={{0,3},{1,0},{2,1},{3,2},{4,7},{5,4},{6,5},{7,6},{8,11},{9,8},{10,9... | collective-permute-start | bytes 786440 | tf_op jit(solution)/shard_map/ppermute | solution.py:344

commit v7 on v6

--- a/solution.py
+++ b/solution.py
@@ -208,17 +208,16 @@
 
     list_rows(lengths_ref, table, heads, rows)
     for device in range(devices):
-        arrived = signal_ref[device].astype(jnp.float32)
-        for h in range(2):
-            blocks[device, :, h * TILE : (h + 1) * TILE] = arrived[h * channels : (h + 1) * channels]
-        edges[device * EDGES : (device + 1) * EDGES, :] = arrived[2 * channels :]
+        edges[device * EDGES : (device + 1) * EDGES, :] = signal_ref[device].astype(jnp.float32)[2 * channels :]
     firsts = first_products(lengths_ref, edges[...], short_ref, channels)
     is_first = lax.broadcasted_iota(jnp.int32, (channels, TILE), 1) < TAPS - 1
     for device in range(devices):
+        arrived = signal_ref[device].astype(jnp.float32)
         at = device * EDGES
         mine = firsts[:, at // TILE * TILE : (at // TILE + 1) * TILE]
         mine = mine if at % TILE == 0 else pltpu.roll(mine, TILE - at % TILE, 1)
-        blocks[device, :, :TILE] = jnp.where(is_first, mine, blocks[device, :, :TILE])
+        blocks[device, :, :TILE] = jnp.where(is_first, mine, arrived[:channels])
+        blocks[device, :, TILE:] = arrived[channels : 2 * channels]
     for row in range(rows):
         slab = only_lanes(table, row, blocks[table[0, row]], 0.0)
         for h in range(2):
@@ -238,7 +237,11 @@
             toep[g, t * TILE : (t + 1) * TILE, :] = sheared[:, t * TILE : (t + 1) * TILE].astype(jnp.bfloat16)
         lefts = [
             [
-                jnp.where(behind >= lag, spread[h, base - lag : base - lag + rows_b, :], 0.0).astype(jnp.bfloat16)
+                (
+                    spread[h, base : base + rows_b, :]
+                    if lag == 0
+                    else jnp.where(behind >= lag, spread[h, base - lag : base - lag + rows_b, :], 0.0)
+                ).astype(jnp.bfloat16)
                 for h in range(2)
             ]
             for lag in range(lags)

time: 72 us -> 72 us (level)
  no operation moved by 1% of the time
where the time goes in v7:
time: 72 us; the launch traced here: 71.7 us
  blocking collectives  20.8 us (29%)
  Pallas kernels  17.2 us (24%)
  starting transfers between devices  16.9 us (23%)
  waiting for transfers between devices  12.2 us (17%)
  local copies, waits for them, and re-layouts  4.47 us (6%)
    all_to_all x1, blocking collectives, per_device(): signal = lax.all_to_all(sent, 'seq', 0, 0, tiled=True)  20.8 us
    ppermute x6, starting transfers between devices, shift(): lax.ppermute(array, axis, [(i, (i + by) % length) for i in range(length)])  9.26 us
    pallas_call x1, Pallas kernels, long_conv(): pl.pallas_call(functools.partial(conv_kernel, rows=rows, rows_b=rows_b),...  8.78 us
    ppermute x6, waiting for transfers between devices, shift(): lax.ppermute(array, axis, [(i, (i + by) % length) for i in range(length)])  5.63 us
    pallas_call x2, Pallas kernels, short_call(): pl.pallas_call(kernel, grid=(steps,), out_shape=jax.ShapeDtypeStruct(shap...  4.77 us
    dynamic_slice x1, local copies, waits for them, and re-layouts, project(): lax.dynamic_slice_in_dim(w_out, (place + i) % size * depth, depth, 0)  4.45 us
    all_to_all x1, waiting for transfers between devices, per_device(): lax.all_to_all(conv, 'seq', 0, 0, tiled=True).reshape(width, tok_rows)  4.12 us
    all_to_all x1, starting transfers between devices, per_device(): lax.all_to_all(conv, 'seq', 0, 0, tiled=True).reshape(width, tok_rows)  4.06 us
  transfers between devices with their start and end apart: 8, of which 4 were waited for; matrix products, arithmetic and copies ran while one was open for 6% of the time, Pallas kernels for 5%

profile of v7, /device:TPU:1, one launch (start us, length us, event | category | flops | bytes accessed | tf_op | source)
XLA Modules:
  0.0 71.7 jit_solution(12115234034691890671)
XLA Ops:
  0.0 0.0 copy-start.1
  0.0 0.0 copy-start.2
  0.0 0.0 copy-start.3
  0.0 3.2 %shard_map.55 = bf16[32,72,128]{2,1,0:T(8,128)(2,1)} custom-call(s32[8]{0:T(128)} %lengths_ref.5, bf16[3,256,1024]{2,1,0:T(8,128)(2,1)} %bitcast.5, bf16[3,256,1024]{2,1,0:T(8,128)(2,1)} %bitcast.6, f32[3,3,1024]{2,1,0:T(4,128)} %taps_ref.3), custom_call_target="tpu_custom_call" | custom-call | flops 5242880 | bytes 2097152 | tf_op jit(solution)/shard_map/pallas_call | solution.py:89
  3.2 20.8 %all_to_all.10.signal_ref = bf16[32,72,128]{2,1,0:T(8,128)(2,1)S(1)} all-to-all(bf16[32,72,128]{2,1,0:T(8,128)(2,1)} %shard_map.55), channel_id=1, replica_groups=mesh['seq'=32,'ch'=4] {'seq'}, dimensions={0} | all-to-all | bytes 1179648 | tf_op jit(solution)/shard_map/all_to_all | solution.py:402
  24.1 0.0 copy-done.1
  24.1 0.0 copy-done.2
  24.1 0.0 copy-done.3
  24.1 0.0 copy-start
  24.1 8.8 %shard_map.56 = bf16[32,32,256]{2,1,0:T(8,128)(2,1)} custom-call(s32[8]{0:T(128)S(1)} %copy-done.2, bf16[32,72,128]{2,1,0:T(8,128)(2,1)S(1)} %all_to_all.10.signal_ref, f32[32,2048]{1,0:T(8,128)S(1)} %bitcast.10, f32[3,3,1024]{2,1,0:T(4,128)S(1)} %copy-done.1), custom_call_target="tpu_custom_call" | custom-call | flops 1509949440 | bytes 2097152 | tf_op jit(solution)/shard_map/pallas_call | solution.py:291
  32.9 4.1 %all-to-all-start.1 = ((bf16[32,32,256]{2,1,0:T(8,128)(2,1)}), bf16[32,32,256]{2,1,0:T(8,128)(2,1)S(1)}, u32[]{:S(2)}, u32[]{:S(2)}) async-start(bf16[32,32,256]{2,1,0:T(8,128)(2,1)} %shard_map.56), calls=%async_computation.1 | async-start | bytes 1048576 | tf_op jit(solution)/shard_map/all_to_all | solution.py:407
  36.9 0.0 copy-done
  37.0 3.5 %collective-permute-start = (bf16[2,1024]{1,0:T(2,128)(2,1)S(1)}, bf16[2,1024]{1,0:T(2,128)(2,1)S(1)}, u32[]{:S(2)}, u32[]{:S(2)}) collective-permute-start(bf16[2,1024]{1,0:T(2,128)(2,1)S(1)} %slice_bitcast_fusion), channel_id=1, source_target_pairs={{0,4},{4,8},{8,12},{12,16},{16,20},{20,24},{24,28},{28,32},{32,36}... | collective-permute-start | bytes 12296 | tf_op jit(solution)/shard_map/ppermute | solution.py:405
  40.5 2.4 %collective-permute-done.edge_ref = bf16[2,1024]{1,0:T(2,128)(2,1)S(1)} collective-permute-done((bf16[2,1024]{1,0:T(2,128)(2,1)S(1)}, bf16[2,1024]{1,0:T(2,128)(2,1)S(1)}, u32[]{:S(2)}, u32[]{:S(2)}) %collective-permute-start) | collective-permute-done | bytes 4128 | tf_op jit(solution)/shard_map/ppermute | solution.py:405
  42.9 1.5 %shard_map.57.query_ref = bf16[256,1024]{1,0:T(8,128)(2,1)S(1)} custom-call(s32[8]{0:T(128)S(1)} %copy-done.2, bf16[3,256,1024]{2,1,0:T(8,128)(2,1)S(1)} %bitcast.8, bf16[2,1024]{1,0:T(2,128)(2,1)S(1)} %collective-permute-done.edge_ref, f32[3,3,1024]{2,1,0:T(4,128)S(1)} %copy-done.1), custom_call_target="tpu_custom_call" | custom-call | flops 5242880 | bytes 2097152 | tf_op jit(solution)/shard_map/pallas_call | solution.py:89
  44.5 4.1 %all-to-all-done.1 = bf16[32,32,256]{2,1,0:T(8,128)(2,1)S(1)} async-done(((bf16[32,32,256]{2,1,0:T(8,128)(2,1)}), bf16[32,32,256]{2,1,0:T(8,128)(2,1)S(1)}, u32[]{:S(2)}, u32[]{:S(2)}) %all-to-all-start.1) | async-done | bytes 524320 | tf_op jit(solution)/shard_map/all_to_all | solution.py:407
  48.6 0.2 shard_map.58
  48.8 1.7 %collective-permute-start.1 = (bf16[128,1024]{1,0:T(8,128)(2,1)S(1)}, bf16[128,1024]{1,0:T(8,128)(2,1)S(1)}, u32[]{:S(2)}, u32[]{:S(2)}) collective-permute-start(bf16[128,1024]{1,0:T(8,128)(2,1)S(1)} %get-tuple-element.11.refs_0_), channel_id=1, source_target_pairs={{0,1},{1,2},{2,3},{3,0},{4,5},{5,6},{6,7},{7,4},{8,9},{9,10},{10,1... | collective-permute-start | bytes 786440 | tf_op jit(solution)/shard_map/ppermute | solution.py:347
  50.5 2.2 %collective-permute-start.3 = (bf16[128,1024]{1,0:T(8,128)(2,1)S(1)}, bf16[128,1024]{1,0:T(8,128)(2,1)S(1)}, u32[]{:S(2)}, u32[]{:S(2)}) collective-permute-start(bf16[128,1024]{1,0:T(8,128)(2,1)S(1)} %get-tuple-element.12.refs_1_), channel_id=1, source_target_pairs={{0,3},{1,0},{2,1},{3,2},{4,7},{5,4},{6,5},{7,6},{8,11},{9,8},{10,9... | collective-permute-start | bytes 786440 | tf_op jit(solution)/shard_map/ppermute | solution.py:347
  52.7 0.0 collective-permute-start.5
  52.7 2.7 %collective-permute-start.6 = (bf16[128,1024]{1,0:T(8,128)(2,1)S(1)}, bf16[128,1024]{1,0:T(8,128)(2,1)S(1)}, u32[]{:S(2)}, u32[]{:S(2)}) collective-permute-start(bf16[128,1024]{1,0:T(8,128)(2,1)S(1)} %get-tuple-element.11.refs_0_), channel_id=1, source_target_pairs={{0,3},{1,0},{2,1},{3,2},{4,7},{5,4},{6,5},{7,6},{8,11},{9,8},{10,9... | collective-permute-start | bytes 786440 | tf_op jit(solution)/shard_map/ppermute | solution.py:347
  55.4 3.5 %collective-permute-done.1.refs_0_ = bf16[128,1024]{1,0:T(8,128)(2,1)S(1)} collective-permute-done((bf16[128,1024]{1,0:T(8,128)(2,1)S(1)}, bf16[128,1024]{1,0:T(8,128)(2,1)S(1)}, u32[]{:S(2)}, u32[]{:S(2)}) %collective-permute-start.1) | collective-permute-done | bytes 262176 | tf_op jit(solution)/shard_map/ppermute | solution.py:347
  58.9 0.0 collective-permute-start.2
  58.9 0.0 collective-permute-done.3.refs_3_
  58.9 2.7 %collective-permute-start.4 = (bf16[128,1024]{1,0:T(8,128)(2,1)S(1)}, bf16[128,1024]{1,0:T(8,128)(2,1)S(1)}, u32[]{:S(2)}, u32[]{:S(2)}) collective-permute-start(bf16[128,1024]{1,0:T(8,128)(2,1)S(1)} %collective-permute-done.3.refs_3_), channel_id=1, source_target_pairs={{0,3},{1,0},{2,1},{3,2},{4,7},{5,4},{6,5},{7,6},{8,11},{9,8},{10,9... | collective-permute-start | bytes 786440 | tf_op jit(solution)/shard_map/ppermute | solution.py:347
  61.6 4.4 %constant_dynamic-slice_fusion = (bf16[1024,1024]{1,0:T(8,128)(2,1)S(1)}, bf16[1024,1024]{1,0:T(8,128)(2,1)S(1)}, bf16[1024,1024]{1,0:T(8,128)(2,1)S(1)}, bf16[1024,1024]{1,0:T(8,128)(2,1)S(1)}) fusion(bf16[4096,1024]{1,0:T(8,128)(2,1)} %param.9, s32[]{:T(128)S(6)} %select_n.38, s32[]{:T(128)S(6)} %select_n.34, s32[]{:T(128)S(6)} %select_n.32, s32[]{:T(128)S(6)} %select_n.36), kind=kLoop, calls=%fused_computation.1 | loop fusion | bytes 16777232 | tf_op jit(solution)/shard_map/dynamic_slice | solution.py:384
  66.1 0.7 shard_map.59.refs_6_
  66.8 0.0 collective-permute-done.5.refs_1_
  66.8 0.0 collective-permute-done.6.refs_2_
  66.8 1.3 %shard_map.60.refs_3_ = f32[256,1024]{1,0:T(8,128)S(1)} custom-call(bf16[128,1024]{1,0:T(8,128)(2,1)S(1)} %collective-permute-done.1.refs_0_, bf16[128,1024]{1,0:T(8,128)(2,1)S(1)} %collective-permute-done.5.refs_1_, bf16[128,1024]{1,0:T(8,128)(2,1)S(1)} %collective-permute-done.6.refs_2_, bf16[128,1024]{1,0:T(8,128)(2,1)S(1)} %collective-permute-done.3.refs_3_, ...), custom_call_target="tpu_custom_call" | custom-call | flops 1073741824 | bytes 4194304 | tf_op jit(solution)/shard_map/pallas_call | solution.py:367
  68.1 2.1 %collective-permute-done.2.refs_0_ = bf16[128,1024]{1,0:T(8,128)(2,1)S(1)} collective-permute-done((bf16[128,1024]{1,0:T(8,128)(2,1)S(1)}, bf16[128,1024]{1,0:T(8,128)(2,1)S(1)}, u32[]{:S(2)}, u32[]{:S(2)}) %collective-permute-start.2) | collective-permute-done | bytes 262176 | tf_op jit(solution)/shard_map/ppermute | solution.py:347
  70.2 0.0 collective-permute-done.4.refs_1_
  70.2 1.5 %shard_map.61 = bf16[256,1024]{1,0:T(8,128)(2,1)} custom-call(bf16[128,1024]{1,0:T(8,128)(2,1)S(1)} %collective-permute-done.2.refs_0_, bf16[128,1024]{1,0:T(8,128)(2,1)S(1)} %collective-permute-done.4.refs_1_, bf16[1024,1024]{1,0:T(8,128)(2,1)S(1)} %get-tuple-element.15.refs_2_, f32[256,1024]{1,0:T(8,128)S(1)} %shard_map.60.refs_3_), custom_call_target="tpu_custom_call" | custom-call | flops 536870912 | bytes 2097152 | tf_op jit(solution)/shard_map/pallas_call | solution.py:367
  (1 shorter events, 0.0 us)
Async XLA Ops:
  0.0 24.1 %copy-start.1 = (f32[3,3,1024]{2,1,0:T(4,128)S(1)}, f32[3,3,1024]{2,1,0:T(4,128)}, u32[]{:S(2)}) copy-start(f32[3,3,1024]{2,1,0:T(4,128)} %taps_ref.3) | copy-start | bytes 110596
  0.0 24.1 %copy-start.2 = (s32[8]{0:T(128)S(1)}, s32[8]{0:T(128)}, u32[]{:S(2)}) copy-start(s32[8]{0:T(128)} %lengths_ref.5) | copy-start | bytes 100
  0.0 24.1 %copy-start.3 = (f32[1,32,2048]{2,1,0:T(8,128)S(1)}, f32[1,32,2048]{2,1,0:T(8,128)}, u32[]{:S(2)}) copy-start(f32[1,32,2048]{2,1,0:T(8,128)} %param.8) | copy-start | bytes 786436
  24.1 12.9 %copy-start = (bf16[256,3,1024]{2,0,1:T(8,128)(2,1)S(1)}, bf16[256,3,1024]{2,0,1:T(8,128)(2,1)}, u32[]{:S(2)}) copy-start(bf16[256,3,1024]{2,0,1:T(8,128)(2,1)} %param.5) | copy-start | bytes 4718596
  32.9 15.7 %all-to-all-start.1 = ((bf16[32,32,256]{2,1,0:T(8,128)(2,1)}), bf16[32,32,256]{2,1,0:T(8,128)(2,1)S(1)}, u32[]{:S(2)}, u32[]{:S(2)}) async-start(bf16[32,32,256]{2,1,0:T(8,128)(2,1)} %shard_map.56), calls=%async_computation.1 | async-start | bytes 1048576 | tf_op jit(solution)/shard_map/all_to_all | solution.py:407
  37.0 6.0 %collective-permute-start = (bf16[2,1024]{1,0:T(2,128)(2,1)S(1)}, bf16[2,1024]{1,0:T(2,128)(2,1)S(1)}, u32[]{:S(2)}, u32[]{:S(2)}) collective-permute-start(bf16[2,1024]{1,0:T(2,128)(2,1)S(1)} %slice_bitcast_fusion), channel_id=1, source_target_pairs={{0,4},{4,8},{8,12},{12,16},{16,20},{20,24},{24,28},{28,32},{32,36}... | collective-permute-start | bytes 12296 | tf_op jit(solution)/shard_map/ppermute | solution.py:405
  48.8 10.1 %collective-permute-start.1 = (bf16[128,1024]{1,0:T(8,128)(2,1)S(1)}, bf16[128,1024]{1,0:T(8,128)(2,1)S(1)}, u32[]{:S(2)}, u32[]{:S(2)}) collective-permute-start(bf16[128,1024]{1,0:T(8,128)(2,1)S(1)} %get-tuple-element.11.refs_0_), channel_id=1, source_target_pairs={{0,1},{1,2},{2,3},{3,0},{4,5},{5,6},{6,7},{7,4},{8,9},{9,10},{10,1... | collective-permute-start | bytes 786440 | tf_op jit(solution)/shard_map/ppermute | solution.py:347
  50.5 8.4 %collective-permute-start.3 = (bf16[128,1024]{1,0:T(8,128)(2,1)S(1)}, bf16[128,1024]{1,0:T(8,128)(2,1)S(1)}, u32[]{:S(2)}, u32[]{:S(2)}) collective-permute-start(bf16[128,1024]{1,0:T(8,128)(2,1)S(1)} %get-tuple-element.12.refs_1_), channel_id=1, source_target_pairs={{0,3},{1,0},{2,1},{3,2},{4,7},{5,4},{6,5},{7,6},{8,11},{9,8},{10,9... | collective-permute-start | bytes 786440 | tf_op jit(solution)/shard_map/ppermute | solution.py:347
  52.7 14.1 %collective-permute-start.5 = (bf16[128,1024]{1,0:T(8,128)(2,1)S(1)}, bf16[128,1024]{1,0:T(8,128)(2,1)S(1)}, u32[]{:S(2)}, u32[]{:S(2)}) collective-permute-start(bf16[128,1024]{1,0:T(8,128)(2,1)S(1)} %get-tuple-element.12.refs_1_), channel_id=1, source_target_pairs={{0,1},{1,2},{2,3},{3,0},{4,5},{5,6},{6,7},{7,4},{8,9},{9,10},{10,1... | collective-permute-start | bytes 786440 | tf_op jit(solution)/shard_map/ppermute | solution.py:347
  52.7 14.1 %collective-permute-start.6 = (bf16[128,1024]{1,0:T(8,128)(2,1)S(1)}, bf16[128,1024]{1,0:T(8,128)(2,1)S(1)}, u32[]{:S(2)}, u32[]{:S(2)}) collective-permute-start(bf16[128,1024]{1,0:T(8,128)(2,1)S(1)} %get-tuple-element.11.refs_0_), channel_id=1, source_target_pairs={{0,3},{1,0},{2,1},{3,2},{4,7},{5,4},{6,5},{7,6},{8,11},{9,8},{10,9... | collective-permute-start | bytes 786440 | tf_op jit(solution)/shard_map/ppermute | solution.py:347
  58.9 11.2 %collective-permute-start.2 = (bf16[128,1024]{1,0:T(8,128)(2,1)S(1)}, bf16[128,1024]{1,0:T(8,128)(2,1)S(1)}, u32[]{:S(2)}, u32[]{:S(2)}) collective-permute-start(bf16[128,1024]{1,0:T(8,128)(2,1)S(1)} %collective-permute-done.1.refs_0_), channel_id=1, source_target_pairs={{0,1},{1,2},{2,3},{3,0},{4,5},{5,6},{6,7},{7,4},{8,9},{9,10},{10,1... | collective-permute-start | bytes 786440 | tf_op jit(solution)/shard_map/ppermute | solution.py:347
  58.9 11.2 %collective-permute-start.4 = (bf16[128,1024]{1,0:T(8,128)(2,1)S(1)}, bf16[128,1024]{1,0:T(8,128)(2,1)S(1)}, u32[]{:S(2)}, u32[]{:S(2)}) collective-permute-start(bf16[128,1024]{1,0:T(8,128)(2,1)S(1)} %collective-permute-done.3.refs_3_), channel_id=1, source_target_pairs={{0,3},{1,0},{2,1},{3,2},{4,7},{5,4},{6,5},{7,6},{8,11},{9,8},{10,9... | collective-permute-start | bytes 786440 | tf_op jit(solution)/shard_map/ppermute | solution.py:347
